TPU v7x, 32 devices: a whole 2x2x4 slice. The times are simulated.
32 devices in a mesh: date: 8 (over y, x, core), swath: 4 (over z).
Axes of the slice: x: 2, y: 2, z: 4, core: 2. Of those that a mesh axis runs over, the one named last changes fastest.
Arguments:
- raw_echo: bfloat16 [8, 2, 1024, 2048], P('date', None, 'swath'), may hold values from -8 to 8
- range_rate: float32 [], replicated, may hold values from 0.5 to 1
- azimuth_rate: float32 [2048], P('swath'), may hold values from 0.25 to 1
- line_offset: int32 [8], P('date'), may hold values from 0 to 24, as said below
- frac_shift: float32 [8], P('date'), may hold values from 0 to 1
Outputs:
- coregistered: bfloat16 [8, 2, 1024, 2048], P('date', None, 'swath')
- coherence: bfloat16 [8, 2, 2, 1024, 2048], P('date', None, None, 'swath')
Inputs may be any that keep to these rules, and one draw needn't show every extreme that they name: `line_offset`: one date has offset 24 and another has offset 0.
All inputs are finite; a program needn't handle non-finite values.
Results may differ from a plain program's by a relative error of at most 0.0076.
Values may be sent and summed in bfloat16 or wider, within the bound.
No kernel may reach another device: no remote copies, remote signals or barrier semaphores. Data moves between devices by JAX's collectives and lax.ppermute only.
A program may use at most 128 MiB of HBM per device.

v0:
```python
import math

import jax
import jax.numpy as jnp
from jax import lax
from jax.sharding import PartitionSpec as P

AZ = 1024
RG = 2048
TAPS = 8
MAX_OFF = 24
WIN_AZ = 11
WIN_RG = 5
SPAN = 2


two_pi = 2.0 * math.pi
epsilon = 1e-06


def with_halo(block, sides, width):
    for axis, dim in sides:
        count = lax.axis_size(axis)
        forward = [(i, i + 1) for i in range(count - 1)]
        backward = [(target, source) for source, target in forward]
        low = lax.ppermute(
            lax.slice_in_dim(block, block.shape[dim] - width, None, axis=dim), axis, forward
        )
        high = lax.ppermute(lax.slice_in_dim(block, 0, width, axis=dim), axis, backward)
        block = jnp.concatenate([low, block, high], axis=dim)
    return block


def shifted(block, axis, distance):
    devices = range(lax.axis_size(axis))
    route = [((i - distance) % len(devices), i) for i in devices]
    return lax.ppermute(block, axis, route)


def local_dot(left, right):
    return jnp.dot(left, right, preferred_element_type=jnp.float32)


def chirp_block(range_rate, row_count, col_count):
    pulse_len = RG // 2
    row_ids = lax.broadcasted_iota(jnp.int32, (row_count, col_count), 0)
    col_ids = lax.broadcasted_iota(jnp.int32, (row_count, col_count), 1)
    lag_ids = row_ids - col_ids
    inside = (lag_ids >= 0) & (lag_ids < pulse_len)
    offset = (lag_ids.astype(jnp.float32) - 0.5 * pulse_len) / pulse_len
    phase_arg = math.pi * pulse_len * range_rate * offset * offset
    amplitude = 1.0 / math.sqrt(pulse_len)
    real_tab = jnp.where(inside, jnp.cos(phase_arg) * amplitude, 0.0).astype(jnp.bfloat16)
    imag_tab = jnp.where(inside, -jnp.sin(phase_arg) * amplitude, 0.0).astype(jnp.bfloat16)
    return (real_tab, imag_tab)


def range_compress(echo_lines, range_rate, product):
    pulse_len = RG // 2
    block_size = min(RG, 256)
    real_tab, imag_tab = chirp_block(range_rate, pulse_len + block_size, block_size)
    line_count = echo_lines.shape[1]
    stacked = echo_lines.reshape(2 * line_count, RG)
    extended = jnp.concatenate([stacked, stacked[:, :pulse_len]], axis=1)

    def one_block(block_id):
        window = lax.dynamic_slice_in_dim(
            extended, block_id * block_size, pulse_len + block_size, 1
        )
        with_real = product(window, real_tab)
        with_imag = product(window, imag_tab)
        real_out = with_real[:line_count] - with_imag[line_count:]
        imag_out = with_imag[:line_count] + with_real[line_count:]
        return jnp.stack([real_out, imag_out])

    blocks = lax.map(one_block, jnp.arange(RG // block_size, dtype=jnp.int32))
    return blocks.transpose(1, 2, 0, 3).reshape(2, line_count, RG)


def fourier_rows(first_row, row_count, length):
    row_ids = lax.broadcasted_iota(jnp.int32, (row_count, length), 0) + first_row
    col_ids = lax.broadcasted_iota(jnp.int32, (row_count, length), 1)
    turn_angle = (row_ids * col_ids % length).astype(jnp.float32) * (two_pi / length)
    amplitude = 1.0 / math.sqrt(length)
    return (
        (jnp.cos(turn_angle) * amplitude).astype(jnp.bfloat16),
        (-jnp.sin(turn_angle) * amplitude).astype(jnp.bfloat16),
    )


def azimuth_compress(columns, azimuth_rate, product):
    col_count = columns.shape[2]
    joined = jnp.concatenate([columns[0], columns[1]], axis=1)
    block_size = min(AZ, 256)
    block_ids = jnp.arange(AZ // block_size, dtype=jnp.int32)

    def forward_block(block_id):
        first_row = block_id * block_size
        real_tab, imag_tab = fourier_rows(first_row, block_size, AZ)
        with_real = product(real_tab, joined)
        with_imag = product(imag_tab, joined)
        spectrum_re = with_real[:, :col_count] - with_imag[:, col_count:]
        spectrum_im = with_real[:, col_count:] + with_imag[:, :col_count]
        freq_ids = lax.broadcasted_iota(jnp.int32, (block_size, 1), 0) + first_row
        centered = ((freq_ids + AZ // 2) % AZ - AZ // 2).astype(jnp.float32) / AZ
        phase_arg = math.pi * AZ * azimuth_rate[None, :] * centered * centered
        filter_re = jnp.cos(phase_arg)
        filter_im = jnp.sin(phase_arg)
        out_re = spectrum_re * filter_re - spectrum_im * filter_im
        out_im = spectrum_re * filter_im + spectrum_im * filter_re
        return jnp.concatenate([out_re, out_im], axis=1).astype(jnp.bfloat16)

    filtered = lax.map(forward_block, block_ids).reshape(AZ, 2 * col_count)

    def inverse_block(block_id):
        real_tab, imag_tab = fourier_rows(block_id * block_size, block_size, AZ)
        with_real = product(real_tab, filtered)
        with_imag = product(imag_tab, filtered)
        focus_re = with_real[:, :col_count] + with_imag[:, col_count:]
        focus_im = with_real[:, col_count:] - with_imag[:, :col_count]
        return jnp.stack([focus_re, focus_im]).astype(jnp.bfloat16)

    pieces = lax.map(inverse_block, block_ids)
    return pieces.transpose(1, 0, 2, 3).reshape(2, AZ, col_count)


def kernel_taps(fraction):
    half_taps = TAPS // 2
    position = jnp.arange(TAPS, dtype=jnp.int32).astype(jnp.float32) - (half_taps - 1) - fraction
    return jnp.sinc(position) * (0.5 + 0.5 * jnp.cos(math.pi * position / half_taps))


def interpolate(window, tap_weights, out_rows):
    running = tap_weights[0] * window[:, 0:out_rows].astype(jnp.float32)
    for tap_id in range(1, TAPS):
        running = running + tap_weights[tap_id] * window[:, tap_id : tap_id + out_rows].astype(
            jnp.float32
        )
    return running.astype(jnp.bfloat16)


def own_power(block_data):
    as_float = block_data.astype(jnp.float32)
    return as_float[0] * as_float[0] + as_float[1] * as_float[1]


def pair_terms(own_block, other_block):
    own_f = own_block.astype(jnp.float32)
    other_f = other_block.astype(jnp.float32)
    cross_re = own_f[0] * other_f[0] + own_f[1] * other_f[1]
    cross_im = own_f[1] * other_f[0] - own_f[0] * other_f[1]
    power_b = other_f[0] * other_f[0] + other_f[1] * other_f[1]
    return jnp.stack([cross_re, cross_im, power_b])


def box_sum(values, out_rows):
    half_rg = WIN_RG // 2
    padded = jnp.pad(values, ((0, 0), (0, 0), (half_rg, half_rg)))
    sample_count = values.shape[2]
    across = padded[:, :, 0:sample_count]
    for offset_id in range(1, WIN_RG):
        across = across + padded[:, :, offset_id : offset_id + sample_count]
    running = across[:, 0:out_rows]
    for offset_id in range(1, WIN_AZ):
        running = running + across[:, offset_id : offset_id + out_rows]
    return running


def coherence_of(box_terms, power_box):
    denominator = jnp.sqrt(power_box * box_terms[2] + epsilon)
    return jnp.stack([box_terms[0] / denominator, box_terms[1] / denominator]).astype(jnp.bfloat16)


def body(raw_echo, range_rate, azimuth_rate, line_offset, frac_shift):
    echo_lines = raw_echo[0]
    line_count = echo_lines.shape[1]
    compressed = range_compress(echo_lines, range_rate, local_dot).astype(jnp.bfloat16)
    columns = lax.all_to_all(compressed, "swath", split_axis=2, concat_axis=1, tiled=True)
    focused = azimuth_compress(columns, azimuth_rate, local_dot)
    tap_weights = kernel_taps(frac_shift[0])
    shift_lines = line_offset[0]
    rim_lines = MAX_OFF + TAPS - 1
    extended = jnp.concatenate([focused, focused[:, :rim_lines]], axis=1)
    window = lax.dynamic_slice_in_dim(extended, shift_lines, AZ + TAPS - 1, 1)
    aligned = interpolate(window, tap_weights, AZ)
    coregistered = lax.all_to_all(aligned, "swath", split_axis=1, concat_axis=2, tiled=True)
    half_win = WIN_AZ // 2
    bordered = with_halo(coregistered, (("swath", 1),), half_win)
    power_box = box_sum(own_power(bordered)[None], line_count)[0]
    partner = bordered
    results = []
    for step_id in range(SPAN):
        partner = shifted(partner, "date", -1)
        box_terms = box_sum(pair_terms(bordered, partner), line_count)
        results.append(coherence_of(box_terms, power_box))
    return (coregistered[None], jnp.stack(results)[None])


def solution(mesh):
    placed = (P("date", None, "swath", None), P(), P("swath"), P("date"), P("date"))
    return jax.shard_map(
        body,
        mesh=mesh,
        in_specs=placed,
        out_specs=(P("date", None, "swath", None), P("date", None, None, "swath", None)),
        check_vma=False,
    )
```

profile of v0, /device:TPU:0, one launch (start us, length us, event | category | flops | bytes accessed | tf_op | source)
XLA Modules:
  0.0 561.6 jit_solution(16169984269317625232)
XLA Ops:
  4.7 109.0 %while.38 = (s32[]{:T(128)}, bf16[8,2,256,256]{2,3,0,1:T(8,128)(2,1)}, s32[8]{0:T(128)S(1)}, bf16[512,3072]{1,0:T(8,128)(2,1)}, f32[]{:T(128)}, /*index=5*/s32[]{:T(128)}, s32[1]{0:T(128)}, s32[]{:T(128)}, s32[]{:T(128)}) while((s32[]{:T(128)}, bf16[8,2,256,256]{2,3,0,1:T(8,128)(2,1)}, s32[8]{0:T(128)S(1)}, ...), condition=%wide.region_1.2_spmd.clone.clone, body=%wide.region_0.1_spmd.clone.clone.sunk | while | flops 679673856 | bytes 6554795 | solution.py:76
  5.9 5.7 %fusion.152 = f32[512,256]{1,0:T(8,128)S(1)} fusion(bf16[512,3072]{1,0:T(8,128)(2,1)} %get-tuple-element.374, s32[]{:T(128)S(6)} %select_n.155, f32[]{:T(128)} %get-tuple-element.375), kind=kOutput, calls=%fused_computation.89.clone.1 | convolution fusion | flops 339476480 | bytes 1835524 | tf_op jit(solution)/shard_map/while/body/eval_jaxpr/dot_general | solution.py:41
  11.6 5.7 %fusion.151 = f32[512,256]{1,0:T(8,128)S(1)} fusion(bf16[512,3072]{1,0:T(8,128)(2,1)} %get-tuple-element.374, s32[]{:T(128)S(6)} %select_n.155, f32[]{:T(128)} %get-tuple-element.375), kind=kOutput, calls=%fused_computation.87.clone.1 | convolution fusion | flops 339804160 | bytes 1835524 | tf_op jit(solution)/shard_map/while/body/eval_jaxpr/dot_general | solution.py:41
  19.5 5.7 %fusion.152 = f32[512,256]{1,0:T(8,128)S(1)} fusion(bf16[512,3072]{1,0:T(8,128)(2,1)} %get-tuple-element.374, s32[]{:T(128)S(6)} %select_n.155, f32[]{:T(128)} %get-tuple-element.375), kind=kOutput, calls=%fused_computation.89.clone.1 | convolution fusion | flops 339476480 | bytes 1835524 | tf_op jit(solution)/shard_map/while/body/eval_jaxpr/dot_general | solution.py:41
  25.2 5.7 %fusion.151 = f32[512,256]{1,0:T(8,128)S(1)} fusion(bf16[512,3072]{1,0:T(8,128)(2,1)} %get-tuple-element.374, s32[]{:T(128)S(6)} %select_n.155, f32[]{:T(128)} %get-tuple-element.375), kind=kOutput, calls=%fused_computation.87.clone.1 | convolution fusion | flops 339804160 | bytes 1835524 | tf_op jit(solution)/shard_map/while/body/eval_jaxpr/dot_general | solution.py:41
  33.1 5.7 %fusion.152 = f32[512,256]{1,0:T(8,128)S(1)} fusion(bf16[512,3072]{1,0:T(8,128)(2,1)} %get-tuple-element.374, s32[]{:T(128)S(6)} %select_n.155, f32[]{:T(128)} %get-tuple-element.375), kind=kOutput, calls=%fused_computation.89.clone.1 | convolution fusion | flops 339476480 | bytes 1835524 | tf_op jit(solution)/shard_map/while/body/eval_jaxpr/dot_general | solution.py:41
  38.8 5.7 %fusion.151 = f32[512,256]{1,0:T(8,128)S(1)} fusion(bf16[512,3072]{1,0:T(8,128)(2,1)} %get-tuple-element.374, s32[]{:T(128)S(6)} %select_n.155, f32[]{:T(128)} %get-tuple-element.375), kind=kOutput, calls=%fused_computation.87.clone.1 | convolution fusion | flops 339804160 | bytes 1835524 | tf_op jit(solution)/shard_map/while/body/eval_jaxpr/dot_general | solution.py:41
  46.7 5.7 %fusion.152 = f32[512,256]{1,0:T(8,128)S(1)} fusion(bf16[512,3072]{1,0:T(8,128)(2,1)} %get-tuple-element.374, s32[]{:T(128)S(6)} %select_n.155, f32[]{:T(128)} %get-tuple-element.375), kind=kOutput, calls=%fused_computation.89.clone.1 | convolution fusion | flops 339476480 | bytes 1835524 | tf_op jit(solution)/shard_map/while/body/eval_jaxpr/dot_general | solution.py:41
  52.4 5.7 %fusion.151 = f32[512,256]{1,0:T(8,128)S(1)} fusion(bf16[512,3072]{1,0:T(8,128)(2,1)} %get-tuple-element.374, s32[]{:T(128)S(6)} %select_n.155, f32[]{:T(128)} %get-tuple-element.375), kind=kOutput, calls=%fused_computation.87.clone.1 | convolution fusion | flops 339804160 | bytes 1835524 | tf_op jit(solution)/shard_map/while/body/eval_jaxpr/dot_general | solution.py:41
  60.3 5.7 %fusion.152 = f32[512,256]{1,0:T(8,128)S(1)} fusion(bf16[512,3072]{1,0:T(8,128)(2,1)} %get-tuple-element.374, s32[]{:T(128)S(6)} %select_n.155, f32[]{:T(128)} %get-tuple-element.375), kind=kOutput, calls=%fused_computation.89.clone.1 | convolution fusion | flops 339476480 | bytes 1835524 | tf_op jit(solution)/shard_map/while/body/eval_jaxpr/dot_general | solution.py:41
  66.1 5.7 %fusion.151 = f32[512,256]{1,0:T(8,128)S(1)} fusion(bf16[512,3072]{1,0:T(8,128)(2,1)} %get-tuple-element.374, s32[]{:T(128)S(6)} %select_n.155, f32[]{:T(128)} %get-tuple-element.375), kind=kOutput, calls=%fused_computation.87.clone.1 | convolution fusion | flops 339804160 | bytes 1835524 | tf_op jit(solution)/shard_map/while/body/eval_jaxpr/dot_general | solution.py:41
  74.0 5.7 %fusion.152 = f32[512,256]{1,0:T(8,128)S(1)} fusion(bf16[512,3072]{1,0:T(8,128)(2,1)} %get-tuple-element.374, s32[]{:T(128)S(6)} %select_n.155, f32[]{:T(128)} %get-tuple-element.375), kind=kOutput, calls=%fused_computation.89.clone.1 | convolution fusion | flops 339476480 | bytes 1835524 | tf_op jit(solution)/shard_map/while/body/eval_jaxpr/dot_general | solution.py:41
  79.7 5.7 %fusion.151 = f32[512,256]{1,0:T(8,128)S(1)} fusion(bf16[512,3072]{1,0:T(8,128)(2,1)} %get-tuple-element.374, s32[]{:T(128)S(6)} %select_n.155, f32[]{:T(128)} %get-tuple-element.375), kind=kOutput, calls=%fused_computation.87.clone.1 | convolution fusion | flops 339804160 | bytes 1835524 | tf_op jit(solution)/shard_map/while/body/eval_jaxpr/dot_general | solution.py:41
  87.6 5.7 %fusion.152 = f32[512,256]{1,0:T(8,128)S(1)} fusion(bf16[512,3072]{1,0:T(8,128)(2,1)} %get-tuple-element.374, s32[]{:T(128)S(6)} %select_n.155, f32[]{:T(128)} %get-tuple-element.375), kind=kOutput, calls=%fused_computation.89.clone.1 | convolution fusion | flops 339476480 | bytes 1835524 | tf_op jit(solution)/shard_map/while/body/eval_jaxpr/dot_general | solution.py:41
  93.3 5.7 %fusion.151 = f32[512,256]{1,0:T(8,128)S(1)} fusion(bf16[512,3072]{1,0:T(8,128)(2,1)} %get-tuple-element.374, s32[]{:T(128)S(6)} %select_n.155, f32[]{:T(128)} %get-tuple-element.375), kind=kOutput, calls=%fused_computation.87.clone.1 | convolution fusion | flops 339804160 | bytes 1835524 | tf_op jit(solution)/shard_map/while/body/eval_jaxpr/dot_general | solution.py:41
  101.2 5.7 %fusion.152 = f32[512,256]{1,0:T(8,128)S(1)} fusion(bf16[512,3072]{1,0:T(8,128)(2,1)} %get-tuple-element.374, s32[]{:T(128)S(6)} %select_n.155, f32[]{:T(128)} %get-tuple-element.375), kind=kOutput, calls=%fused_computation.89.clone.1 | convolution fusion | flops 339476480 | bytes 1835524 | tf_op jit(solution)/shard_map/while/body/eval_jaxpr/dot_general | solution.py:41
  106.9 5.7 %fusion.151 = f32[512,256]{1,0:T(8,128)S(1)} fusion(bf16[512,3072]{1,0:T(8,128)(2,1)} %get-tuple-element.374, s32[]{:T(128)S(6)} %select_n.155, f32[]{:T(128)} %get-tuple-element.375), kind=kOutput, calls=%fused_computation.87.clone.1 | convolution fusion | flops 339804160 | bytes 1835524 | tf_op jit(solution)/shard_map/while/body/eval_jaxpr/dot_general | solution.py:41
  113.7 5.8 %copy.18 = bf16[2,256,2048]{1,0,2:T(2,128)(2,1)} copy(bf16[2,256,2048]{1,2,0:T(8,128)(2,1)} %bitcast.110) | data formatting | bytes 4194304 | tf_op jit(solution)/shard_map/convert_element_type | solution.py:177
  119.4 6.5 %all-to-all-start = ((bf16[2,256,2048]{1,0,2:T(2,128)(2,1)}), bf16[2,256,2048]{1,0,2:T(2,128)(2,1)S(1)}, u32[]{:S(2)}, u32[]{:S(2)}) async-start(bf16[2,256,2048]{1,0,2:T(2,128)(2,1)} %copy.18), calls=%async_computation | async-start | bytes 4194304 | tf_op jit(solution)/shard_map/all_to_all | solution.py:178
  128.0 46.1 %all-to-all-done = bf16[2,256,2048]{1,0,2:T(2,128)(2,1)S(1)} async-done(((bf16[2,256,2048]{1,0,2:T(2,128)(2,1)}), bf16[2,256,2048]{1,0,2:T(2,128)(2,1)S(1)}, u32[]{:S(2)}, u32[]{:S(2)}) %all-to-all-start) | async-done | bytes 2097184 | tf_op jit(solution)/shard_map/all_to_all | solution.py:178
  177.4 60.3 %while.36 = (s32[]{:T(128)}, bf16[4,256,1024]{2,1,0:T(8,128)(2,1)}, s32[4]{0:T(128)S(1)}, bf16[1024,1024]{1,0:T(8,128)(2,1)}, f32[512]{0:T(512)S(1)}, /*index=5*/s32[]{:T(128)}, s32[1]{0:T(128)}) while((s32[]{:T(128)}, bf16[4,256,1024]{2,1,0:T(8,128)(2,1)}, s32[4]{0:T(128)S(1)}, bf16[1024,1024]{1,0:T(8,128)(2,1)}, f32[512]{0:T(512)S(1)}, ...), condition=%wide.region_3.4_spmd, body=%wide.region_2.3_spmd.sunk | while | flops 1085018880 | bytes 18361492 | solution.py:113
  178.6 6.1 %fusion.141 = f32[256,1024]{1,0:T(8,128)S(1)} fusion(bf16[1024,1024]{1,0:T(8,128)(2,1)} %get-tuple-element.397, s32[256]{0:T(256)S(1)} %iota_add_fusion.4), kind=kOutput, calls=%fused_computation.13.clone.1 | convolution fusion | flops 541065216 | bytes 3146752 | tf_op jit(solution)/shard_map/while/body/eval_jaxpr/dot_general | solution.py:41
  184.8 4.4 fusion.140
  193.7 6.1 %fusion.141 = f32[256,1024]{1,0:T(8,128)S(1)} fusion(bf16[1024,1024]{1,0:T(8,128)(2,1)} %get-tuple-element.397, s32[256]{0:T(256)S(1)} %iota_add_fusion.4), kind=kOutput, calls=%fused_computation.13.clone.1 | convolution fusion | flops 541065216 | bytes 3146752 | tf_op jit(solution)/shard_map/while/body/eval_jaxpr/dot_general | solution.py:41
  208.8 6.1 %fusion.141 = f32[256,1024]{1,0:T(8,128)S(1)} fusion(bf16[1024,1024]{1,0:T(8,128)(2,1)} %get-tuple-element.397, s32[256]{0:T(256)S(1)} %iota_add_fusion.4), kind=kOutput, calls=%fused_computation.13.clone.1 | convolution fusion | flops 541065216 | bytes 3146752 | tf_op jit(solution)/shard_map/while/body/eval_jaxpr/dot_general | solution.py:41
  214.9 4.4 fusion.140
  223.8 6.1 %fusion.141 = f32[256,1024]{1,0:T(8,128)S(1)} fusion(bf16[1024,1024]{1,0:T(8,128)(2,1)} %get-tuple-element.397, s32[256]{0:T(256)S(1)} %iota_add_fusion.4), kind=kOutput, calls=%fused_computation.13.clone.1 | convolution fusion | flops 541065216 | bytes 3146752 | tf_op jit(solution)/shard_map/while/body/eval_jaxpr/dot_general | solution.py:41
  237.7 49.2 %while.37 = (s32[]{:T(128)}, bf16[4,2,256,512]{3,2,0,1:T(8,128)(2,1)S(1)}, s32[4]{0:T(128)S(1)}, bf16[1024,1024]{1,0:T(8,128)(2,1)}, s32[]{:T(128)}, /*index=5*/s32[1]{0:T(128)}) while((s32[]{:T(128)}, bf16[4,2,256,512]{3,2,0,1:T(8,128)(2,1)S(1)}, s32[4]{0:T(128)S(1)}, bf16[1024,1024]{1,0:T(8,128)(2,1)}, s32[]{:T(128)}, ...), condition=%wide.region_5.6_spmd, body=%wide.region_4.5_spmd.sunk | while | flops 1083965696 | bytes 18353288 | solution.py:123
  239.3 6.1 %fusion.146 = f32[256,1024]{1,0:T(8,128)S(1)} fusion(bf16[1024,1024]{1,0:T(8,128)(2,1)} %get-tuple-element.416, s32[256]{0:T(256)S(1)} %iota_add_fusion.5), kind=kOutput, calls=%fused_computation.57.clone.1 | convolution fusion | flops 541065216 | bytes 3146752 | tf_op jit(solution)/shard_map/while/body/eval_jaxpr/dot_general | solution.py:41
  245.5 4.4 fusion.145
  251.5 6.1 %fusion.146 = f32[256,1024]{1,0:T(8,128)S(1)} fusion(bf16[1024,1024]{1,0:T(8,128)(2,1)} %get-tuple-element.416, s32[256]{0:T(256)S(1)} %iota_add_fusion.5), kind=kOutput, calls=%fused_computation.57.clone.1 | convolution fusion | flops 541065216 | bytes 3146752 | tf_op jit(solution)/shard_map/while/body/eval_jaxpr/dot_general | solution.py:41
  263.7 6.1 %fusion.146 = f32[256,1024]{1,0:T(8,128)S(1)} fusion(bf16[1024,1024]{1,0:T(8,128)(2,1)} %get-tuple-element.416, s32[256]{0:T(256)S(1)} %iota_add_fusion.5), kind=kOutput, calls=%fused_computation.57.clone.1 | convolution fusion | flops 541065216 | bytes 3146752 | tf_op jit(solution)/shard_map/while/body/eval_jaxpr/dot_general | solution.py:41
  276.0 6.1 %fusion.146 = f32[256,1024]{1,0:T(8,128)S(1)} fusion(bf16[1024,1024]{1,0:T(8,128)(2,1)} %get-tuple-element.416, s32[256]{0:T(256)S(1)} %iota_add_fusion.5), kind=kOutput, calls=%fused_computation.57.clone.1 | convolution fusion | flops 541065216 | bytes 3146752 | tf_op jit(solution)/shard_map/while/body/eval_jaxpr/dot_general | solution.py:41
  288.8 9.2 %add_convert_fusion.1 = bf16[2,1024,512]{2,1,0:T(8,128)(2,1)S(1)} fusion(bf16[2,1031,512]{2,1,0:T(8,128)(2,1)S(1)} %fusion.94, f32[]{:T(128)} %bitcast.27, f32[]{:T(128)} %bitcast.26, f32[]{:T(128)} %bitcast.25, f32[]{:T(128)} %bitcast.24, f32[]{:T(128)} %bitcast.23, f32[]{:T(128)} %bitcast.22, f32[]{:T(128)} %bitcast.21, f32[]{:T(128)} %bitcast.7), kind=kLoop, calls=%fused_computation.146 | loop fusion | flops 25165824 | bytes 18874400 | tf_op jit(solution)/shard_map/convert_element_type | solution.py:139
  300.1 50.2 %all_to_all.33 = bf16[2,1024,512]{2,0,1:T(2,128)(2,1)S(1)} all-to-all(bf16[2,1024,512]{2,0,1:T(2,128)(2,1)S(1)} %copy.23), channel_id=1, replica_groups=mesh['date'=8,'swath'=4] {'swath'}, dimensions={1} | all-to-all | bytes 4194304 | tf_op jit(solution)/shard_map/all_to_all | solution.py:186
  367.6 5.7 %fusion.112 = (f32[2,266,2048]{1,2,0:T(8,128)}, bf16[2,266,2048]{1,2,0:T(8,128)(2,1)}) fusion(bf16[2,5,2048]{1,2,0:T(8,128)(2,1)} %copy.30, bf16[2,256,2048]{1,2,0:T(8,128)(2,1)S(1)} %bitcast.98, bf16[2,5,2048]{1,2,0:T(8,128)(2,1)S(1)} %copy.29), kind=kLoop, calls=%fused_computation.204 | loop fusion | flops 7626752 | bytes 8716288 | tf_op jit(solution)/shard_map/convert_element_type | solution.py:148
  373.4 6.7 %copy.31 = bf16[2,266,2048]{2,0,1:T(2,128)(2,1)} copy(bf16[2,266,2048]{1,2,0:T(8,128)(2,1)} %get-tuple-element.225) | data formatting | bytes 4358144 | tf_op jit(solution)/shard_map/concatenate | solution.py:30
  382.4 22.4 %collective-permute-done.2 = bf16[2,266,2048]{2,0,1:T(2,128)(2,1)} collective-permute-done((bf16[2,266,2048]{2,0,1:T(2,128)(2,1)}, bf16[2,266,2048]{2,0,1:T(2,128)(2,1)}, u32[]{:S(2)}, u32[]{:S(2)}) %collective-permute-start.2) | collective-permute-done | bytes 2179104 | tf_op jit(solution)/shard_map/ppermute | solution.py:37
  404.8 6.6 %copy.32 = bf16[2,266,2048]{1,2,0:T(8,128)(2,1)} copy(bf16[2,266,2048]{2,0,1:T(2,128)(2,1)} %collective-permute-done.2) | data formatting | bytes 4358144 | tf_op jit(solution)/shard_map/ppermute | solution.py:37
  425.9 6.3 %slice_add_fusion.4 = f32[3,266,2048]{1,2,0:T(8,128)} fusion(f32[3,266,2048]{1,2,0:T(8,128)S(1)} %pad_maximum_fusion), kind=kLoop, calls=%fused_computation.123 | loop fusion | flops 6537216 | bytes 13074432 | tf_op jit(solution)/shard_map/add | solution.py:162
  432.2 38.2 %slice_add_fusion.15 = f32[3,256,2048]{1,2,0:T(8,128)} fusion(f32[3,266,2048]{1,2,0:T(8,128)} %slice_add_fusion.4), kind=kLoop, calls=%fused_computation.135 | loop fusion | flops 15728640 | bytes 75497472 | tf_op jit(solution)/shard_map/add | solution.py:165
  470.4 6.7 %copy.33 = bf16[2,266,2048]{1,2,0:T(8,128)(2,1)} copy(bf16[2,266,2048]{2,0,1:T(2,128)(2,1)} %collective-permute-done.3) | data formatting | bytes 4358144 | tf_op jit(solution)/shard_map/ppermute | solution.py:37
  480.2 5.1 multiply_add_fusion.1
  489.6 6.1 %slice_add_fusion.3 = f32[3,266,2048]{1,2,0:T(8,128)} fusion(f32[3,266,2048]{1,2,0:T(8,128)S(1)} %pad_maximum_fusion.1), kind=kLoop, calls=%fused_computation.121 | loop fusion | flops 6537216 | bytes 13074432 | tf_op jit(solution)/shard_map/add | solution.py:162
  495.7 38.5 %slice_add_fusion.5 = f32[3,256,2048]{1,2,0:T(8,128)} fusion(f32[3,266,2048]{1,2,0:T(8,128)} %slice_add_fusion.3), kind=kLoop, calls=%fused_computation.125 | loop fusion | flops 15728640 | bytes 75497472 | tf_op jit(solution)/shard_map/add | solution.py:165
  534.2 7.3 %slice_add_fusion.25 = f32[1,266,2048]{1,2,0:T(8,128)S(1)} fusion(f32[1,266,2048]{1,2,0:T(8,128)} %get-tuple-element.238), kind=kLoop, calls=%fused_computation.152 | loop fusion | flops 2179072 | bytes 4358144 | tf_op jit(solution)/shard_map/add | solution.py:162
  541.5 8.5 %fusion.103 = (bf16[1,1,256,2048]{2,3,1,0:T(8,128)(2,1)}, f32[1,256,2048]{1,2,0:T(8,128)}) fusion(f32[3,256,2048]{1,2,0:T(8,128)} %slice_add_fusion.15, f32[1,266,2048]{1,2,0:T(8,128)S(1)} %slice_add_fusion.25), kind=kLoop, calls=%fused_computation.186 | loop fusion | flops 7340032 | bytes 30408704 | tf_op jit(solution)/shard_map/stack | solution.py:171
  554.9 6.2 %copy.35 = bf16[1,2,2,256,2048]{4,3,2,1,0:T(8,128)(2,1)} copy(bf16[1,2,2,256,2048]{3,4,2,1,0:T(8,128)(2,1)} %maximum_bitcast_fusion.2) | data formatting | bytes 8388608
  (169 shorter events, 111.4 us)
Async XLA Ops:
  0.6 2.1 copy-start
  119.4 54.7 %all-to-all-start = ((bf16[2,256,2048]{1,0,2:T(2,128)(2,1)}), bf16[2,256,2048]{1,0,2:T(2,128)(2,1)S(1)}, u32[]{:S(2)}, u32[]{:S(2)}) async-start(bf16[2,256,2048]{1,0,2:T(2,128)(2,1)} %copy.18), calls=%async_computation | async-start | bytes 4194304 | tf_op jit(solution)/shard_map/all_to_all | solution.py:178
  175.1 2.2 copy-start.4
  177.4 60.3 %copy-start.2 = (bf16[4,2,256,512]{3,2,0,1:T(8,128)(2,1)S(1)}, bf16[4,2,256,512]{3,2,0,1:T(8,128)(2,1)}, u32[]{:S(2)}) copy-start(bf16[4,2,256,512]{3,2,0,1:T(8,128)(2,1)} %custom-call.1) | copy-start | bytes 6291460
  178.6 6.2 %copy-start.3 = (bf16[1024,1024]{1,0:T(8,128)(2,1)S(1)}, bf16[1024,1024]{1,0:T(8,128)(2,1)}, u32[]{:S(2)}) copy-start(bf16[1024,1024]{1,0:T(8,128)(2,1)} %get-tuple-element.397) | copy-start | bytes 6291460 | tf_op jit(solution)/shard_map/while
  193.7 6.2 %copy-start.3 = (bf16[1024,1024]{1,0:T(8,128)(2,1)S(1)}, bf16[1024,1024]{1,0:T(8,128)(2,1)}, u32[]{:S(2)}) copy-start(bf16[1024,1024]{1,0:T(8,128)(2,1)} %get-tuple-element.397) | copy-start | bytes 6291460 | tf_op jit(solution)/shard_map/while
  208.8 6.2 %copy-start.3 = (bf16[1024,1024]{1,0:T(8,128)(2,1)S(1)}, bf16[1024,1024]{1,0:T(8,128)(2,1)}, u32[]{:S(2)}) copy-start(bf16[1024,1024]{1,0:T(8,128)(2,1)} %get-tuple-element.397) | copy-start | bytes 6291460 | tf_op jit(solution)/shard_map/while
  223.8 6.2 %copy-start.3 = (bf16[1024,1024]{1,0:T(8,128)(2,1)S(1)}, bf16[1024,1024]{1,0:T(8,128)(2,1)}, u32[]{:S(2)}) copy-start(bf16[1024,1024]{1,0:T(8,128)(2,1)} %get-tuple-element.397) | copy-start | bytes 6291460 | tf_op jit(solution)/shard_map/while
  239.3 6.2 %copy-start.5 = (bf16[1024,1024]{1,0:T(8,128)(2,1)S(1)}, bf16[1024,1024]{1,0:T(8,128)(2,1)}, u32[]{:S(2)}) copy-start(bf16[1024,1024]{1,0:T(8,128)(2,1)} %get-tuple-element.416) | copy-start | bytes 6291460 | tf_op jit(solution)/shard_map/while
  251.5 6.2 %copy-start.5 = (bf16[1024,1024]{1,0:T(8,128)(2,1)S(1)}, bf16[1024,1024]{1,0:T(8,128)(2,1)}, u32[]{:S(2)}) copy-start(bf16[1024,1024]{1,0:T(8,128)(2,1)} %get-tuple-element.416) | copy-start | bytes 6291460 | tf_op jit(solution)/shard_map/while
  263.7 6.2 %copy-start.5 = (bf16[1024,1024]{1,0:T(8,128)(2,1)S(1)}, bf16[1024,1024]{1,0:T(8,128)(2,1)}, u32[]{:S(2)}) copy-start(bf16[1024,1024]{1,0:T(8,128)(2,1)} %get-tuple-element.416) | copy-start | bytes 6291460 | tf_op jit(solution)/shard_map/while
  275.9 6.2 %copy-start.5 = (bf16[1024,1024]{1,0:T(8,128)(2,1)S(1)}, bf16[1024,1024]{1,0:T(8,128)(2,1)}, u32[]{:S(2)}) copy-start(bf16[1024,1024]{1,0:T(8,128)(2,1)} %get-tuple-element.416) | copy-start | bytes 6291460 | tf_op jit(solution)/shard_map/while
  357.8 3.8 collective-permute-start
  360.3 5.9 %collective-permute-start.1 = (bf16[2,5,2048]{2,0,1:T(2,128)(2,1)S(1)}, bf16[2,5,2048]{2,0,1:T(2,128)(2,1)S(1)}, u32[]{:S(2)}, u32[]{:S(2)}) collective-permute-start(bf16[2,5,2048]{2,0,1:T(2,128)(2,1)S(1)} %copy.28), channel_id=1, source_target_pairs={{1,0},{2,1},{3,2},{5,4},{6,5},{7,6},{9,8},{10,9},{11,10},{13,12},{... | collective-permute-start | bytes 122888 | tf_op jit(solution)/shard_map/ppermute | solution.py:29
  380.0 24.7 %collective-permute-start.2 = (bf16[2,266,2048]{2,0,1:T(2,128)(2,1)}, bf16[2,266,2048]{2,0,1:T(2,128)(2,1)}, u32[]{:S(2)}, u32[]{:S(2)}) collective-permute-start(bf16[2,266,2048]{2,0,1:T(2,128)(2,1)} %copy.31), channel_id=1, source_target_pairs={{4,0},{8,4},{12,8},{16,12},{20,16},{24,20},{28,24},{0,28},{5,1},{9... | collective-permute-start | bytes 6537224 | tf_op jit(solution)/shard_map/ppermute | solution.py:37
  404.8 9.1 %slice-start = ((s8[6291456]{0:T(1024)(128)(4,1)}), s8[2097152]{0:T(1024)(128)(4,1)S(1)}, s32[]{:S(2)}) async-start(s8[6291456]{0:T(1024)(128)(4,1)} %bitcast.91), calls=%async_computation.2 | async-start | bytes 4194304
  411.4 3.1 slice-start.1
  418.7 51.7 %collective-permute-start.3 = (bf16[2,266,2048]{2,0,1:T(2,128)(2,1)}, bf16[2,266,2048]{2,0,1:T(2,128)(2,1)}, u32[]{:S(2)}, u32[]{:S(2)}) collective-permute-start(bf16[2,266,2048]{2,0,1:T(2,128)(2,1)} %collective-permute-done.2), channel_id=1, source_target_pairs={{4,0},{8,4},{12,8},{16,12},{20,16},{24,20},{28,24},{0,28},{5,1},{9... | collective-permute-start | bytes 6537224 | tf_op jit(solution)/shard_map/ppermute | solution.py:37
  470.4 9.1 %slice-start.2 = ((s8[6291456]{0:T(1024)(128)(4,1)}), s8[2097152]{0:T(1024)(128)(4,1)S(1)}, s32[]{:S(2)}) async-start(s8[6291456]{0:T(1024)(128)(4,1)} %bitcast.93), calls=%async_computation.4 | async-start | bytes 4194304
  477.1 3.1 slice-start.3
  534.2 15.8 %slice-start.4 = ((s8[6291456]{0:T(1024)(128)(4,1)}), s8[4194304]{0:T(1024)(128)(4,1)S(1)}, s32[]{:S(2)}) async-start(s8[6291456]{0:T(1024)(128)(4,1)} %bitcast.95), calls=%async_computation.6 | async-start | bytes 8388608
  534.2 15.8 %slice-start.6 = ((s8[6291456]{0:T(1024)(128)(4,1)}), s8[4194304]{0:T(1024)(128)(4,1)S(1)}, s32[]{:S(2)}) async-start(s8[6291456]{0:T(1024)(128)(4,1)} %bitcast.100), calls=%async_computation.8 | async-start | bytes 8388608
  541.5 8.5 %slice-start.5 = ((s8[6291456]{0:T(1024)(128)(4,1)}), s8[2097152]{0:T(1024)(128)(4,1)S(1)}, s32[]{:S(2)}) async-start(s8[6291456]{0:T(1024)(128)(4,1)} %bitcast.95), calls=%async_computation.7 | async-start | bytes 4194304
  541.5 8.5 %slice-start.7 = ((s8[6291456]{0:T(1024)(128)(4,1)}), s8[2097152]{0:T(1024)(128)(4,1)S(1)}, s32[]{:S(2)}) async-start(s8[6291456]{0:T(1024)(128)(4,1)} %bitcast.100), calls=%async_computation.9 | async-start | bytes 4194304
  550.0 2.7 copy-start.1
where the time goes:
time: 571 us; the launch traced here: 562 us
  matrix products  176 us (31%)
  other arithmetic  168 us (29%)
  waiting for transfers between devices  72.6 us (13%)
  local copies, waits for them, and re-layouts  67.4 us (12%)
  blocking collectives  50.2 us (9%)
  starting transfers between devices  12.7 us (2%)
  loops' own time  10.8 us (2%)
    dot_general x32, matrix products, local_dot(): return jnp.dot(left, right, preferred_element_type=jnp.float32)  176 us
    add x2, other arithmetic, box_sum(): running = running + across[:, offset_id:offset_id + out_rows]  76.7 us
    all_to_all x1, blocking collectives, body(): lax.all_to_all(aligned, 'swath', split_axis=1, concat_axis=2, tiled=True)  50.2 us
    all_to_all x1, waiting for transfers between devices, body(): lax.all_to_all(compressed, 'swath', split_axis=2, concat_axis=1, tiled=True)  46.1 us
    ppermute x2, waiting for transfers between devices, shifted(): return lax.ppermute(block, axis, route)  22.4 us
    add x3, other arithmetic, box_sum(): across = across + padded[:, :, offset_id:offset_id + sample_count]  19.6 us
    ppermute x2, local copies, waits for them, and re-layouts, shifted(): return lax.ppermute(block, axis, route)  13.3 us
  transfers between devices with their start and end apart: 5, of which 3 were waited for; matrix products, arithmetic and copies ran while one was open for 9% of the time, Pallas kernels for 0%

commit v1 on v0

v1 whole, which is shorter than its diff:
```python
import functools
import math

import jax
import jax.numpy as jnp
from jax import lax
from jax.experimental import pallas as pl
from jax.experimental.pallas import tpu as pltpu
from jax.sharding import PartitionSpec as P

TAPS = 8
WIN_AZ = 11
WIN_RG = 5
SPAN = 2
LANES = 128
PACK = 16
RIM = 8
LINE_STEP = 64

two_pi = 2.0 * math.pi
epsilon = 1e-06
F32 = jnp.float32
BF16 = jnp.bfloat16


def params(mib):
    return pltpu.CompilerParams(vmem_limit_bytes=mib * 1024 * 1024)


def cost(flops, bytes_accessed):
    return pl.CostEstimate(flops=int(flops), bytes_accessed=int(bytes_accessed), transcendentals=0)


def vmem():
    return pl.BlockSpec(memory_space=pltpu.VMEM)


def smem():
    return pl.BlockSpec(memory_space=pltpu.SMEM)


def sincos_turns(turns):
    quarter = jnp.floor(turns * 4.0 + 0.5)
    x = (turns - quarter * 0.25) * two_pi
    x2 = x * x
    s = x * (1.0 + x2 * (-1.0 / 6 + x2 * (1.0 / 120 + x2 * (-1.0 / 5040 + x2 * (1.0 / 362880)))))
    c = 1.0 + x2 * (-0.5 + x2 * (1.0 / 24 + x2 * (-1.0 / 720 + x2 * (1.0 / 40320))))
    quad = quarter.astype(jnp.int32) & 3
    odd = (quad & 1) == 1
    sin_v = jnp.where(odd, c, s)
    cos_v = jnp.where(odd, s, c)
    sin_v = jnp.where(quad >= 2, -sin_v, sin_v)
    cos_v = jnp.where((quad == 1) | (quad == 2), -cos_v, cos_v)
    return sin_v, cos_v


def build_chirp(rate_ref, table_ref, base_ref, pulse_len, width):
    top = pulse_len + width - PACK
    span = base_ref.shape[2]
    lag = (
        lax.broadcasted_iota(jnp.int32, (PACK, span), 0)
        + top
        - lax.broadcasted_iota(jnp.int32, (PACK, span), 1)
    )
    inside = (lag >= 0) & (lag < pulse_len)
    offset = (lag.astype(F32) - 0.5 * pulse_len) / pulse_len
    turns = 0.5 * pulse_len * rate_ref[0] * offset * offset
    sin_v, cos_v = sincos_turns(turns)
    amplitude = 1.0 / math.sqrt(pulse_len)
    base_ref[0] = jnp.where(inside, cos_v * amplitude, 0.0)
    base_ref[1] = jnp.where(inside, -sin_v * amplitude, 0.0)
    for block in range((pulse_len + width) // PACK):
        start = top - PACK * block
        aligned = start // LANES * LANES
        skew = start - aligned
        size = width + LANES
        for part in range(2):
            window = base_ref[part, :, aligned : aligned + size]
            if skew:
                window = pltpu.roll(window, size - skew, 1)
            table_ref[block * PACK : (block + 1) * PACK, part * width : (part + 1) * width] = (
                window[:, :width].astype(BF16)
            )


def range_blocks(me_ref, echo_ref, table, outs, chunks, chunk_count, devices, pulse_len):
    lines = echo_ref.shape[0] // 2
    samples = echo_ref.shape[1]
    width = outs[0].shape[1] // 2
    lane_blocks = samples // LANES
    window_blocks = (pulse_len + width) // LANES
    index = 0
    for chunk in chunks:
        for step in range(devices):
            target = lax.rem(me_ref[0] + step, devices)
            first = target * (samples // devices // LANES) + chunk * (width // LANES)
            pieces = [
                echo_ref[
                    :,
                    pl.ds(
                        pl.multiple_of(lax.rem(first + j, lane_blocks) * LANES, LANES), LANES
                    ),
                ]
                for j in range(window_blocks)
            ]
            window = jnp.concatenate(pieces, axis=1)
            product = jnp.dot(window, table, preferred_element_type=F32)
            out = outs[index]
            out[:, :width] = (product[:lines, :width] - product[lines:, width:]).astype(BF16)
            out[:, width:] = (product[lines:, :width] + product[:lines, width:]).astype(BF16)
            index += 1


def first_range_kernel(devices, chunk_count, pulse_len, me_ref, rate_ref, echo_ref, table_ref, *rest):
    outs, base_ref = rest[:-1], rest[-1]
    width = table_ref.shape[1] // 2
    build_chirp(rate_ref, table_ref, base_ref, pulse_len, width)
    range_blocks(
        me_ref, echo_ref, table_ref[...], outs, [0], chunk_count, devices, pulse_len
    )


def rest_range_kernel(devices, chunk_count, pulse_len, me_ref, echo_ref, table_ref, *outs):
    range_blocks(
        me_ref,
        echo_ref,
        table_ref[...],
        outs,
        range(1, chunk_count),
        chunk_count,
        devices,
        pulse_len,
    )


def tables_kernel(
    shift_ref, taps_ref, rate_ref, _, dft_ref, inv_ref, coef_ref, filt_ref
):
    size = dft_ref.shape[0]
    half = size // 2
    amplitude = 1.0 / math.sqrt(size)
    rows = lax.broadcasted_iota(jnp.int32, (PACK, LANES), 0)
    lanes = lax.broadcasted_iota(jnp.int32, (PACK, LANES), 1)
    period = size // LANES
    turn_of = []
    for block in range(period):
        sin_b, cos_b = sincos_turns(((rows * block) % period).astype(F32) / period)
        turn_of.append((sin_b * amplitude, cos_b * amplitude))

    def base_of(ids):
        return sincos_turns(((ids * lanes) & (size - 1)).astype(F32) / size)

    def alternate(ids):
        return jnp.where((ids & 1) == 0, amplitude, -amplitude)

    def dft_rows(tile, _):
        ids = rows + tile * PACK
        sin_0, cos_0 = base_of(ids)
        row = pl.multiple_of(tile * PACK, PACK)
        for block in range(period):
            sin_b, cos_b = turn_of[block]
            cols = slice(block * LANES, (block + 1) * LANES)
            dft_ref[pl.ds(row, PACK), cols] = (cos_0 * cos_b - sin_0 * sin_b).astype(BF16)
            sin_v = sin_0 * cos_b + cos_0 * sin_b
            sin_v = jnp.where(ids == 0, alternate(lanes), sin_v)
            dft_ref[pl.ds(half + row, PACK), cols] = sin_v.astype(BF16)
        return 0

    lax.fori_loop(0, half // PACK, dft_rows, 0)

    def inv_rows(tile, _):
        ids = rows + (tile * PACK - RIM)
        sin_0, cos_0 = base_of(ids)
        row = pl.multiple_of(tile * PACK, PACK)
        for block in range(half // LANES):
            sin_b, cos_b = turn_of[block]
            cos_v = cos_0 * cos_b - sin_0 * sin_b
            sin_v = sin_0 * cos_b + cos_0 * sin_b
            if block == 0:
                sin_v = jnp.where(lanes == 0, alternate(ids), sin_v)
            first = block * LANES
            inv_ref[pl.ds(row, PACK), first : first + LANES] = cos_v.astype(BF16)
            first += half
            inv_ref[pl.ds(row, PACK), first : first + LANES] = sin_v.astype(BF16)
        return 0

    lax.fori_loop(0, inv_ref.shape[0] // PACK, inv_rows, 0)

    shift = shift_ref[0]

    def coef_rows(tile, _):
        ids = rows + tile * PACK
        row = pl.multiple_of(tile * PACK, PACK)
        sin_v, cos_v = sincos_turns(((ids * shift) & (size - 1)).astype(F32) / size)
        sin_1, cos_1 = sincos_turns(ids.astype(F32) / size)
        sum_c = taps_ref[0] * cos_v
        sum_s = taps_ref[0] * sin_v
        for tap in range(1, TAPS):
            sin_v, cos_v = sin_v * cos_1 + cos_v * sin_1, cos_v * cos_1 - sin_v * sin_1
            sum_c = sum_c + taps_ref[tap] * cos_v
            sum_s = sum_s + taps_ref[tap] * sin_v
        first = ids == 0
        coef_ref[0, pl.ds(row, PACK), :] = jnp.where(first, sum_c, 2.0 * sum_c)
        coef_ref[1, pl.ds(row, PACK), :] = 2.0 * sum_s
        coef_ref[2, pl.ds(row, PACK), :] = jnp.where(first, taps_ref[TAPS], 2.0 * sum_c)
        return 0

    lax.fori_loop(0, half // PACK, coef_rows, 0)

    width = rate_ref.shape[1]
    rate = rate_ref[...]

    def filter_rows(tile, _):
        ids = lax.broadcasted_iota(jnp.int32, (RIM, width), 0) + tile * RIM
        row = pl.multiple_of(tile * RIM, RIM)
        centered = jnp.minimum(ids, half).astype(F32) / size
        sin_v, cos_v = sincos_turns(0.5 * size * rate * centered * centered)
        filt_ref[0, pl.ds(row, RIM), :] = cos_v
        filt_ref[1, pl.ds(row, RIM), :] = sin_v
        return 0

    lax.fori_loop(0, half // RIM + 1, filter_rows, 0)


def forward_kernel(devices, chunk, me_ref, dft_ref, coef_ref, filt_ref, *rest):
    blocks, out_ref, joined = rest[:devices], rest[devices], rest[devices + 1]
    size = dft_ref.shape[0]
    half = size // 2
    lines, width = blocks[0].shape[0], blocks[0].shape[1] // 2
    for step in range(devices):
        source = lax.rem(me_ref[0] + (devices - step), devices)
        joined[pl.ds(pl.multiple_of(source * lines, lines), lines), :] = blocks[step][...]
    columns = joined[...]
    tile = min(half, 128)
    copies = width // LANES
    for first in range(0, half, tile):
        rows = slice(first, first + tile)
        even = jnp.dot(dft_ref[rows, :], columns, preferred_element_type=F32)
        odd = jnp.dot(
            dft_ref[half + first : half + first + tile, :], columns, preferred_element_type=F32
        )
        coefs = [coef_ref[i, rows, :] for i in range(3)]
        if copies > 1:
            coefs = [jnp.concatenate([value] * copies, axis=1) for value in coefs]
        even_re, even_im = even[:, :width], even[:, width:]
        odd_re, odd_im = odd[:, :width], odd[:, width:]
        u_re = coefs[0] * even_re + coefs[1] * odd_re
        u_im = coefs[0] * even_im + coefs[1] * odd_im
        v_re = coefs[2] * odd_re - coefs[1] * even_re
        v_im = coefs[2] * odd_im - coefs[1] * even_im
        cols = slice(chunk * width, (chunk + 1) * width)
        filt_re, filt_im = filt_ref[0, rows, cols], filt_ref[1, rows, cols]
        out_ref[rows, :width] = (filt_re * u_re - filt_im * u_im).astype(BF16)
        out_ref[rows, width:] = (filt_re * u_im + filt_im * u_re).astype(BF16)
        if first == 0:
            top = lax.broadcasted_iota(jnp.int32, (tile, width), 0) == 0
            filt_re = jnp.where(top, filt_ref[0, half : half + 1, cols], filt_re)
            filt_im = jnp.where(top, filt_ref[1, half : half + 1, cols], filt_im)
        rows = slice(half + first, half + first + tile)
        out_ref[rows, :width] = (filt_re * v_re - filt_im * v_im).astype(BF16)
        out_ref[rows, width:] = (filt_re * v_im + filt_im * v_re).astype(BF16)


def inverse_kernel(devices, line_count, first_row, rows, chunk_count, me_ref, inv_ref, *rest):
    spectra, outs = rest[:chunk_count], rest[chunk_count:]
    pieces = []
    for step in range(devices):
        target = lax.rem(me_ref[0] + step, devices)
        start = pl.multiple_of(target * line_count + first_row, PACK)
        pieces.append(inv_ref[pl.ds(start, rows), :])
    left = jnp.concatenate(pieces, axis=0)
    total = outs[0].shape[1] // 2
    width = total // chunk_count
    for chunk in range(chunk_count):
        product = jnp.dot(left, spectra[chunk][...], preferred_element_type=F32).astype(BF16)
        for step in range(devices):
            part = product[step * rows : (step + 1) * rows]
            first = chunk * width
            outs[step][:, first : first + width] = part[:, :width]
            first += total
            outs[step][:, first : first + width] = part[:, width:]


def join_kernel(devices, has_first, has_last, me_ref, *rest):
    blocks, out_ref = rest[:devices], rest[devices]
    rows, width = blocks[0].shape[0], blocks[0].shape[1] // 2
    samples = out_ref.shape[1] // 2
    for step in range(devices):
        source = lax.rem(me_ref[0] + (devices - step), devices)
        for part in range(2):
            start = pl.multiple_of(part * samples + source * width, LANES)
            out_ref[:, pl.ds(start, width)] = blocks[step][:, part * width : (part + 1) * width]

    def clear(first, low, high):
        edge = out_ref[first : first + PACK, :].astype(F32)
        ids = lax.broadcasted_iota(jnp.int32, edge.shape, 0)
        edge = jnp.where((ids >= low) & (ids < high), 0.0, edge)
        out_ref[first : first + PACK, :] = edge.astype(BF16)

    if has_first:

        @pl.when(me_ref[0] == 0)
        def _():
            clear(0, 0, RIM)

    if has_last:

        @pl.when(me_ref[0] == devices - 1)
        def _():
            clear(rows - PACK, PACK - RIM, PACK)


def coherence_kernel(has_before, *refs):
    dates = SPAN + 1
    now = refs[:dates]
    position = dates
    before = None
    if has_before:
        before = refs[position : position + dates]
        position += dates + 2
    image_ref, result_ref, sums_ref = refs[position : position + 3]
    lines = image_ref.shape[1]
    samples = image_ref.shape[2]
    window = lines + 2 * RIM
    half_az, half_rg = WIN_AZ // 2, WIN_RG // 2
    block = min(samples, 256)
    out_id = lax.broadcasted_iota(jnp.int32, (lines, window), 0)
    in_id = lax.broadcasted_iota(jnp.int32, (lines, window), 1) - RIM
    band = jnp.where(jnp.abs(in_id - out_id) <= half_az, 1.0, 0.0).astype(BF16)
    band = jnp.concatenate([band, band], axis=1)
    terms = 1 + 3 * SPAN

    def load(date, start):
        piece = now[date][:, pl.ds(start, block)]
        if has_before:
            held = before[date]
            piece = jnp.concatenate(
                [held[held.shape[0] - 2 * RIM :, pl.ds(start, block)], piece], axis=0
            )
        return piece

    def add_lines(value, term, start):
        high = value.astype(BF16)
        low = (value - high.astype(F32)).astype(BF16)
        both = jnp.concatenate([high, low], axis=0)
        sums_ref[term, :, pl.ds(start + LANES, block)] = jnp.dot(
            band, both, preferred_element_type=F32
        )

    def first_pass(index, _):
        start = pl.multiple_of(index * block, block)
        re = load(0, start)
        im = load(0, samples + start)
        re, im = re.astype(F32), im.astype(F32)
        image_ref[0, :, pl.ds(start, block)] = re[RIM : RIM + lines].astype(BF16)
        image_ref[1, :, pl.ds(start, block)] = im[RIM : RIM + lines].astype(BF16)
        add_lines(re * re + im * im, 0, start)
        for date in range(1, dates):
            other_re = load(date, start).astype(F32)
            other_im = load(date, samples + start).astype(F32)
            term = 3 * date - 2
            add_lines(re * other_re + im * other_im, term, start)
            add_lines(im * other_re - re * other_im, term + 1, start)
            add_lines(other_re * other_re + other_im * other_im, term + 2, start)
        return 0

    edge = jnp.zeros((lines, LANES), F32)
    for term in range(terms):
        sums_ref[term, :, :LANES] = edge
        sums_ref[term, :, samples + LANES :] = edge
    lax.fori_loop(0, samples // block, first_pass, 0)

    def second_pass(index, _):
        start = pl.multiple_of(index * block, block)
        size = block + 2 * LANES

        def box(term):
            wide = sums_ref[term, :, pl.ds(start, size)]
            pair = wide + pltpu.roll(wide, 1, 1)
            four = pair + pltpu.roll(pair, 2, 1)
            five = four + pltpu.roll(wide, 4, 1)
            return pltpu.roll(five, size - half_rg, 1)[:, LANES : LANES + block]

        own = box(0)
        for date in range(1, dates):
            term = 3 * date - 2
            scale = lax.rsqrt(own * box(term + 2) + epsilon)
            result_ref[date - 1, 0, :, pl.ds(start, block)] = (box(term) * scale).astype(BF16)
            result_ref[date - 1, 1, :, pl.ds(start, block)] = (box(term + 1) * scale).astype(BF16)
        return 0

    lax.fori_loop(0, samples // block, second_pass, 0)


def kernel_taps(fraction):
    half_taps = TAPS // 2
    position = jnp.arange(TAPS, dtype=jnp.int32).astype(F32) - (half_taps - 1) - fraction
    return jnp.sinc(position) * (0.5 + 0.5 * jnp.cos(math.pi * position / half_taps))


def scatter(blocks, axis):
    count = lax.axis_size(axis)
    moved = [blocks[0]]
    for step in range(1, count):
        route = [(i, (i + step) % count) for i in range(count)]
        moved.append(lax.ppermute(blocks[step], axis, route))
    return moved


def from_next(block, axis):
    count = lax.axis_size(axis)
    return lax.ppermute(block, axis, [((i + 1) % count, i) for i in range(count)])


def body(raw_echo, range_rate, azimuth_rate, line_offset, frac_shift):
    devices = lax.axis_size("swath")
    lines, samples = raw_echo.shape[2], raw_echo.shape[3]
    size = lines * devices
    half = size // 2
    owned = azimuth_rate.shape[0]
    pulse_len = samples // 2
    me = lax.axis_index("swath").astype(jnp.int32).reshape(1)
    echo = raw_echo.reshape(2 * lines, samples)

    chunk_count = max(1, min(4, owned // LANES))
    width = owned // chunk_count
    depth = pulse_len + width
    block_type = jax.ShapeDtypeStruct((lines, 2 * width), BF16)
    flops = 2 * 2 * lines * depth * 2 * width * devices
    table, *first_blocks = pl.pallas_call(
        functools.partial(first_range_kernel, devices, chunk_count, pulse_len),
        out_shape=[jax.ShapeDtypeStruct((depth, 2 * width), BF16)] + [block_type] * devices,
        in_specs=[smem(), smem(), vmem()],
        out_specs=[vmem()] * (devices + 1),
        scratch_shapes=[pltpu.VMEM((2, PACK, pulse_len + 2 * width + LANES), F32)],
        compiler_params=params(40),
        cost_estimate=cost(2 * flops, 4 * lines * samples),
        name="range_first",
    )(me, range_rate.reshape(1), echo)
    columns = [scatter(first_blocks, "swath")]
    order = first_blocks[0]
    if chunk_count > 1:
        rest = pl.pallas_call(
            functools.partial(rest_range_kernel, devices, chunk_count, pulse_len),
            out_shape=[block_type] * (devices * (chunk_count - 1)),
            in_specs=[smem(), vmem(), vmem()],
            out_specs=[vmem()] * (devices * (chunk_count - 1)),
            compiler_params=params(40),
            cost_estimate=cost((chunk_count - 1) * flops, 4 * lines * samples),
            name="range_rest",
        )(me, echo, table)
        for chunk in range(chunk_count - 1):
            columns.append(scatter(rest[chunk * devices : (chunk + 1) * devices], "swath"))
        order = rest[-1]

    taps = kernel_taps(frac_shift[0])
    signs = 1.0 - 2.0 * ((line_offset[0] + jnp.arange(TAPS, dtype=jnp.int32)) % 2).astype(F32)
    taps = jnp.concatenate([taps, jnp.sum(taps * signs).reshape(1)])
    dft, inv, coef, filt = pl.pallas_call(
        tables_kernel,
        out_shape=[
            jax.ShapeDtypeStruct((size, size), BF16),
            jax.ShapeDtypeStruct((size + 2 * RIM, size), BF16),
            jax.ShapeDtypeStruct((3, half, LANES), F32),
            jax.ShapeDtypeStruct((2, half + RIM, owned), F32),
        ],
        in_specs=[smem(), smem(), vmem(), pl.BlockSpec(memory_space=pl.ANY)],
        out_specs=[vmem()] * 4,
        compiler_params=params(40),
        cost_estimate=cost(size * size * 64, 8 * size * size),
        name="azimuth_tables",
    )(line_offset, taps, azimuth_rate.reshape(1, owned), order)

    spectra = []
    for chunk in range(chunk_count):
        spectra.append(
            pl.pallas_call(
                functools.partial(forward_kernel, devices, chunk),
                out_shape=jax.ShapeDtypeStruct((size, 2 * width), BF16),
                in_specs=[smem()] + [vmem()] * (3 + devices),
                out_specs=vmem(),
                scratch_shapes=[pltpu.VMEM((size, 2 * width), BF16)],
                compiler_params=params(40),
                cost_estimate=cost(4 * size * size * width, 2 * size * size + 8 * size * width),
                name="azimuth_forward",
            )(me, dft, coef, filt, *columns[chunk])
        )

    step_lines = min(lines, LINE_STEP)
    steps = lines // step_lines
    image = result = held = None
    for step in range(steps):
        rows = step_lines + (2 * RIM if step == 0 else 0)
        first_row = step * step_lines + (0 if step == 0 else 2 * RIM)
        outs = pl.pallas_call(
            functools.partial(inverse_kernel, devices, lines, first_row, rows, chunk_count),
            out_shape=[jax.ShapeDtypeStruct((rows, 2 * owned), BF16)] * devices,
            in_specs=[smem()] + [vmem()] * (1 + chunk_count),
            out_specs=[vmem()] * devices,
            compiler_params=params(40),
            cost_estimate=cost(
                4 * devices * rows * size * owned, 2 * size * size + 4 * size * owned
            ),
            name="azimuth_inverse",
        )(me, inv, *spectra)
        strips = scatter(outs, "swath")
        own = pl.pallas_call(
            functools.partial(join_kernel, devices, step == 0, step == steps - 1),
            out_shape=jax.ShapeDtypeStruct((rows, 2 * samples), BF16),
            in_specs=[smem()] + [vmem()] * devices,
            out_specs=vmem(),
            compiler_params=params(40),
            cost_estimate=cost(rows * samples, 8 * rows * samples),
            name="join_strips",
        )(me, *strips)
        now = [own]
        for _ in range(SPAN):
            now.append(from_next(now[-1], "date"))
        operands = list(now)
        in_specs = [vmem()] * len(now)
        aliases = {}
        if held is not None:
            operands += held + [image, result]
            in_specs += [vmem()] * len(held) + [pl.BlockSpec(memory_space=pl.ANY)] * 2
            aliases = {len(operands) - 2: 0, len(operands) - 1: 1}
        image, result = pl.pallas_call(
            functools.partial(coherence_kernel, held is not None),
            grid=(1,),
            out_shape=[
                jax.ShapeDtypeStruct((2, lines, samples), BF16),
                jax.ShapeDtypeStruct((SPAN, 2, lines, samples), BF16),
            ],
            in_specs=in_specs,
            out_specs=[
                pl.BlockSpec((2, step_lines, samples), lambda i, s=step: (0, s, 0)),
                pl.BlockSpec((SPAN, 2, step_lines, samples), lambda i, s=step: (0, 0, s, 0)),
            ],
            scratch_shapes=[
                pltpu.VMEM((1 + 3 * SPAN, step_lines, samples + 2 * LANES), F32)
            ],
            input_output_aliases=aliases,
            compiler_params=params(48),
            cost_estimate=cost(500 * step_lines * samples, 30 * step_lines * samples),
            name="coherence",
        )(*operands)
        held = now
    return (image[None], result[None])


def solution(mesh):
    placed = (P("date", None, "swath", None), P(), P("swath"), P("date"), P("date"))
    return jax.shard_map(
        body,
        mesh=mesh,
        in_specs=placed,
        out_specs=(P("date", None, "swath", None), P("date", None, None, "swath", None)),
        check_vma=False,
    )
```

time: 571 us -> 198 us (0.35); the launches traced: 562 us -> 196 us
  matrix products: 176 us -> 0 us
  other arithmetic: 168 us -> 1.35 us
  Pallas kernels: 0 us -> 89.7 us
  local copies, waits for them, and re-layouts: 67.4 us -> 1.59 us
  starting transfers between devices: 12.7 us -> 66.5 us
  blocking collectives: 50.2 us -> 0 us
  waiting for transfers between devices: 72.6 us -> 34.2 us
  loops' own time: 10.8 us -> 0 us
    dot_general x32 -> x0, matrix products: 176 us -> none  [local_dot(): return jnp.dot(left, right, preferred_element_type=jnp.float32)]
    add x15 -> x0, other arithmetic: 106 us -> none  [the longest x2 76.7 us: box_sum(): running = running + across[:, offset_id:offset_id + out_rows]]
    pallas_call x0 -> x19, Pallas kernels: none -> 89.7 us  [the longest x4 68.1 us: body(): pl.pallas_call(functools.partial(coherence_kernel, held is not None), gri...]
    ppermute x4 -> x32, starting transfers between devices: 6.22 us -> 66.5 us  [the longest x24 54.8 us: scatter(): moved.append(lax.ppermute(blocks[step], axis, route))]
    all_to_all x1 -> x0, blocking collectives: 50.2 us -> none  [body(): lax.all_to_all(aligned, 'swath', split_axis=1, concat_axis=2, tiled=True)]
    all_to_all x1 -> x0, waiting for transfers between devices: 46.1 us -> none  [body(): lax.all_to_all(compressed, 'swath', split_axis=2, concat_axis=1, tiled=True)]
    another operation x16 -> x0, other arithmetic: 21.6 us -> none  [the longest x2 11.2 us: coherence_of(): jnp.stack([box_terms[0] / denominator, box_terms[1] / denominator])]
    convert_element_type x4 -> x0, other arithmetic: 19.8 us -> none  [the longest x1 9.17 us: interpolate(): return running.astype(jnp.bfloat16)]
  transfers between devices with their start and end apart: 5 -> 32, of which waited for: 3 -> 11; matrix products, arithmetic and copies ran while one was open for 9% -> 1% of each run, Pallas kernels for 0% -> 33%
where the time goes in v1:
time: 198 us; the launch traced here: 196 us
  Pallas kernels  89.7 us (45%)
  starting transfers between devices  66.5 us (34%)
  waiting for transfers between devices  34.2 us (17%)
  between operations  2.8 us (1%)
    pallas_call x4, Pallas kernels, body(): pl.pallas_call(functools.partial(coherence_kernel, held is not None), gri...  68.1 us
    ppermute x24, starting transfers between devices, scatter(): moved.append(lax.ppermute(blocks[step], axis, route))  54.8 us
    ppermute x24, waiting for transfers between devices, scatter(): moved.append(lax.ppermute(blocks[step], axis, route))  24.4 us
    ppermute x8, starting transfers between devices, from_next(): lax.ppermute(block, axis, [((i + 1) % count, i) for i in range(count)])  11.8 us
    ppermute x8, waiting for transfers between devices, from_next(): lax.ppermute(block, axis, [((i + 1) % count, i) for i in range(count)])  9.85 us
    pallas_call x1, Pallas kernels, body(): pl.pallas_call(tables_kernel, out_shape=[jax.ShapeDtypeStruct((size, size...  8.61 us
    pallas_call x1, Pallas kernels, body(): pl.pallas_call(functools.partial(rest_range_kernel, devices, chunk_count,...  4.45 us
  transfers between devices with their start and end apart: 32, of which 11 were waited for; matrix products, arithmetic and copies ran while one was open for 1% of the time, Pallas kernels for 33%

profile of v1, /device:TPU:0, one launch (start us, length us, event | category | flops | bytes accessed | tf_op | source)
XLA Modules:
  0.0 196.3 jit_solution(15808753891002102584)
XLA Ops:
  1.3 1.6 copy-done
  2.9 1.8 range_first.1
  4.7 4.4 %range_rest.1 = (bf16[256,256]{1,0:T(8,128)(2,1)S(1)}, bf16[256,256]{1,0:T(8,128)(2,1)S(1)}, bf16[256,256]{1,0:T(8,128)(2,1)S(1)}, bf16[256,256]{1,0:T(8,128)(2,...) custom-call(s32[1]{0:T(128)} %bitcast.me_ref, ...), custom_call_target="tpu_custom_call" | custom-call | flops 3623878656 | bytes 2097152 | tf_op jit(solution)/shard_map/range_rest/pallas_call | solution.py:443
  9.1 3.1 %collective-permute-start.3 = (bf16[256,256]{1,0:T(8,128)(2,1)S(1)}, bf16[256,256]{1,0:T(8,128)(2,1)S(1)}, u32[]{:S(2)}, u32[]{:S(2)}) collective-permute-start(bf16[256,256]{1,0:T(8,128)(2,1)S(1)} %get-tuple-element.58), channel_id=1, source_target_pairs={{0,1},{1,2},{2,3},{3,0},{4,5},{5,6},{6,7},{7,4},{8,9},{9,10},{10,1... | collective-permute-start | bytes 393224 | tf_op jit(solution)/shard_map/ppermute | solution.py:406
  12.2 1.6 collective-permute-start.6
  13.8 1.1 collective-permute-start.7
  14.8 2.9 %collective-permute-start.8 = (bf16[256,256]{1,0:T(8,128)(2,1)S(1)}, bf16[256,256]{1,0:T(8,128)(2,1)S(1)}, u32[]{:S(2)}, u32[]{:S(2)}) collective-permute-start(bf16[256,256]{1,0:T(8,128)(2,1)S(1)} %get-tuple-element.64), channel_id=1, source_target_pairs={{0,3},{1,0},{2,1},{3,2},{4,7},{5,4},{6,5},{7,6},{8,11},{9,8},{10,9... | collective-permute-start | bytes 393224 | tf_op jit(solution)/shard_map/ppermute | solution.py:406
  19.0 1.1 collective-permute-start.10
  20.1 1.4 collective-permute-done.6.rest_1_
  21.5 2.6 %collective-permute-start.11 = (bf16[256,256]{1,0:T(8,128)(2,1)S(1)}, bf16[256,256]{1,0:T(8,128)(2,1)S(1)}, u32[]{:S(2)}, u32[]{:S(2)}) collective-permute-start(bf16[256,256]{1,0:T(8,128)(2,1)S(1)} %get-tuple-element.48._), channel_id=1, source_target_pairs={{0,3},{1,0},{2,1},{3,2},{4,7},{5,4},{6,5},{7,6},{8,11},{9,8},{10,9... | collective-permute-start | bytes 393224 | tf_op jit(solution)/shard_map/ppermute | solution.py:406
  24.8 2.4 %collective-permute-done.7.rest_2_ = bf16[256,256]{1,0:T(8,128)(2,1)S(1)} collective-permute-done((bf16[256,256]{1,0:T(8,128)(2,1)S(1)}, bf16[256,256]{1,0:T(8,128)(2,1)S(1)}, u32[]{:S(2)}, u32[]{:S(2)}) %collective-permute-start.7) | collective-permute-done | bytes 131104 | tf_op jit(solution)/shard_map/ppermute | solution.py:406
  27.1 1.5 collective-permute-start.4
  28.7 12.9 %collective-permute-start.5 = (bf16[256,256]{1,0:T(8,128)(2,1)S(1)}, bf16[256,256]{1,0:T(8,128)(2,1)S(1)}, u32[]{:S(2)}, u32[]{:S(2)}) collective-permute-start(bf16[256,256]{1,0:T(8,128)(2,1)S(1)} %get-tuple-element.60), channel_id=1, source_target_pairs={{0,3},{1,0},{2,1},{3,2},{4,7},{5,4},{6,5},{7,6},{8,11},{9,8},{10,9... | collective-permute-start | bytes 393224 | tf_op jit(solution)/shard_map/ppermute | solution.py:406
  42.3 8.6 %azimuth_tables.1 = (bf16[1024,1024]{1,0:T(8,128)(2,1)S(1)}, bf16[1040,1024]{1,0:T(8,128)(2,1)S(1)}, f32[3,512,128]{2,1,0:T(8,128)S(1)}, f32[2,520,512]{2,1,0:T(8,128)S(1)}) custom-call(s32[1]{0:T(128)} %copy.20.shift_ref, f32[9]{0:T(128)S(1)} %pad_maximum_fusion.taps_ref, f32[1,512]{1,0:T(1,128)S(1)} %bitcast.14, bf16[256,256]{1,0:T(8,128)(2,1)S(1)} %get-tuple-element.48._), custom_call_target="tpu_custom_call" | custom-call | flops 67108864 | bytes 8388608 | tf_op jit(solution)/shard_map/azimuth_tables/pallas_call | solution.py:459
  51.5 1.5 collective-permute-start.1
  53.1 2.8 %collective-permute-start.2 = (bf16[256,256]{1,0:T(8,128)(2,1)S(1)}, bf16[256,256]{1,0:T(8,128)(2,1)S(1)}, u32[]{:S(2)}, u32[]{:S(2)}) collective-permute-start(bf16[256,256]{1,0:T(8,128)(2,1)S(1)} %get-tuple-element.56), channel_id=1, source_target_pairs={{0,3},{1,0},{2,1},{3,2},{4,7},{5,4},{6,5},{7,6},{8,11},{9,8},{10,9... | collective-permute-start | bytes 393224 | tf_op jit(solution)/shard_map/ppermute | solution.py:406
  55.9 0.9 azimuth_forward.7.rest_3_
  56.8 0.9 azimuth_forward.6.rest_2_
  57.8 0.9 azimuth_forward.5.rest_1_
  58.7 5.7 %collective-permute-done.1.rest_2_ = bf16[256,256]{1,0:T(8,128)(2,1)S(1)} collective-permute-done((bf16[256,256]{1,0:T(8,128)(2,1)S(1)}, bf16[256,256]{1,0:T(8,128)(2,1)S(1)}, u32[]{:S(2)}, u32[]{:S(2)}) %collective-permute-start.1) | collective-permute-done | bytes 131104 | tf_op jit(solution)/shard_map/ppermute | solution.py:406
  64.4 0.9 azimuth_forward.4.rest_0_
  65.3 0.9 azimuth_inverse.7
  66.2 6.2 %collective-permute-start.27 = (bf16[80,1024]{1,0:T(8,128)(2,1)S(1)}, bf16[80,1024]{1,0:T(8,128)(2,1)S(1)}, u32[]{:S(2)}, u32[]{:S(2)}) collective-permute-start(bf16[80,1024]{1,0:T(8,128)(2,1)S(1)} %get-tuple-element.81), channel_id=1, source_target_pairs={{0,1},{1,2},{2,3},{3,0},{4,5},{5,6},{6,7},{7,4},{8,9},{9,10},{10,1... | collective-permute-start | bytes 491528 | tf_op jit(solution)/shard_map/ppermute | solution.py:406
  72.4 2.4 %collective-permute-start.29 = (bf16[80,1024]{1,0:T(8,128)(2,1)S(1)}, bf16[80,1024]{1,0:T(8,128)(2,1)S(1)}, u32[]{:S(2)}, u32[]{:S(2)}) collective-permute-start(bf16[80,1024]{1,0:T(8,128)(2,1)S(1)} %get-tuple-element.83), channel_id=1, source_target_pairs={{0,3},{1,0},{2,1},{3,2},{4,7},{5,4},{6,5},{7,6},{8,11},{9,8},{10,9... | collective-permute-start | bytes 491528 | tf_op jit(solution)/shard_map/ppermute | solution.py:406
  75.6 2.5 %collective-permute-start.23 = (bf16[64,1024]{1,0:T(8,128)(2,1)S(1)}, bf16[64,1024]{1,0:T(8,128)(2,1)S(1)}, u32[]{:S(2)}, u32[]{:S(2)}) collective-permute-start(bf16[64,1024]{1,0:T(8,128)(2,1)S(1)} %get-tuple-element.78), channel_id=1, source_target_pairs={{0,2},{1,3},{2,0},{3,1},{4,6},{5,7},{6,4},{7,5},{8,10},{9,11},{10,... | collective-permute-start | bytes 393224 | tf_op jit(solution)/shard_map/ppermute | solution.py:406
  78.2 1.3 collective-permute-start.24
  80.0 0.7 azimuth_inverse.5
  80.8 5.2 %collective-permute-start.17 = (bf16[64,1024]{1,0:T(8,128)(2,1)S(1)}, bf16[64,1024]{1,0:T(8,128)(2,1)S(1)}, u32[]{:S(2)}, u32[]{:S(2)}) collective-permute-start(bf16[64,1024]{1,0:T(8,128)(2,1)S(1)} %get-tuple-element.73), channel_id=1, source_target_pairs={{0,1},{1,2},{2,3},{3,0},{4,5},{5,6},{6,7},{7,4},{8,9},{9,10},{10,1... | collective-permute-start | bytes 393224 | tf_op jit(solution)/shard_map/ppermute | solution.py:406
  85.9 0.8 collective-permute-start.18
  86.7 2.0 %collective-permute-done.23.rest_2_ = bf16[64,1024]{1,0:T(8,128)(2,1)S(1)} collective-permute-done((bf16[64,1024]{1,0:T(8,128)(2,1)S(1)}, bf16[64,1024]{1,0:T(8,128)(2,1)S(1)}, u32[]{:S(2)}, u32[]{:S(2)}) %collective-permute-start.23) | collective-permute-done | bytes 131104 | tf_op jit(solution)/shard_map/ppermute | solution.py:406
  89.8 4.1 %collective-permute-start.12 = (bf16[64,1024]{1,0:T(8,128)(2,1)S(1)}, bf16[64,1024]{1,0:T(8,128)(2,1)S(1)}, u32[]{:S(2)}, u32[]{:S(2)}) collective-permute-start(bf16[64,1024]{1,0:T(8,128)(2,1)S(1)} %get-tuple-element.69), channel_id=1, source_target_pairs={{0,1},{1,2},{2,3},{3,0},{4,5},{5,6},{6,7},{7,4},{8,9},{9,10},{10,1... | collective-permute-start | bytes 393224 | tf_op jit(solution)/shard_map/ppermute | solution.py:406
  93.9 7.9 %collective-permute-done.18.rest_2_ = bf16[64,1024]{1,0:T(8,128)(2,1)S(1)} collective-permute-done((bf16[64,1024]{1,0:T(8,128)(2,1)S(1)}, bf16[64,1024]{1,0:T(8,128)(2,1)S(1)}, u32[]{:S(2)}, u32[]{:S(2)}) %collective-permute-start.18) | collective-permute-done | bytes 131104 | tf_op jit(solution)/shard_map/ppermute | solution.py:406
  101.9 1.3 collective-permute-start.25
  103.2 1.4 collective-permute-start.20
  104.6 2.9 %collective-permute-done.13.rest_2_ = bf16[64,1024]{1,0:T(8,128)(2,1)S(1)} collective-permute-done((bf16[64,1024]{1,0:T(8,128)(2,1)S(1)}, bf16[64,1024]{1,0:T(8,128)(2,1)S(1)}, u32[]{:S(2)}, u32[]{:S(2)}) %collective-permute-start.13) | collective-permute-done | bytes 131104 | tf_op jit(solution)/shard_map/ppermute | solution.py:406
  107.5 1.7 collective-permute-done.14.rest_3_
  109.2 1.5 collective-permute-start.15
  110.7 1.1 collective-permute-start.31
  111.9 0.8 collective-permute-start.26
  112.7 2.8 %collective-permute-done.20.refs_1_.refs_4_ = bf16[64,4096]{1,0:T(8,128)(2,1)S(1)} collective-permute-done((bf16[64,4096]{1,0:T(8,128)(2,1)S(1)}, bf16[64,4096]{1,0:T(8,128)(2,1)S(1)}, u32[]{:S(2)}, u32[]{:S(2)}) %collective-permute-start.20) | collective-permute-done | bytes 524320 | tf_op jit(solution)/shard_map/ppermute | solution.py:412
  115.5 2.8 %collective-permute-start.21 = (bf16[64,4096]{1,0:T(8,128)(2,1)S(1)}, bf16[64,4096]{1,0:T(8,128)(2,1)S(1)}, u32[]{:S(2)}, u32[]{:S(2)}) collective-permute-start(bf16[64,4096]{1,0:T(8,128)(2,1)S(1)} %collective-permute-done.20.refs_1_.refs_4_), channel_id=1, source_target_pairs={{4,0},{8,4},{12,8},{16,12},{20,16},{24,20},{28,24},{0,28},{5,1},{9... | collective-permute-start | bytes 1572872 | tf_op jit(solution)/shard_map/ppermute | solution.py:412
  118.3 2.8 %collective-permute-done.15.refs_1_ = bf16[64,4096]{1,0:T(8,128)(2,1)S(1)} collective-permute-done((bf16[64,4096]{1,0:T(8,128)(2,1)S(1)}, bf16[64,4096]{1,0:T(8,128)(2,1)S(1)}, u32[]{:S(2)}, u32[]{:S(2)}) %collective-permute-start.15) | collective-permute-done | bytes 524320 | tf_op jit(solution)/shard_map/ppermute | solution.py:412
  121.1 2.8 %collective-permute-start.16 = (bf16[64,4096]{1,0:T(8,128)(2,1)S(1)}, bf16[64,4096]{1,0:T(8,128)(2,1)S(1)}, u32[]{:S(2)}, u32[]{:S(2)}) collective-permute-start(bf16[64,4096]{1,0:T(8,128)(2,1)S(1)} %collective-permute-done.15.refs_1_), channel_id=1, source_target_pairs={{4,0},{8,4},{12,8},{16,12},{20,16},{24,20},{28,24},{0,28},{5,1},{9... | collective-permute-start | bytes 1572872 | tf_op jit(solution)/shard_map/ppermute | solution.py:412
  123.9 4.2 %collective-permute-done.31.refs_2_.refs_5_ = bf16[80,4096]{1,0:T(8,128)(2,1)S(1)} collective-permute-done((bf16[80,4096]{1,0:T(8,128)(2,1)S(1)}, bf16[80,4096]{1,0:T(8,128)(2,1)S(1)}, u32[]{:S(2)}, u32[]{:S(2)}) %collective-permute-start.31) | collective-permute-done | bytes 655392 | tf_op jit(solution)/shard_map/ppermute | solution.py:412
  128.1 17.0 %coherence.4 = (bf16[2,256,2048]{2,1,0:T(8,128)(2,1)}, bf16[2,2,256,2048]{3,2,1,0:T(8,128)(2,1)}) custom-call(bf16[80,4096]{1,0:T(8,128)(2,1)S(1)} %join_strips.7.refs_0_.refs_3_, bf16[80,4096]{1,0:T(8,128)(2,1)S(1)} %collective-permute-done.30.refs_1_.refs_4_, bf16[80,4096]{1,0:T(8,128)(2,1)S(1)} %collective-permute-done.31.refs_2_.refs_5_), custom_call_target="tpu_custom_call" | custom-call | flops 65536000 | bytes 3932160 | tf_op jit(solution)/shard_map/coherence/pallas_call | solution.py:526
  145.1 17.0 %coherence.5 = (bf16[2,256,2048]{2,1,0:T(8,128)(2,1)}, bf16[2,2,256,2048]{3,2,1,0:T(8,128)(2,1)}) custom-call(bf16[64,4096]{1,0:T(8,128)(2,1)S(1)} %join_strips.6.refs_0_.refs_3_, bf16[64,4096]{1,0:T(8,128)(2,1)S(1)} %collective-permute-done.25.refs_1_.refs_4_, ...), custom_call_target="tpu_custom_call", output_to_operand_aliasing={{0}: (6, {}), {1}: (7, {})} | custom-call | flops 65536000 | bytes 3932160 | tf_op jit(solution)/shard_map/coherence/pallas_call | solution.py:526
  162.2 17.0 %coherence.6 = (bf16[2,256,2048]{2,1,0:T(8,128)(2,1)}, bf16[2,2,256,2048]{3,2,1,0:T(8,128)(2,1)}) custom-call(bf16[64,4096]{1,0:T(8,128)(2,1)S(1)} %join_strips.5.refs_0_.refs_3_, bf16[64,4096]{1,0:T(8,128)(2,1)S(1)} %collective-permute-done.20.refs_1_.refs_4_, ...), custom_call_target="tpu_custom_call", output_to_operand_aliasing={{0}: (6, {}), {1}: (7, {})} | custom-call | flops 65536000 | bytes 3932160 | tf_op jit(solution)/shard_map/coherence/pallas_call | solution.py:526
  179.2 17.0 %coherence.7 = (bf16[2,256,2048]{2,1,0:T(8,128)(2,1)}, bf16[2,2,256,2048]{3,2,1,0:T(8,128)(2,1)}) custom-call(bf16[64,4096]{1,0:T(8,128)(2,1)S(1)} %join_strips.4.refs_0_, bf16[64,4096]{1,0:T(8,128)(2,1)S(1)} %collective-permute-done.15.refs_1_, bf16[64,4096]{1,0:T(8,128)(2,1)S(1)} %collective-permute-done.16.refs_2_, ...), custom_call_target="tpu_custom_call", output_to_operand_aliasing={{0}: (6, {}), {1}: (7, {})} | custom-call | flops 65536000 | bytes 3932160 | tf_op jit(solution)/shard_map/coherence/pallas_call | solution.py:526
  (41 shorter events, 4.6 us)
Async XLA Ops:
  1.3 1.6 copy-start
  4.6 37.6 %copy-start.1 = (f32[512]{0:T(512)S(1)}, f32[512]{0:T(512)}, u32[]{:S(2)}) copy-start(f32[512]{0:T(512)} %param.7) | copy-start | bytes 6148
  9.1 9.9 %collective-permute-start.3 = (bf16[256,256]{1,0:T(8,128)(2,1)S(1)}, bf16[256,256]{1,0:T(8,128)(2,1)S(1)}, u32[]{:S(2)}, u32[]{:S(2)}) collective-permute-start(bf16[256,256]{1,0:T(8,128)(2,1)S(1)} %get-tuple-element.58), channel_id=1, source_target_pairs={{0,1},{1,2},{2,3},{3,0},{4,5},{5,6},{6,7},{7,4},{8,9},{9,10},{10,1... | collective-permute-start | bytes 393224 | tf_op jit(solution)/shard_map/ppermute | solution.py:406
  12.2 9.3 %collective-permute-start.6 = (bf16[256,256]{1,0:T(8,128)(2,1)S(1)}, bf16[256,256]{1,0:T(8,128)(2,1)S(1)}, u32[]{:S(2)}, u32[]{:S(2)}) collective-permute-start(bf16[256,256]{1,0:T(8,128)(2,1)S(1)} %get-tuple-element.62), channel_id=1, source_target_pairs={{0,1},{1,2},{2,3},{3,0},{4,5},{5,6},{6,7},{7,4},{8,9},{9,10},{10,1... | collective-permute-start | bytes 393224 | tf_op jit(solution)/shard_map/ppermute | solution.py:406
  13.8 13.4 %collective-permute-start.7 = (bf16[256,256]{1,0:T(8,128)(2,1)S(1)}, bf16[256,256]{1,0:T(8,128)(2,1)S(1)}, u32[]{:S(2)}, u32[]{:S(2)}) collective-permute-start(bf16[256,256]{1,0:T(8,128)(2,1)S(1)} %get-tuple-element.63), channel_id=1, source_target_pairs={{0,2},{1,3},{2,0},{3,1},{4,6},{5,7},{6,4},{7,5},{8,10},{9,11},{10,... | collective-permute-start | bytes 393224 | tf_op jit(solution)/shard_map/ppermute | solution.py:406
  14.8 13.9 %collective-permute-start.8 = (bf16[256,256]{1,0:T(8,128)(2,1)S(1)}, bf16[256,256]{1,0:T(8,128)(2,1)S(1)}, u32[]{:S(2)}, u32[]{:S(2)}) collective-permute-start(bf16[256,256]{1,0:T(8,128)(2,1)S(1)} %get-tuple-element.64), channel_id=1, source_target_pairs={{0,3},{1,0},{2,1},{3,2},{4,7},{5,4},{6,5},{7,6},{8,11},{9,8},{10,9... | collective-permute-start | bytes 393224 | tf_op jit(solution)/shard_map/ppermute | solution.py:406
  17.7 33.2 %collective-permute-start.9 = (bf16[256,256]{1,0:T(8,128)(2,1)S(1)}, bf16[256,256]{1,0:T(8,128)(2,1)S(1)}, u32[]{:S(2)}, u32[]{:S(2)}) collective-permute-start(bf16[256,256]{1,0:T(8,128)(2,1)S(1)} %get-tuple-element.66), channel_id=1, source_target_pairs={{0,1},{1,2},{2,3},{3,0},{4,5},{5,6},{6,7},{7,4},{8,9},{9,10},{10,1... | collective-permute-start | bytes 393224 | tf_op jit(solution)/shard_map/ppermute | solution.py:406
  19.0 32.5 %collective-permute-start.10 = (bf16[256,256]{1,0:T(8,128)(2,1)S(1)}, bf16[256,256]{1,0:T(8,128)(2,1)S(1)}, u32[]{:S(2)}, u32[]{:S(2)}) collective-permute-start(bf16[256,256]{1,0:T(8,128)(2,1)S(1)} %get-tuple-element.67), channel_id=1, source_target_pairs={{0,2},{1,3},{2,0},{3,1},{4,6},{5,7},{6,4},{7,5},{8,10},{9,11},{10,... | collective-permute-start | bytes 393224 | tf_op jit(solution)/shard_map/ppermute | solution.py:406
  21.5 31.6 %collective-permute-start.11 = (bf16[256,256]{1,0:T(8,128)(2,1)S(1)}, bf16[256,256]{1,0:T(8,128)(2,1)S(1)}, u32[]{:S(2)}, u32[]{:S(2)}) collective-permute-start(bf16[256,256]{1,0:T(8,128)(2,1)S(1)} %get-tuple-element.48._), channel_id=1, source_target_pairs={{0,3},{1,0},{2,1},{3,2},{4,7},{5,4},{6,5},{7,6},{8,11},{9,8},{10,9... | collective-permute-start | bytes 393224 | tf_op jit(solution)/shard_map/ppermute | solution.py:406
  27.1 30.6 %collective-permute-start.4 = (bf16[256,256]{1,0:T(8,128)(2,1)S(1)}, bf16[256,256]{1,0:T(8,128)(2,1)S(1)}, u32[]{:S(2)}, u32[]{:S(2)}) collective-permute-start(bf16[256,256]{1,0:T(8,128)(2,1)S(1)} %get-tuple-element.59), channel_id=1, source_target_pairs={{0,2},{1,3},{2,0},{3,1},{4,6},{5,7},{6,4},{7,5},{8,10},{9,11},{10,... | collective-permute-start | bytes 393224 | tf_op jit(solution)/shard_map/ppermute | solution.py:406
  28.7 29.1 %collective-permute-start.5 = (bf16[256,256]{1,0:T(8,128)(2,1)S(1)}, bf16[256,256]{1,0:T(8,128)(2,1)S(1)}, u32[]{:S(2)}, u32[]{:S(2)}) collective-permute-start(bf16[256,256]{1,0:T(8,128)(2,1)S(1)} %get-tuple-element.60), channel_id=1, source_target_pairs={{0,3},{1,0},{2,1},{3,2},{4,7},{5,4},{6,5},{7,6},{8,11},{9,8},{10,9... | collective-permute-start | bytes 393224 | tf_op jit(solution)/shard_map/ppermute | solution.py:406
  50.9 7.8 %collective-permute-start = (bf16[256,256]{1,0:T(8,128)(2,1)S(1)}, bf16[256,256]{1,0:T(8,128)(2,1)S(1)}, u32[]{:S(2)}, u32[]{:S(2)}) collective-permute-start(bf16[256,256]{1,0:T(8,128)(2,1)S(1)} %get-tuple-element.54), channel_id=1, source_target_pairs={{0,1},{1,2},{2,3},{3,0},{4,5},{5,6},{6,7},{7,4},{8,9},{9,10},{10,1... | collective-permute-start | bytes 393224 | tf_op jit(solution)/shard_map/ppermute | solution.py:406
  51.5 12.9 %collective-permute-start.1 = (bf16[256,256]{1,0:T(8,128)(2,1)S(1)}, bf16[256,256]{1,0:T(8,128)(2,1)S(1)}, u32[]{:S(2)}, u32[]{:S(2)}) collective-permute-start(bf16[256,256]{1,0:T(8,128)(2,1)S(1)} %get-tuple-element.55), channel_id=1, source_target_pairs={{0,2},{1,3},{2,0},{3,1},{4,6},{5,7},{6,4},{7,5},{8,10},{9,11},{10,... | collective-permute-start | bytes 393224 | tf_op jit(solution)/shard_map/ppermute | solution.py:406
  53.1 11.3 %collective-permute-start.2 = (bf16[256,256]{1,0:T(8,128)(2,1)S(1)}, bf16[256,256]{1,0:T(8,128)(2,1)S(1)}, u32[]{:S(2)}, u32[]{:S(2)}) collective-permute-start(bf16[256,256]{1,0:T(8,128)(2,1)S(1)} %get-tuple-element.56), channel_id=1, source_target_pairs={{0,3},{1,0},{2,1},{3,2},{4,7},{5,4},{6,5},{7,6},{8,11},{9,8},{10,9... | collective-permute-start | bytes 393224 | tf_op jit(solution)/shard_map/ppermute | solution.py:406
  66.2 12.0 %collective-permute-start.27 = (bf16[80,1024]{1,0:T(8,128)(2,1)S(1)}, bf16[80,1024]{1,0:T(8,128)(2,1)S(1)}, u32[]{:S(2)}, u32[]{:S(2)}) collective-permute-start(bf16[80,1024]{1,0:T(8,128)(2,1)S(1)} %get-tuple-element.81), channel_id=1, source_target_pairs={{0,1},{1,2},{2,3},{3,0},{4,5},{5,6},{6,7},{7,4},{8,9},{9,10},{10,1... | collective-permute-start | bytes 491528 | tf_op jit(solution)/shard_map/ppermute | solution.py:406
  72.4 7.5 %collective-permute-start.28 = (bf16[80,1024]{1,0:T(8,128)(2,1)S(1)}, bf16[80,1024]{1,0:T(8,128)(2,1)S(1)}, u32[]{:S(2)}, u32[]{:S(2)}) collective-permute-start(bf16[80,1024]{1,0:T(8,128)(2,1)S(1)} %get-tuple-element.82), channel_id=1, source_target_pairs={{0,2},{1,3},{2,0},{3,1},{4,6},{5,7},{6,4},{7,5},{8,10},{9,11},{10,... | collective-permute-start | bytes 491528 | tf_op jit(solution)/shard_map/ppermute | solution.py:406
  72.4 7.5 %collective-permute-start.29 = (bf16[80,1024]{1,0:T(8,128)(2,1)S(1)}, bf16[80,1024]{1,0:T(8,128)(2,1)S(1)}, u32[]{:S(2)}, u32[]{:S(2)}) collective-permute-start(bf16[80,1024]{1,0:T(8,128)(2,1)S(1)} %get-tuple-element.83), channel_id=1, source_target_pairs={{0,3},{1,0},{2,1},{3,2},{4,7},{5,4},{6,5},{7,6},{8,11},{9,8},{10,9... | collective-permute-start | bytes 491528 | tf_op jit(solution)/shard_map/ppermute | solution.py:406
  75.6 10.3 %collective-permute-start.22 = (bf16[64,1024]{1,0:T(8,128)(2,1)S(1)}, bf16[64,1024]{1,0:T(8,128)(2,1)S(1)}, u32[]{:S(2)}, u32[]{:S(2)}) collective-permute-start(bf16[64,1024]{1,0:T(8,128)(2,1)S(1)} %get-tuple-element.77), channel_id=1, source_target_pairs={{0,1},{1,2},{2,3},{3,0},{4,5},{5,6},{6,7},{7,4},{8,9},{9,10},{10,1... | collective-permute-start | bytes 393224 | tf_op jit(solution)/shard_map/ppermute | solution.py:406
  75.6 13.0 %collective-permute-start.23 = (bf16[64,1024]{1,0:T(8,128)(2,1)S(1)}, bf16[64,1024]{1,0:T(8,128)(2,1)S(1)}, u32[]{:S(2)}, u32[]{:S(2)}) collective-permute-start(bf16[64,1024]{1,0:T(8,128)(2,1)S(1)} %get-tuple-element.78), channel_id=1, source_target_pairs={{0,2},{1,3},{2,0},{3,1},{4,6},{5,7},{6,4},{7,5},{8,10},{9,11},{10,... | collective-permute-start | bytes 393224 | tf_op jit(solution)/shard_map/ppermute | solution.py:406
  78.2 11.7 %collective-permute-start.24 = (bf16[64,1024]{1,0:T(8,128)(2,1)S(1)}, bf16[64,1024]{1,0:T(8,128)(2,1)S(1)}, u32[]{:S(2)}, u32[]{:S(2)}) collective-permute-start(bf16[64,1024]{1,0:T(8,128)(2,1)S(1)} %get-tuple-element.79), channel_id=1, source_target_pairs={{0,3},{1,0},{2,1},{3,2},{4,7},{5,4},{6,5},{7,6},{8,11},{9,8},{10,9... | collective-permute-start | bytes 393224 | tf_op jit(solution)/shard_map/ppermute | solution.py:406
  80.0 30.8 %collective-permute-start.30 = (bf16[80,4096]{1,0:T(8,128)(2,1)S(1)}, bf16[80,4096]{1,0:T(8,128)(2,1)S(1)}, u32[]{:S(2)}, u32[]{:S(2)}) collective-permute-start(bf16[80,4096]{1,0:T(8,128)(2,1)S(1)} %join_strips.7.refs_0_.refs_3_), channel_id=1, source_target_pairs={{4,0},{8,4},{12,8},{16,12},{20,16},{24,20},{28,24},{0,28},{5,1},{9... | collective-permute-start | bytes 1966088 | tf_op jit(solution)/shard_map/ppermute | solution.py:412
  80.8 13.2 %collective-permute-start.17 = (bf16[64,1024]{1,0:T(8,128)(2,1)S(1)}, bf16[64,1024]{1,0:T(8,128)(2,1)S(1)}, u32[]{:S(2)}, u32[]{:S(2)}) collective-permute-start(bf16[64,1024]{1,0:T(8,128)(2,1)S(1)} %get-tuple-element.73), channel_id=1, source_target_pairs={{0,1},{1,2},{2,3},{3,0},{4,5},{5,6},{6,7},{7,4},{8,9},{9,10},{10,1... | collective-permute-start | bytes 393224 | tf_op jit(solution)/shard_map/ppermute | solution.py:406
  85.9 15.9 %collective-permute-start.18 = (bf16[64,1024]{1,0:T(8,128)(2,1)S(1)}, bf16[64,1024]{1,0:T(8,128)(2,1)S(1)}, u32[]{:S(2)}, u32[]{:S(2)}) collective-permute-start(bf16[64,1024]{1,0:T(8,128)(2,1)S(1)} %get-tuple-element.74), channel_id=1, source_target_pairs={{0,2},{1,3},{2,0},{3,1},{4,6},{5,7},{6,4},{7,5},{8,10},{9,11},{10,... | collective-permute-start | bytes 393224 | tf_op jit(solution)/shard_map/ppermute | solution.py:406
  88.7 13.2 %collective-permute-start.19 = (bf16[64,1024]{1,0:T(8,128)(2,1)S(1)}, bf16[64,1024]{1,0:T(8,128)(2,1)S(1)}, u32[]{:S(2)}, u32[]{:S(2)}) collective-permute-start(bf16[64,1024]{1,0:T(8,128)(2,1)S(1)} %get-tuple-element.75), channel_id=1, source_target_pairs={{0,3},{1,0},{2,1},{3,2},{4,7},{5,4},{6,5},{7,6},{8,11},{9,8},{10,9... | collective-permute-start | bytes 393224 | tf_op jit(solution)/shard_map/ppermute | solution.py:406
  89.8 13.4 %collective-permute-start.12 = (bf16[64,1024]{1,0:T(8,128)(2,1)S(1)}, bf16[64,1024]{1,0:T(8,128)(2,1)S(1)}, u32[]{:S(2)}, u32[]{:S(2)}) collective-permute-start(bf16[64,1024]{1,0:T(8,128)(2,1)S(1)} %get-tuple-element.69), channel_id=1, source_target_pairs={{0,1},{1,2},{2,3},{3,0},{4,5},{5,6},{6,7},{7,4},{8,9},{9,10},{10,1... | collective-permute-start | bytes 393224 | tf_op jit(solution)/shard_map/ppermute | solution.py:406
  93.9 13.6 %collective-permute-start.13 = (bf16[64,1024]{1,0:T(8,128)(2,1)S(1)}, bf16[64,1024]{1,0:T(8,128)(2,1)S(1)}, u32[]{:S(2)}, u32[]{:S(2)}) collective-permute-start(bf16[64,1024]{1,0:T(8,128)(2,1)S(1)} %get-tuple-element.70), channel_id=1, source_target_pairs={{0,2},{1,3},{2,0},{3,1},{4,6},{5,7},{6,4},{7,5},{8,10},{9,11},{10,... | collective-permute-start | bytes 393224 | tf_op jit(solution)/shard_map/ppermute | solution.py:406
  101.8 7.4 %collective-permute-start.14 = (bf16[64,1024]{1,0:T(8,128)(2,1)S(1)}, bf16[64,1024]{1,0:T(8,128)(2,1)S(1)}, u32[]{:S(2)}, u32[]{:S(2)}) collective-permute-start(bf16[64,1024]{1,0:T(8,128)(2,1)S(1)} %get-tuple-element.71), channel_id=1, source_target_pairs={{0,3},{1,0},{2,1},{3,2},{4,7},{5,4},{6,5},{7,6},{8,11},{9,8},{10,9... | collective-permute-start | bytes 393224 | tf_op jit(solution)/shard_map/ppermute | solution.py:406
  101.9 10.0 %collective-permute-start.25 = (bf16[64,4096]{1,0:T(8,128)(2,1)S(1)}, bf16[64,4096]{1,0:T(8,128)(2,1)S(1)}, u32[]{:S(2)}, u32[]{:S(2)}) collective-permute-start(bf16[64,4096]{1,0:T(8,128)(2,1)S(1)} %join_strips.6.refs_0_.refs_3_), channel_id=1, source_target_pairs={{4,0},{8,4},{12,8},{16,12},{20,16},{24,20},{28,24},{0,28},{5,1},{9... | collective-permute-start | bytes 1572872 | tf_op jit(solution)/shard_map/ppermute | solution.py:412
  103.2 12.3 %collective-permute-start.20 = (bf16[64,4096]{1,0:T(8,128)(2,1)S(1)}, bf16[64,4096]{1,0:T(8,128)(2,1)S(1)}, u32[]{:S(2)}, u32[]{:S(2)}) collective-permute-start(bf16[64,4096]{1,0:T(8,128)(2,1)S(1)} %join_strips.5.refs_0_.refs_3_), channel_id=1, source_target_pairs={{4,0},{8,4},{12,8},{16,12},{20,16},{24,20},{28,24},{0,28},{5,1},{9... | collective-permute-start | bytes 1572872 | tf_op jit(solution)/shard_map/ppermute | solution.py:412
  109.2 11.9 %collective-permute-start.15 = (bf16[64,4096]{1,0:T(8,128)(2,1)S(1)}, bf16[64,4096]{1,0:T(8,128)(2,1)S(1)}, u32[]{:S(2)}, u32[]{:S(2)}) collective-permute-start(bf16[64,4096]{1,0:T(8,128)(2,1)S(1)} %join_strips.4.refs_0_), channel_id=1, source_target_pairs={{4,0},{8,4},{12,8},{16,12},{20,16},{24,20},{28,24},{0,28},{5,1},{9... | collective-permute-start | bytes 1572872 | tf_op jit(solution)/shard_map/ppermute | solution.py:412
  110.7 17.4 %collective-permute-start.31 = (bf16[80,4096]{1,0:T(8,128)(2,1)S(1)}, bf16[80,4096]{1,0:T(8,128)(2,1)S(1)}, u32[]{:S(2)}, u32[]{:S(2)}) collective-permute-start(bf16[80,4096]{1,0:T(8,128)(2,1)S(1)} %collective-permute-done.30.refs_1_.refs_4_), channel_id=1, source_target_pairs={{4,0},{8,4},{12,8},{16,12},{20,16},{24,20},{28,24},{0,28},{5,1},{9... | collective-permute-start | bytes 1966088 | tf_op jit(solution)/shard_map/ppermute | solution.py:412
  111.9 33.2 %collective-permute-start.26 = (bf16[64,4096]{1,0:T(8,128)(2,1)S(1)}, bf16[64,4096]{1,0:T(8,128)(2,1)S(1)}, u32[]{:S(2)}, u32[]{:S(2)}) collective-permute-start(bf16[64,4096]{1,0:T(8,128)(2,1)S(1)} %collective-permute-done.25.refs_1_.refs_4_), channel_id=1, source_target_pairs={{4,0},{8,4},{12,8},{16,12},{20,16},{24,20},{28,24},{0,28},{5,1},{9... | collective-permute-start | bytes 1572872 | tf_op jit(solution)/shard_map/ppermute | solution.py:412
  115.5 46.7 %collective-permute-start.21 = (bf16[64,4096]{1,0:T(8,128)(2,1)S(1)}, bf16[64,4096]{1,0:T(8,128)(2,1)S(1)}, u32[]{:S(2)}, u32[]{:S(2)}) collective-permute-start(bf16[64,4096]{1,0:T(8,128)(2,1)S(1)} %collective-permute-done.20.refs_1_.refs_4_), channel_id=1, source_target_pairs={{4,0},{8,4},{12,8},{16,12},{20,16},{24,20},{28,24},{0,28},{5,1},{9... | collective-permute-start | bytes 1572872 | tf_op jit(solution)/shard_map/ppermute | solution.py:412
  121.1 58.1 %collective-permute-start.16 = (bf16[64,4096]{1,0:T(8,128)(2,1)S(1)}, bf16[64,4096]{1,0:T(8,128)(2,1)S(1)}, u32[]{:S(2)}, u32[]{:S(2)}) collective-permute-start(bf16[64,4096]{1,0:T(8,128)(2,1)S(1)} %collective-permute-done.15.refs_1_), channel_id=1, source_target_pairs={{4,0},{8,4},{12,8},{16,12},{20,16},{24,20},{28,24},{0,28},{5,1},{9... | collective-permute-start | bytes 1572872 | tf_op jit(solution)/shard_map/ppermute | solution.py:412

commit v2 on v1

--- a/solution.py
+++ b/solution.py
@@ -27,12 +27,16 @@
     return pltpu.CompilerParams(vmem_limit_bytes=mib * 1024 * 1024)
 
 
-def cost(flops, bytes_accessed):
-    return pl.CostEstimate(flops=int(flops), bytes_accessed=int(bytes_accessed), transcendentals=0)
+def cost(micros):
+    return pl.CostEstimate(flops=int(micros * 1e9), bytes_accessed=0, transcendentals=0)
 
 
 def vmem():
     return pl.BlockSpec(memory_space=pltpu.VMEM)
+
+
+def hold():
+    return pl.BlockSpec(memory_space=pl.ANY)
 
 
 def smem():
@@ -83,54 +87,38 @@
             )
 
 
-def range_blocks(me_ref, echo_ref, table, outs, chunks, chunk_count, devices, pulse_len):
+def range_blocks(me_ref, echo_ref, table, outs, chunk, devices, pulse_len):
     lines = echo_ref.shape[0] // 2
     samples = echo_ref.shape[1]
     width = outs[0].shape[1] // 2
     lane_blocks = samples // LANES
     window_blocks = (pulse_len + width) // LANES
-    index = 0
-    for chunk in chunks:
-        for step in range(devices):
-            target = lax.rem(me_ref[0] + step, devices)
-            first = target * (samples // devices // LANES) + chunk * (width // LANES)
-            pieces = [
-                echo_ref[
-                    :,
-                    pl.ds(
-                        pl.multiple_of(lax.rem(first + j, lane_blocks) * LANES, LANES), LANES
-                    ),
-                ]
-                for j in range(window_blocks)
+    for step in range(devices):
+        target = lax.rem(me_ref[0] + step, devices)
+        first = target * (samples // devices // LANES) + chunk * (width // LANES)
+        pieces = [
+            echo_ref[
+                :,
+                pl.ds(pl.multiple_of(lax.rem(first + j, lane_blocks) * LANES, LANES), LANES),
             ]
-            window = jnp.concatenate(pieces, axis=1)
-            product = jnp.dot(window, table, preferred_element_type=F32)
-            out = outs[index]
-            out[:, :width] = (product[:lines, :width] - product[lines:, width:]).astype(BF16)
-            out[:, width:] = (product[lines:, :width] + product[:lines, width:]).astype(BF16)
-            index += 1
-
-
-def first_range_kernel(devices, chunk_count, pulse_len, me_ref, rate_ref, echo_ref, table_ref, *rest):
+            for j in range(window_blocks)
+        ]
+        window = jnp.concatenate(pieces, axis=1)
+        product = jnp.dot(window, table, preferred_element_type=F32)
+        out = outs[step]
+        out[:, :width] = (product[:lines, :width] - product[lines:, width:]).astype(BF16)
+        out[:, width:] = (product[lines:, :width] + product[:lines, width:]).astype(BF16)
+
+
+def first_range_kernel(devices, pulse_len, me_ref, rate_ref, echo_ref, table_ref, *rest):
     outs, base_ref = rest[:-1], rest[-1]
     width = table_ref.shape[1] // 2
     build_chirp(rate_ref, table_ref, base_ref, pulse_len, width)
-    range_blocks(
-        me_ref, echo_ref, table_ref[...], outs, [0], chunk_count, devices, pulse_len
-    )
-
-
-def rest_range_kernel(devices, chunk_count, pulse_len, me_ref, echo_ref, table_ref, *outs):
-    range_blocks(
-        me_ref,
-        echo_ref,
-        table_ref[...],
-        outs,
-        range(1, chunk_count),
-        chunk_count,
-        devices,
-        pulse_len,
-    )
+    range_blocks(me_ref, echo_ref, table_ref[...], outs, 0, devices, pulse_len)
+
+
+def next_range_kernel(devices, chunk, pulse_len, me_ref, echo_ref, table_ref, _, *outs):
+    range_blocks(me_ref, echo_ref, table_ref[...], outs, chunk, devices, pulse_len)
 
 
 def tables_kernel(
@@ -222,7 +210,7 @@
     lax.fori_loop(0, half // RIM + 1, filter_rows, 0)
 
 
-def forward_kernel(devices, chunk, me_ref, dft_ref, coef_ref, filt_ref, *rest):
+def forward_kernel(devices, chunk, me_ref, dft_ref, coef_ref, filt_ref, _, *rest):
     blocks, out_ref, joined = rest[:devices], rest[devices], rest[devices + 1]
     size = dft_ref.shape[0]
     half = size // 2
@@ -261,7 +249,7 @@
         out_ref[rows, width:] = (filt_re * v_im + filt_im * v_re).astype(BF16)
 
 
-def inverse_kernel(devices, line_count, first_row, rows, chunk_count, me_ref, inv_ref, *rest):
+def inverse_kernel(devices, line_count, first_row, rows, chunk_count, me_ref, inv_ref, _, *rest):
     spectra, outs = rest[:chunk_count], rest[chunk_count:]
     pieces = []
     for step in range(devices):
@@ -281,7 +269,7 @@
             outs[step][:, first : first + width] = part[:, width:]
 
 
-def join_kernel(devices, has_first, has_last, me_ref, *rest):
+def join_kernel(devices, has_first, has_last, me_ref, _before, _passed, *rest):
     blocks, out_ref = rest[:devices], rest[devices]
     rows, width = blocks[0].shape[0], blocks[0].shape[1] // 2
     samples = out_ref.shape[1] // 2
@@ -318,17 +306,26 @@
     if has_before:
         before = refs[position : position + dates]
         position += dates + 2
-    image_ref, result_ref, sums_ref = refs[position : position + 3]
+    image_ref, result_ref, token_ref, sums_ref = refs[position : position + 4]
+    token_ref[...] = jnp.zeros(token_ref.shape, F32)
     lines = image_ref.shape[1]
     samples = image_ref.shape[2]
     window = lines + 2 * RIM
     half_az, half_rg = WIN_AZ // 2, WIN_RG // 2
     block = min(samples, 256)
+    terms = 1 + 3 * SPAN
     out_id = lax.broadcasted_iota(jnp.int32, (lines, window), 0)
     in_id = lax.broadcasted_iota(jnp.int32, (lines, window), 1) - RIM
-    band = jnp.where(jnp.abs(in_id - out_id) <= half_az, 1.0, 0.0).astype(BF16)
-    band = jnp.concatenate([band, band], axis=1)
-    terms = 1 + 3 * SPAN
+    down = jnp.where(jnp.abs(in_id - out_id) <= half_az, 1.0, 0.0).astype(BF16)
+    down = jnp.concatenate([down, down], axis=1)
+    size = block + 2 * LANES
+    in_id = lax.broadcasted_iota(jnp.int32, (size, block), 0) - LANES
+    out_id = lax.broadcasted_iota(jnp.int32, (size, block), 1)
+    across = jnp.where(jnp.abs(in_id - out_id) <= half_rg, 1.0, 0.0).astype(BF16)
+
+    def halves(value):
+        high = value.astype(BF16)
+        return high, (value - high.astype(F32)).astype(BF16)
 
     def load(date, start):
         piece = now[date][:, pl.ds(start, block)]
@@ -337,49 +334,45 @@
             piece = jnp.concatenate(
                 [held[held.shape[0] - 2 * RIM :, pl.ds(start, block)], piece], axis=0
             )
-        return piece
+        return piece.astype(F32)
 
     def add_lines(value, term, start):
-        high = value.astype(BF16)
-        low = (value - high.astype(F32)).astype(BF16)
-        both = jnp.concatenate([high, low], axis=0)
-        sums_ref[term, :, pl.ds(start + LANES, block)] = jnp.dot(
-            band, both, preferred_element_type=F32
-        )
+        both = jnp.concatenate(halves(value), axis=0)
+        total = jnp.dot(down, both, preferred_element_type=F32)
+        rows = slice(term * lines, (term + 1) * lines)
+        for half, part in enumerate(halves(total)):
+            sums_ref[half, rows, pl.ds(start + LANES, block)] = part
+
+    edge = jnp.zeros((terms * lines, LANES), BF16)
+    for half in range(2):
+        sums_ref[half, :, :LANES] = edge
+        sums_ref[half, :, samples + LANES :] = edge
 
     def first_pass(index, _):
         start = pl.multiple_of(index * block, block)
         re = load(0, start)
         im = load(0, samples + start)
-        re, im = re.astype(F32), im.astype(F32)
         image_ref[0, :, pl.ds(start, block)] = re[RIM : RIM + lines].astype(BF16)
         image_ref[1, :, pl.ds(start, block)] = im[RIM : RIM + lines].astype(BF16)
         add_lines(re * re + im * im, 0, start)
         for date in range(1, dates):
-            other_re = load(date, start).astype(F32)
-            other_im = load(date, samples + start).astype(F32)
+            other_re = load(date, start)
+            other_im = load(date, samples + start)
             term = 3 * date - 2
             add_lines(re * other_re + im * other_im, term, start)
             add_lines(im * other_re - re * other_im, term + 1, start)
             add_lines(other_re * other_re + other_im * other_im, term + 2, start)
         return 0
 
-    edge = jnp.zeros((lines, LANES), F32)
-    for term in range(terms):
-        sums_ref[term, :, :LANES] = edge
-        sums_ref[term, :, samples + LANES :] = edge
-    lax.fori_loop(0, samples // block, first_pass, 0)
+    lax.fori_loop(0, samples // block, first_pass, 0, unroll=2)
 
     def second_pass(index, _):
         start = pl.multiple_of(index * block, block)
-        size = block + 2 * LANES
+        total = jnp.dot(sums_ref[0, :, pl.ds(start, size)], across, preferred_element_type=F32)
+        total += jnp.dot(sums_ref[1, :, pl.ds(start, size)], across, preferred_element_type=F32)
 
         def box(term):
-            wide = sums_ref[term, :, pl.ds(start, size)]
-            pair = wide + pltpu.roll(wide, 1, 1)
-            four = pair + pltpu.roll(pair, 2, 1)
-            five = four + pltpu.roll(wide, 4, 1)
-            return pltpu.roll(five, size - half_rg, 1)[:, LANES : LANES + block]
+            return total[term * lines : (term + 1) * lines]
 
         own = box(0)
         for date in range(1, dates):
@@ -389,7 +382,7 @@
             result_ref[date - 1, 1, :, pl.ds(start, block)] = (box(term + 1) * scale).astype(BF16)
         return 0
 
-    lax.fori_loop(0, samples // block, second_pass, 0)
+    lax.fori_loop(0, samples // block, second_pass, 0, unroll=2)
 
 
 def kernel_taps(fraction):
@@ -426,32 +419,30 @@
     width = owned // chunk_count
     depth = pulse_len + width
     block_type = jax.ShapeDtypeStruct((lines, 2 * width), BF16)
-    flops = 2 * 2 * lines * depth * 2 * width * devices
-    table, *first_blocks = pl.pallas_call(
-        functools.partial(first_range_kernel, devices, chunk_count, pulse_len),
+    table, *blocks = pl.pallas_call(
+        functools.partial(first_range_kernel, devices, pulse_len),
         out_shape=[jax.ShapeDtypeStruct((depth, 2 * width), BF16)] + [block_type] * devices,
         in_specs=[smem(), smem(), vmem()],
         out_specs=[vmem()] * (devices + 1),
         scratch_shapes=[pltpu.VMEM((2, PACK, pulse_len + 2 * width + LANES), F32)],
         compiler_params=params(40),
-        cost_estimate=cost(2 * flops, 4 * lines * samples),
+        cost_estimate=cost(2),
         name="range_first",
     )(me, range_rate.reshape(1), echo)
-    columns = [scatter(first_blocks, "swath")]
-    order = first_blocks[0]
-    if chunk_count > 1:
-        rest = pl.pallas_call(
-            functools.partial(rest_range_kernel, devices, chunk_count, pulse_len),
-            out_shape=[block_type] * (devices * (chunk_count - 1)),
-            in_specs=[smem(), vmem(), vmem()],
-            out_specs=[vmem()] * (devices * (chunk_count - 1)),
-            compiler_params=params(40),
-            cost_estimate=cost((chunk_count - 1) * flops, 4 * lines * samples),
-            name="range_rest",
-        )(me, echo, table)
-        for chunk in range(chunk_count - 1):
-            columns.append(scatter(rest[chunk * devices : (chunk + 1) * devices], "swath"))
-        order = rest[-1]
+    columns = []
+    for chunk in range(chunk_count):
+        if chunk > 0:
+            blocks = pl.pallas_call(
+                functools.partial(next_range_kernel, devices, chunk, pulse_len),
+                out_shape=[block_type] * devices,
+                in_specs=[smem(), vmem(), vmem(), hold()],
+                out_specs=[vmem()] * devices,
+                compiler_params=params(40),
+                cost_estimate=cost(1.5),
+                name="range_next",
+            )(me, echo, table, blocks[0])
+        with jax.named_scope(f"columns_{chunk}"):
+            columns.append(scatter(blocks, "swath"))
 
     taps = kernel_taps(frac_shift[0])
     signs = 1.0 - 2.0 * ((line_offset[0] + jnp.arange(TAPS, dtype=jnp.int32)) % 2).astype(F32)
@@ -464,12 +455,12 @@
             jax.ShapeDtypeStruct((3, half, LANES), F32),
             jax.ShapeDtypeStruct((2, half + RIM, owned), F32),
         ],
-        in_specs=[smem(), smem(), vmem(), pl.BlockSpec(memory_space=pl.ANY)],
+        in_specs=[smem(), smem(), vmem(), hold()],
         out_specs=[vmem()] * 4,
         compiler_params=params(40),
-        cost_estimate=cost(size * size * 64, 8 * size * size),
+        cost_estimate=cost(8.5),
         name="azimuth_tables",
-    )(line_offset, taps, azimuth_rate.reshape(1, owned), order)
+    )(line_offset, taps, azimuth_rate.reshape(1, owned), blocks[0])
 
     spectra = []
     for chunk in range(chunk_count):
@@ -477,45 +468,46 @@
             pl.pallas_call(
                 functools.partial(forward_kernel, devices, chunk),
                 out_shape=jax.ShapeDtypeStruct((size, 2 * width), BF16),
-                in_specs=[smem()] + [vmem()] * (3 + devices),
+                in_specs=[smem()] + [vmem()] * 3 + [hold()] + [vmem()] * devices,
                 out_specs=vmem(),
                 scratch_shapes=[pltpu.VMEM((size, 2 * width), BF16)],
                 compiler_params=params(40),
-                cost_estimate=cost(4 * size * size * width, 2 * size * size + 8 * size * width),
+                cost_estimate=cost(1),
                 name="azimuth_forward",
-            )(me, dft, coef, filt, *columns[chunk])
+            )(me, dft, coef, filt, spectra[-1] if spectra else coef, *columns[chunk])
         )
 
     step_lines = min(lines, LINE_STEP)
     steps = lines // step_lines
-    image = result = held = None
+    image = result = held = outs = own = None
+    passed = []
     for step in range(steps):
         rows = step_lines + (2 * RIM if step == 0 else 0)
         first_row = step * step_lines + (0 if step == 0 else 2 * RIM)
         outs = pl.pallas_call(
             functools.partial(inverse_kernel, devices, lines, first_row, rows, chunk_count),
             out_shape=[jax.ShapeDtypeStruct((rows, 2 * owned), BF16)] * devices,
-            in_specs=[smem()] + [vmem()] * (1 + chunk_count),
+            in_specs=[smem(), vmem(), hold()] + [vmem()] * chunk_count,
             out_specs=[vmem()] * devices,
             compiler_params=params(40),
-            cost_estimate=cost(
-                4 * devices * rows * size * owned, 2 * size * size + 4 * size * owned
-            ),
+            cost_estimate=cost(0.8),
             name="azimuth_inverse",
-        )(me, inv, *spectra)
-        strips = scatter(outs, "swath")
+        )(me, inv, outs[0] if outs else spectra[-1], *spectra)
+        with jax.named_scope(f"strips_{step}"):
+            strips = scatter(outs, "swath")
         own = pl.pallas_call(
             functools.partial(join_kernel, devices, step == 0, step == steps - 1),
             out_shape=jax.ShapeDtypeStruct((rows, 2 * samples), BF16),
-            in_specs=[smem()] + [vmem()] * devices,
+            in_specs=[smem(), hold(), hold()] + [vmem()] * devices,
             out_specs=vmem(),
             compiler_params=params(40),
-            cost_estimate=cost(rows * samples, 8 * rows * samples),
+            cost_estimate=cost(0.3),
             name="join_strips",
-        )(me, *strips)
+        )(me, own if step else me, passed[step - 2] if step > 1 else me, *strips)
         now = [own]
-        for _ in range(SPAN):
-            now.append(from_next(now[-1], "date"))
+        for span in range(SPAN):
+            with jax.named_scope(f"date_{step}_{span}"):
+                now.append(from_next(now[-1], "date"))
         operands = list(now)
         in_specs = [vmem()] * len(now)
         aliases = {}
@@ -523,27 +515,30 @@
             operands += held + [image, result]
             in_specs += [vmem()] * len(held) + [pl.BlockSpec(memory_space=pl.ANY)] * 2
             aliases = {len(operands) - 2: 0, len(operands) - 1: 1}
-        image, result = pl.pallas_call(
+        image, result, token = pl.pallas_call(
             functools.partial(coherence_kernel, held is not None),
             grid=(1,),
             out_shape=[
                 jax.ShapeDtypeStruct((2, lines, samples), BF16),
                 jax.ShapeDtypeStruct((SPAN, 2, lines, samples), BF16),
+                jax.ShapeDtypeStruct((8, LANES), F32),
             ],
             in_specs=in_specs,
             out_specs=[
                 pl.BlockSpec((2, step_lines, samples), lambda i, s=step: (0, s, 0)),
                 pl.BlockSpec((SPAN, 2, step_lines, samples), lambda i, s=step: (0, 0, s, 0)),
+                pl.BlockSpec((8, LANES), lambda i: (0, 0)),
             ],
             scratch_shapes=[
-                pltpu.VMEM((1 + 3 * SPAN, step_lines, samples + 2 * LANES), F32)
+                pltpu.VMEM((2, (1 + 3 * SPAN) * step_lines, samples + 2 * LANES), BF16)
             ],
             input_output_aliases=aliases,
             compiler_params=params(48),
-            cost_estimate=cost(500 * step_lines * samples, 30 * step_lines * samples),
+            cost_estimate=cost(6),
             name="coherence",
         )(*operands)
         held = now
+        passed.append(token)
     return (image[None], result[None])
 
 

time: 198 us -> 144 us (0.73)
  Pallas kernels: 89.7 us -> 45.9 us
  starting transfers between devices: 66.5 us -> 61.4 us
  waiting for transfers between devices: 34.2 us -> 30 us
    pallas_call x4, Pallas kernels: 68.1 us -> 24 us  [body(): pl.pallas_call(functools.partial(coherence_kernel, held is not None), gri...]
    ppermute x24, starting transfers between devices: 54.8 us -> 45.5 us  [scatter(): moved.append(lax.ppermute(blocks[step], axis, route))]
    ppermute x24, waiting for transfers between devices: 24.4 us -> 19.5 us  [scatter(): moved.append(lax.ppermute(blocks[step], axis, route))]
    ppermute x8, starting transfers between devices: 11.8 us -> 15.9 us  [from_next(): lax.ppermute(block, axis, [((i + 1) % count, i) for i in range(count)])]
    pallas_call x2 -> x4, Pallas kernels: 6.22 us -> 6.53 us  [the longest x3 4.76 us: body(): pl.pallas_call(functools.partial(next_range_kernel, devices, chunk, pulse...]
  transfers between devices with their start and end apart: 32 -> 32, of which waited for: 11 -> 9; matrix products, arithmetic and copies ran while one was open for 1% -> 1% of each run, Pallas kernels for 33% -> 25%
where the time goes in v2:
time: 144 us; the launch traced here: 143 us
  starting transfers between devices  61.4 us (43%)
  Pallas kernels  45.9 us (32%)
  waiting for transfers between devices  30 us (21%)
  between operations  2.79 us (2%)
  local copies, waits for them, and re-layouts  1.59 us (1%)
    ppermute x24, starting transfers between devices, scatter(): moved.append(lax.ppermute(blocks[step], axis, route))  45.5 us
    pallas_call x4, Pallas kernels, body(): pl.pallas_call(functools.partial(coherence_kernel, held is not None), gri...  24 us
    ppermute x24, waiting for transfers between devices, scatter(): moved.append(lax.ppermute(blocks[step], axis, route))  19.5 us
    ppermute x8, starting transfers between devices, from_next(): lax.ppermute(block, axis, [((i + 1) % count, i) for i in range(count)])  15.9 us
    ppermute x8, waiting for transfers between devices, from_next(): lax.ppermute(block, axis, [((i + 1) % count, i) for i in range(count)])  10.5 us
    pallas_call x1, Pallas kernels, body(): pl.pallas_call(tables_kernel, out_shape=[jax.ShapeDtypeStruct((size, size...  8.61 us
    pallas_call x3, Pallas kernels, body(): pl.pallas_call(functools.partial(next_range_kernel, devices, chunk, pulse...  4.76 us
    pallas_call x4, Pallas kernels, body(): pl.pallas_call(functools.partial(forward_kernel, devices, chunk), out_sha...  3.62 us
  transfers between devices with their start and end apart: 32, of which 9 were waited for; matrix products, arithmetic and copies ran while one was open for 1% of the time, Pallas kernels for 25%

profile of v2, /device:TPU:0, one launch (start us, length us, event | category | flops | bytes accessed | tf_op | source)
XLA Modules:
  0.0 143.0 jit_solution(10961854014259276031)
XLA Ops:
  1.3 1.6 %copy-done = bf16[1,2,256,2048]{3,2,1,0:T(8,128)(2,1)S(1)} copy-done((bf16[1,2,256,2048]{3,2,1,0:T(8,128)(2,1)S(1)}, bf16[1,2,256,2048]{3,2,1,0:T(8,128)(2,1)}, u32[]{:S(2)}) %copy-start) | copy-done | bytes 2097176
  2.9 1.8 %range_first.1 = (bf16[1152,256]{1,0:T(8,128)(2,1)S(1)}, bf16[256,256]{1,0:T(8,128)(2,1)S(1)}, bf16[256,256]{1,0:T(8,128)(2,1)S(1)}, bf16[256,256]{1,0:T(8,128)(2,1)S(1)}, bf16[256,256]{1,0:T(8,128)(2,1)S(1)}) custom-call(s32[1]{0:T(128)} %bitcast.me_ref._before._passed, f32[1]{0:T(128)} %bitcast.9.rate_ref, bf16[512,2048]{1,0:T(8,128)(2,1)S(1)} %bitcast.12), custom_call_target="tpu_custom_call" | custom-call | flops 2000000000 | tf_op jit(solution)/shard_map/range_first/pallas_call | solution.py:422
  4.6 3.1 %collective-permute-start = (bf16[256,256]{1,0:T(8,128)(2,1)S(1)}, bf16[256,256]{1,0:T(8,128)(2,1)S(1)}, u32[]{:S(2)}, u32[]{:S(2)}) collective-permute-start(bf16[256,256]{1,0:T(8,128)(2,1)S(1)} %get-tuple-element.58), channel_id=1, source_target_pairs={{0,1},{1,2},{2,3},{3,0},{4,5},{5,6},{6,7},{7,4},{8,9},{9,10},{10,1... | collective-permute-start | bytes 393224 | tf_op jit(solution)/shard_map/columns_0/ppermute | solution.py:399
  7.7 2.6 %collective-permute-start.1 = (bf16[256,256]{1,0:T(8,128)(2,1)S(1)}, bf16[256,256]{1,0:T(8,128)(2,1)S(1)}, u32[]{:S(2)}, u32[]{:S(2)}) collective-permute-start(bf16[256,256]{1,0:T(8,128)(2,1)S(1)} %get-tuple-element.59), channel_id=1, source_target_pairs={{0,2},{1,3},{2,0},{3,1},{4,6},{5,7},{6,4},{7,5},{8,10},{9,11},{10,... | collective-permute-start | bytes 393224 | tf_op jit(solution)/shard_map/columns_0/ppermute | solution.py:399
  10.3 1.4 collective-permute-start.2
  11.7 1.6 %range_next.3 = (bf16[256,256]{1,0:T(8,128)(2,1)S(1)}, bf16[256,256]{1,0:T(8,128)(2,1)S(1)}, bf16[256,256]{1,0:T(8,128)(2,1)S(1)}, bf16[256,256]{1,0:T(8,128)(2,1)S(1)}) custom-call(s32[1]{0:T(128)} %bitcast.me_ref._before._passed, bf16[512,2048]{1,0:T(8,128)(2,1)S(1)} %bitcast.13, bf16[1152,256]{1,0:T(8,128)(2,1)S(1)} %get-tuple-element.49.table_ref, ...), custom_call_target="tpu_custom_call" | custom-call | flops 1500000000 | tf_op jit(solution)/shard_map/range_next/pallas_call | solution.py:435
  15.6 1.6 %range_next.4 = (bf16[256,256]{1,0:T(8,128)(2,1)S(1)}, bf16[256,256]{1,0:T(8,128)(2,1)S(1)}, bf16[256,256]{1,0:T(8,128)(2,1)S(1)}, bf16[256,256]{1,0:T(8,128)(2,1)S(1)}) custom-call(s32[1]{0:T(128)} %bitcast.me_ref._before._passed, bf16[512,2048]{1,0:T(8,128)(2,1)S(1)} %bitcast.14, bf16[1152,256]{1,0:T(8,128)(2,1)S(1)} %get-tuple-element.49.table_ref, ...), custom_call_target="tpu_custom_call" | custom-call | flops 1500000000 | tf_op jit(solution)/shard_map/range_next/pallas_call | solution.py:435
  18.4 1.6 %range_next.5 = (bf16[256,256]{1,0:T(8,128)(2,1)S(1)}, bf16[256,256]{1,0:T(8,128)(2,1)S(1)}, bf16[256,256]{1,0:T(8,128)(2,1)S(1)}, bf16[256,256]{1,0:T(8,128)(2,1)S(1)}) custom-call(s32[1]{0:T(128)} %bitcast.me_ref._before._passed, bf16[512,2048]{1,0:T(8,128)(2,1)S(1)} %bitcast.15, bf16[1152,256]{1,0:T(8,128)(2,1)S(1)} %get-tuple-element.49.table_ref, ...), custom_call_target="tpu_custom_call" | custom-call | flops 1500000000 | tf_op jit(solution)/shard_map/range_next/pallas_call | solution.py:435
  20.1 2.9 %collective-permute-start.5 = (bf16[256,256]{1,0:T(8,128)(2,1)S(1)}, bf16[256,256]{1,0:T(8,128)(2,1)S(1)}, u32[]{:S(2)}, u32[]{:S(2)}) collective-permute-start(bf16[256,256]{1,0:T(8,128)(2,1)S(1)} %get-tuple-element.63), channel_id=1, source_target_pairs={{0,3},{1,0},{2,1},{3,2},{4,7},{5,4},{6,5},{7,6},{8,11},{9,8},{10,9... | collective-permute-start | bytes 393224 | tf_op jit(solution)/shard_map/columns_1/ppermute | solution.py:399
  22.9 2.8 %collective-permute-start.6 = (bf16[256,256]{1,0:T(8,128)(2,1)S(1)}, bf16[256,256]{1,0:T(8,128)(2,1)S(1)}, u32[]{:S(2)}, u32[]{:S(2)}) collective-permute-start(bf16[256,256]{1,0:T(8,128)(2,1)S(1)} %get-tuple-element.64), channel_id=1, source_target_pairs={{0,1},{1,2},{2,3},{3,0},{4,5},{5,6},{6,7},{7,4},{8,9},{9,10},{10,1... | collective-permute-start | bytes 393224 | tf_op jit(solution)/shard_map/columns_2/ppermute | solution.py:399
  25.8 8.6 %azimuth_tables.1 = (bf16[1024,1024]{1,0:T(8,128)(2,1)S(1)}, bf16[1040,1024]{1,0:T(8,128)(2,1)S(1)}, f32[3,512,128]{2,1,0:T(8,128)S(1)}, f32[2,520,512]{2,1,0:T(8,128)S(1)}) custom-call(s32[1]{0:T(128)} %copy.20.shift_ref, f32[9]{0:T(128)S(1)} %pad_maximum_fusion.taps_ref, f32[1,512]{1,0:T(1,128)S(1)} %bitcast.16, ...), custom_call_target="tpu_custom_call" | custom-call | flops 8499999744 | tf_op jit(solution)/shard_map/azimuth_tables/pallas_call | solution.py:450
  34.4 3.9 %collective-permute-start.7 = (bf16[256,256]{1,0:T(8,128)(2,1)S(1)}, bf16[256,256]{1,0:T(8,128)(2,1)S(1)}, u32[]{:S(2)}, u32[]{:S(2)}) collective-permute-start(bf16[256,256]{1,0:T(8,128)(2,1)S(1)} %get-tuple-element.65), channel_id=1, source_target_pairs={{0,2},{1,3},{2,0},{3,1},{4,6},{5,7},{6,4},{7,5},{8,10},{9,11},{10,... | collective-permute-start | bytes 393224 | tf_op jit(solution)/shard_map/columns_2/ppermute | solution.py:399
  38.4 0.9 azimuth_forward.4._.rest_0_
  39.3 2.1 %collective-permute-start.9 = (bf16[256,256]{1,0:T(8,128)(2,1)S(1)}, bf16[256,256]{1,0:T(8,128)(2,1)S(1)}, u32[]{:S(2)}, u32[]{:S(2)}) collective-permute-start(bf16[256,256]{1,0:T(8,128)(2,1)S(1)} %get-tuple-element.67), channel_id=1, source_target_pairs={{0,1},{1,2},{2,3},{3,0},{4,5},{5,6},{6,7},{7,4},{8,9},{9,10},{10,1... | collective-permute-start | bytes 393224 | tf_op jit(solution)/shard_map/columns_3/ppermute | solution.py:399
  41.4 2.4 %collective-permute-start.11 = (bf16[256,256]{1,0:T(8,128)(2,1)S(1)}, bf16[256,256]{1,0:T(8,128)(2,1)S(1)}, u32[]{:S(2)}, u32[]{:S(2)}) collective-permute-start(bf16[256,256]{1,0:T(8,128)(2,1)S(1)} %get-tuple-element.69), channel_id=1, source_target_pairs={{0,3},{1,0},{2,1},{3,2},{4,7},{5,4},{6,5},{7,6},{8,11},{9,8},{10,9... | collective-permute-start | bytes 393224 | tf_op jit(solution)/shard_map/columns_3/ppermute | solution.py:399
  43.8 0.9 azimuth_forward.5._.rest_1_
  44.7 4.6 %collective-permute-done.7.rest_2_ = bf16[256,256]{1,0:T(8,128)(2,1)S(1)} collective-permute-done((bf16[256,256]{1,0:T(8,128)(2,1)S(1)}, bf16[256,256]{1,0:T(8,128)(2,1)S(1)}, u32[]{:S(2)}, u32[]{:S(2)}) %collective-permute-start.7) | collective-permute-done | bytes 131104 | tf_op jit(solution)/shard_map/columns_2/ppermute | solution.py:399
  49.3 0.9 azimuth_forward.6._.rest_2_
  50.2 3.8 %collective-permute-done.10.rest_2_ = bf16[256,256]{1,0:T(8,128)(2,1)S(1)} collective-permute-done((bf16[256,256]{1,0:T(8,128)(2,1)S(1)}, bf16[256,256]{1,0:T(8,128)(2,1)S(1)}, u32[]{:S(2)}, u32[]{:S(2)}) %collective-permute-start.10) | collective-permute-done | bytes 131104 | tf_op jit(solution)/shard_map/columns_3/ppermute | solution.py:399
  54.0 0.9 azimuth_forward.7._.rest_3_
  54.9 0.9 azimuth_inverse.4
  55.8 2.0 %collective-permute-start.12 = (bf16[80,1024]{1,0:T(8,128)(2,1)S(1)}, bf16[80,1024]{1,0:T(8,128)(2,1)S(1)}, u32[]{:S(2)}, u32[]{:S(2)}) collective-permute-start(bf16[80,1024]{1,0:T(8,128)(2,1)S(1)} %get-tuple-element.71), channel_id=1, source_target_pairs={{0,1},{1,2},{2,3},{3,0},{4,5},{5,6},{6,7},{7,4},{8,9},{9,10},{10,1... | collective-permute-start | bytes 491528 | tf_op jit(solution)/shard_map/strips_0/ppermute | solution.py:399
  57.8 1.7 %collective-permute-start.13 = (bf16[80,1024]{1,0:T(8,128)(2,1)S(1)}, bf16[80,1024]{1,0:T(8,128)(2,1)S(1)}, u32[]{:S(2)}, u32[]{:S(2)}) collective-permute-start(bf16[80,1024]{1,0:T(8,128)(2,1)S(1)} %get-tuple-element.72), channel_id=1, source_target_pairs={{0,2},{1,3},{2,0},{3,1},{4,6},{5,7},{6,4},{7,5},{8,10},{9,11},{10,... | collective-permute-start | bytes 491528 | tf_op jit(solution)/shard_map/strips_0/ppermute | solution.py:399
  60.2 4.6 %collective-permute-done.12.rest_1_ = bf16[80,1024]{1,0:T(8,128)(2,1)S(1)} collective-permute-done((bf16[80,1024]{1,0:T(8,128)(2,1)S(1)}, bf16[80,1024]{1,0:T(8,128)(2,1)S(1)}, u32[]{:S(2)}, u32[]{:S(2)}) %collective-permute-start.12) | collective-permute-done | bytes 163872 | tf_op jit(solution)/shard_map/strips_0/ppermute | solution.py:399
  64.9 4.4 %collective-permute-done.13.rest_2_ = bf16[80,1024]{1,0:T(8,128)(2,1)S(1)} collective-permute-done((bf16[80,1024]{1,0:T(8,128)(2,1)S(1)}, bf16[80,1024]{1,0:T(8,128)(2,1)S(1)}, u32[]{:S(2)}, u32[]{:S(2)}) %collective-permute-start.13) | collective-permute-done | bytes 163872 | tf_op jit(solution)/shard_map/strips_0/ppermute | solution.py:399
  69.3 2.2 %collective-permute-start.18 = (bf16[80,4096]{1,0:T(8,128)(2,1)S(1)}, bf16[80,4096]{1,0:T(8,128)(2,1)S(1)}, u32[]{:S(2)}, u32[]{:S(2)}) collective-permute-start(bf16[80,4096]{1,0:T(8,128)(2,1)S(1)} %join_strips.4._before.refs_0_.refs_3_), channel_id=1, source_target_pairs={{4,0},{8,4},{12,8},{16,12},{20,16},{24,20},{28,24},{0,28},{5,1},{9... | collective-permute-start | bytes 1966088 | tf_op jit(solution)/shard_map/date_0_0/ppermute | solution.py:405
  71.5 0.7 azimuth_inverse.5
  72.2 4.1 %collective-permute-start.15 = (bf16[64,1024]{1,0:T(8,128)(2,1)S(1)}, bf16[64,1024]{1,0:T(8,128)(2,1)S(1)}, u32[]{:S(2)}, u32[]{:S(2)}) collective-permute-start(bf16[64,1024]{1,0:T(8,128)(2,1)S(1)} %get-tuple-element.75), channel_id=1, source_target_pairs={{0,1},{1,2},{2,3},{3,0},{4,5},{5,6},{6,7},{7,4},{8,9},{9,10},{10,1... | collective-permute-start | bytes 393224 | tf_op jit(solution)/shard_map/strips_1/ppermute | solution.py:399
  76.3 2.4 %collective-permute-start.17 = (bf16[64,1024]{1,0:T(8,128)(2,1)S(1)}, bf16[64,1024]{1,0:T(8,128)(2,1)S(1)}, u32[]{:S(2)}, u32[]{:S(2)}) collective-permute-start(bf16[64,1024]{1,0:T(8,128)(2,1)S(1)} %get-tuple-element.77), channel_id=1, source_target_pairs={{0,3},{1,0},{2,1},{3,2},{4,7},{5,4},{6,5},{7,6},{8,11},{9,8},{10,9... | collective-permute-start | bytes 393224 | tf_op jit(solution)/shard_map/strips_1/ppermute | solution.py:399
  78.8 0.8 collective-permute-done.18.refs_1_.refs_4_
  79.6 3.1 %collective-permute-start.19 = (bf16[80,4096]{1,0:T(8,128)(2,1)S(1)}, bf16[80,4096]{1,0:T(8,128)(2,1)S(1)}, u32[]{:S(2)}, u32[]{:S(2)}) collective-permute-start(bf16[80,4096]{1,0:T(8,128)(2,1)S(1)} %collective-permute-done.18.refs_1_.refs_4_), channel_id=1, source_target_pairs={{4,0},{8,4},{12,8},{16,12},{20,16},{24,20},{28,24},{0,28},{5,1},{9... | collective-permute-start | bytes 1966088 | tf_op jit(solution)/shard_map/date_0_1/ppermute | solution.py:405
  82.7 2.1 %collective-permute-done.16.rest_2_ = bf16[64,1024]{1,0:T(8,128)(2,1)S(1)} collective-permute-done((bf16[64,1024]{1,0:T(8,128)(2,1)S(1)}, bf16[64,1024]{1,0:T(8,128)(2,1)S(1)}, u32[]{:S(2)}, u32[]{:S(2)}) %collective-permute-start.16) | collective-permute-done | bytes 131104 | tf_op jit(solution)/shard_map/strips_1/ppermute | solution.py:399
  84.8 1.8 %collective-permute-start.23 = (bf16[64,4096]{1,0:T(8,128)(2,1)S(1)}, bf16[64,4096]{1,0:T(8,128)(2,1)S(1)}, u32[]{:S(2)}, u32[]{:S(2)}) collective-permute-start(bf16[64,4096]{1,0:T(8,128)(2,1)S(1)} %join_strips.5._before.refs_0_.refs_3_), channel_id=1, source_target_pairs={{4,0},{8,4},{12,8},{16,12},{20,16},{24,20},{28,24},{0,28},{5,1},{9... | collective-permute-start | bytes 1572872 | tf_op jit(solution)/shard_map/date_1_0/ppermute | solution.py:405
  87.3 3.4 %collective-permute-start.20 = (bf16[64,1024]{1,0:T(8,128)(2,1)S(1)}, bf16[64,1024]{1,0:T(8,128)(2,1)S(1)}, u32[]{:S(2)}, u32[]{:S(2)}) collective-permute-start(bf16[64,1024]{1,0:T(8,128)(2,1)S(1)} %get-tuple-element.80), channel_id=1, source_target_pairs={{0,1},{1,2},{2,3},{3,0},{4,5},{5,6},{6,7},{7,4},{8,9},{9,10},{10,1... | collective-permute-start | bytes 393224 | tf_op jit(solution)/shard_map/strips_2/ppermute | solution.py:399
  90.8 1.7 %collective-permute-start.21 = (bf16[64,1024]{1,0:T(8,128)(2,1)S(1)}, bf16[64,1024]{1,0:T(8,128)(2,1)S(1)}, u32[]{:S(2)}, u32[]{:S(2)}) collective-permute-start(bf16[64,1024]{1,0:T(8,128)(2,1)S(1)} %get-tuple-element.81), channel_id=1, source_target_pairs={{0,2},{1,3},{2,0},{3,1},{4,6},{5,7},{6,4},{7,5},{8,10},{9,11},{10,... | collective-permute-start | bytes 393224 | tf_op jit(solution)/shard_map/strips_2/ppermute | solution.py:399
  93.9 2.5 %collective-permute-done.23.refs_1_.refs_4_ = bf16[64,4096]{1,0:T(8,128)(2,1)S(1)} collective-permute-done((bf16[64,4096]{1,0:T(8,128)(2,1)S(1)}, bf16[64,4096]{1,0:T(8,128)(2,1)S(1)}, u32[]{:S(2)}, u32[]{:S(2)}) %collective-permute-start.23) | collective-permute-done | bytes 524320 | tf_op jit(solution)/shard_map/date_1_0/ppermute | solution.py:405
  96.4 3.8 %collective-permute-start.25 = (bf16[64,1024]{1,0:T(8,128)(2,1)S(1)}, bf16[64,1024]{1,0:T(8,128)(2,1)S(1)}, u32[]{:S(2)}, u32[]{:S(2)}) collective-permute-start(bf16[64,1024]{1,0:T(8,128)(2,1)S(1)} %get-tuple-element.87), channel_id=1, source_target_pairs={{0,1},{1,2},{2,3},{3,0},{4,5},{5,6},{6,7},{7,4},{8,9},{9,10},{10,1... | collective-permute-start | bytes 393224 | tf_op jit(solution)/shard_map/strips_3/ppermute | solution.py:399
  100.2 2.5 %collective-permute-start.24 = (bf16[64,4096]{1,0:T(8,128)(2,1)S(1)}, bf16[64,4096]{1,0:T(8,128)(2,1)S(1)}, u32[]{:S(2)}, u32[]{:S(2)}) collective-permute-start(bf16[64,4096]{1,0:T(8,128)(2,1)S(1)} %collective-permute-done.23.refs_1_.refs_4_), channel_id=1, source_target_pairs={{4,0},{8,4},{12,8},{16,12},{20,16},{24,20},{28,24},{0,28},{5,1},{9... | collective-permute-start | bytes 1572872 | tf_op jit(solution)/shard_map/date_1_1/ppermute | solution.py:405
  102.7 6.0 %coherence.4 = (bf16[2,256,2048]{2,1,0:T(8,128)(2,1)}, bf16[2,2,256,2048]{3,2,1,0:T(8,128)(2,1)}, f32[8,128]{1,0:T(8,128)S(1)}) custom-call(bf16[80,4096]{1,0:T(8,128)(2,1)S(1)} %join_strips.4._before.refs_0_.refs_3_, bf16[80,4096]{1,0:T(8,128)(2,1)S(1)} %collective-permute-done.18.refs_1_.refs_4_, bf16[80,4096]{1,0:T(8,128)(2,1)S(1)} %collective-permute-done.19.refs_2_.refs_5_), custom_call_target="tpu_custom_call" | custom-call | flops 6000000000 | tf_op jit(solution)/shard_map/coherence/pallas_call | solution.py:518
  108.7 2.6 %collective-permute-start.27 = (bf16[64,1024]{1,0:T(8,128)(2,1)S(1)}, bf16[64,1024]{1,0:T(8,128)(2,1)S(1)}, u32[]{:S(2)}, u32[]{:S(2)}) collective-permute-start(bf16[64,1024]{1,0:T(8,128)(2,1)S(1)} %get-tuple-element.89), channel_id=1, source_target_pairs={{0,3},{1,0},{2,1},{3,2},{4,7},{5,4},{6,5},{7,6},{8,11},{9,8},{10,9... | collective-permute-start | bytes 393224 | tf_op jit(solution)/shard_map/strips_3/ppermute | solution.py:399
  111.5 6.0 %coherence.5 = (bf16[2,256,2048]{2,1,0:T(8,128)(2,1)}, bf16[2,2,256,2048]{3,2,1,0:T(8,128)(2,1)}, f32[8,128]{1,0:T(8,128)S(1)}) custom-call(bf16[64,4096]{1,0:T(8,128)(2,1)S(1)} %join_strips.5._before.refs_0_.refs_3_, bf16[64,4096]{1,0:T(8,128)(2,1)S(1)} %collective-permute-done.23.refs_1_.refs_4_, ...), custom_call_target="tpu_custom_call", output_to_operand_aliasing={{0}: (6, {}), {1}: (7, {})} | custom-call | flops 6000000000 | tf_op jit(solution)/shard_map/coherence/pallas_call | solution.py:518
  117.5 1.1 collective-permute-start.28
  118.6 2.3 %collective-permute-start.31 = (bf16[64,4096]{1,0:T(8,128)(2,1)S(1)}, bf16[64,4096]{1,0:T(8,128)(2,1)S(1)}, u32[]{:S(2)}, u32[]{:S(2)}) collective-permute-start(bf16[64,4096]{1,0:T(8,128)(2,1)S(1)} %collective-permute-done.30.refs_1_.refs_4_), channel_id=1, source_target_pairs={{4,0},{8,4},{12,8},{16,12},{20,16},{24,20},{28,24},{0,28},{5,1},{9... | collective-permute-start | bytes 1572872 | tf_op jit(solution)/shard_map/date_2_1/ppermute | solution.py:405
  120.9 4.4 %collective-permute-done.28.refs_1_ = bf16[64,4096]{1,0:T(8,128)(2,1)S(1)} collective-permute-done((bf16[64,4096]{1,0:T(8,128)(2,1)S(1)}, bf16[64,4096]{1,0:T(8,128)(2,1)S(1)}, u32[]{:S(2)}, u32[]{:S(2)}) %collective-permute-start.28) | collective-permute-done | bytes 524320 | tf_op jit(solution)/shard_map/date_3_0/ppermute | solution.py:405
  125.3 2.8 %collective-permute-start.29 = (bf16[64,4096]{1,0:T(8,128)(2,1)S(1)}, bf16[64,4096]{1,0:T(8,128)(2,1)S(1)}, u32[]{:S(2)}, u32[]{:S(2)}) collective-permute-start(bf16[64,4096]{1,0:T(8,128)(2,1)S(1)} %collective-permute-done.28.refs_1_), channel_id=1, source_target_pairs={{4,0},{8,4},{12,8},{16,12},{20,16},{24,20},{28,24},{0,28},{5,1},{9... | collective-permute-start | bytes 1572872 | tf_op jit(solution)/shard_map/date_3_1/ppermute | solution.py:405
  128.1 2.8 %collective-permute-done.31.refs_2_.refs_5_ = bf16[64,4096]{1,0:T(8,128)(2,1)S(1)} collective-permute-done((bf16[64,4096]{1,0:T(8,128)(2,1)S(1)}, bf16[64,4096]{1,0:T(8,128)(2,1)S(1)}, u32[]{:S(2)}, u32[]{:S(2)}) %collective-permute-start.31) | collective-permute-done | bytes 524320 | tf_op jit(solution)/shard_map/date_2_1/ppermute | solution.py:405
  131.0 6.0 %coherence.6 = (bf16[2,256,2048]{2,1,0:T(8,128)(2,1)}, bf16[2,2,256,2048]{3,2,1,0:T(8,128)(2,1)}, f32[8,128]{1,0:T(8,128)}) custom-call(bf16[64,4096]{1,0:T(8,128)(2,1)S(1)} %join_strips.6._before.refs_0_.refs_3_, bf16[64,4096]{1,0:T(8,128)(2,1)S(1)} %collective-permute-done.30.refs_1_.refs_4_, ...), custom_call_target="tpu_custom_call", output_to_operand_aliasing={{0}: (6, {}), {1}: (7, {})} | custom-call | flops 6000000000 | tf_op jit(solution)/shard_map/coherence/pallas_call | solution.py:518
  137.0 6.0 %coherence.7 = (bf16[2,256,2048]{2,1,0:T(8,128)(2,1)}, bf16[2,2,256,2048]{3,2,1,0:T(8,128)(2,1)}, f32[8,128]{1,0:T(8,128)}) custom-call(bf16[64,4096]{1,0:T(8,128)(2,1)S(1)} %join_strips.7.refs_0_, bf16[64,4096]{1,0:T(8,128)(2,1)S(1)} %collective-permute-done.28.refs_1_, ...), custom_call_target="tpu_custom_call", output_to_operand_aliasing={{0}: (6, {}), {1}: (7, {})} | custom-call | flops 6000000000 | tf_op jit(solution)/shard_map/coherence/pallas_call | solution.py:518
  (43 shorter events, 5.5 us)
Async XLA Ops:
  1.3 1.6 %copy-start = (bf16[1,2,256,2048]{3,2,1,0:T(8,128)(2,1)S(1)}, bf16[1,2,256,2048]{3,2,1,0:T(8,128)(2,1)}, u32[]{:S(2)}) copy-start(bf16[1,2,256,2048]{3,2,1,0:T(8,128)(2,1)} %param.5) | copy-start | bytes 6291460
  4.6 15.4 %collective-permute-start = (bf16[256,256]{1,0:T(8,128)(2,1)S(1)}, bf16[256,256]{1,0:T(8,128)(2,1)S(1)}, u32[]{:S(2)}, u32[]{:S(2)}) collective-permute-start(bf16[256,256]{1,0:T(8,128)(2,1)S(1)} %get-tuple-element.58), channel_id=1, source_target_pairs={{0,1},{1,2},{2,3},{3,0},{4,5},{5,6},{6,7},{7,4},{8,9},{9,10},{10,1... | collective-permute-start | bytes 393224 | tf_op jit(solution)/shard_map/columns_0/ppermute | solution.py:399
  7.7 15.2 %collective-permute-start.1 = (bf16[256,256]{1,0:T(8,128)(2,1)S(1)}, bf16[256,256]{1,0:T(8,128)(2,1)S(1)}, u32[]{:S(2)}, u32[]{:S(2)}) collective-permute-start(bf16[256,256]{1,0:T(8,128)(2,1)S(1)} %get-tuple-element.59), channel_id=1, source_target_pairs={{0,2},{1,3},{2,0},{3,1},{4,6},{5,7},{6,4},{7,5},{8,10},{9,11},{10,... | collective-permute-start | bytes 393224 | tf_op jit(solution)/shard_map/columns_0/ppermute | solution.py:399
  10.3 24.1 %collective-permute-start.2 = (bf16[256,256]{1,0:T(8,128)(2,1)S(1)}, bf16[256,256]{1,0:T(8,128)(2,1)S(1)}, u32[]{:S(2)}, u32[]{:S(2)}) collective-permute-start(bf16[256,256]{1,0:T(8,128)(2,1)S(1)} %get-tuple-element.60), channel_id=1, source_target_pairs={{0,3},{1,0},{2,1},{3,2},{4,7},{5,4},{6,5},{7,6},{8,11},{9,8},{10,9... | collective-permute-start | bytes 393224 | tf_op jit(solution)/shard_map/columns_0/ppermute | solution.py:399
  13.3 25.1 %collective-permute-start.3 = (bf16[256,256]{1,0:T(8,128)(2,1)S(1)}, bf16[256,256]{1,0:T(8,128)(2,1)S(1)}, u32[]{:S(2)}, u32[]{:S(2)}) collective-permute-start(bf16[256,256]{1,0:T(8,128)(2,1)S(1)} %get-tuple-element.61), channel_id=1, source_target_pairs={{0,1},{1,2},{2,3},{3,0},{4,5},{5,6},{6,7},{7,4},{8,9},{9,10},{10,1... | collective-permute-start | bytes 393224 | tf_op jit(solution)/shard_map/columns_1/ppermute | solution.py:399
  14.0 25.3 %collective-permute-start.4 = (bf16[256,256]{1,0:T(8,128)(2,1)S(1)}, bf16[256,256]{1,0:T(8,128)(2,1)S(1)}, u32[]{:S(2)}, u32[]{:S(2)}) collective-permute-start(bf16[256,256]{1,0:T(8,128)(2,1)S(1)} %get-tuple-element.62), channel_id=1, source_target_pairs={{0,2},{1,3},{2,0},{3,1},{4,6},{5,7},{6,4},{7,5},{8,10},{9,11},{10,... | collective-permute-start | bytes 393224 | tf_op jit(solution)/shard_map/columns_1/ppermute | solution.py:399
  18.4 7.3 %copy-start.1 = (f32[512]{0:T(512)S(1)}, f32[512]{0:T(512)}, u32[]{:S(2)}) copy-start(f32[512]{0:T(512)} %param.7) | copy-start | bytes 6148
  20.1 21.3 %collective-permute-start.5 = (bf16[256,256]{1,0:T(8,128)(2,1)S(1)}, bf16[256,256]{1,0:T(8,128)(2,1)S(1)}, u32[]{:S(2)}, u32[]{:S(2)}) collective-permute-start(bf16[256,256]{1,0:T(8,128)(2,1)S(1)} %get-tuple-element.63), channel_id=1, source_target_pairs={{0,3},{1,0},{2,1},{3,2},{4,7},{5,4},{6,5},{7,6},{8,11},{9,8},{10,9... | collective-permute-start | bytes 393224 | tf_op jit(solution)/shard_map/columns_1/ppermute | solution.py:399
  22.9 18.5 %collective-permute-start.6 = (bf16[256,256]{1,0:T(8,128)(2,1)S(1)}, bf16[256,256]{1,0:T(8,128)(2,1)S(1)}, u32[]{:S(2)}, u32[]{:S(2)}) collective-permute-start(bf16[256,256]{1,0:T(8,128)(2,1)S(1)} %get-tuple-element.64), channel_id=1, source_target_pairs={{0,1},{1,2},{2,3},{3,0},{4,5},{5,6},{6,7},{7,4},{8,9},{9,10},{10,1... | collective-permute-start | bytes 393224 | tf_op jit(solution)/shard_map/columns_2/ppermute | solution.py:399
  34.4 14.9 %collective-permute-start.7 = (bf16[256,256]{1,0:T(8,128)(2,1)S(1)}, bf16[256,256]{1,0:T(8,128)(2,1)S(1)}, u32[]{:S(2)}, u32[]{:S(2)}) collective-permute-start(bf16[256,256]{1,0:T(8,128)(2,1)S(1)} %get-tuple-element.65), channel_id=1, source_target_pairs={{0,2},{1,3},{2,0},{3,1},{4,6},{5,7},{6,4},{7,5},{8,10},{9,11},{10,... | collective-permute-start | bytes 393224 | tf_op jit(solution)/shard_map/columns_2/ppermute | solution.py:399
  38.4 10.9 %collective-permute-start.8 = (bf16[256,256]{1,0:T(8,128)(2,1)S(1)}, bf16[256,256]{1,0:T(8,128)(2,1)S(1)}, u32[]{:S(2)}, u32[]{:S(2)}) collective-permute-start(bf16[256,256]{1,0:T(8,128)(2,1)S(1)} %get-tuple-element.66), channel_id=1, source_target_pairs={{0,3},{1,0},{2,1},{3,2},{4,7},{5,4},{6,5},{7,6},{8,11},{9,8},{10,9... | collective-permute-start | bytes 393224 | tf_op jit(solution)/shard_map/columns_2/ppermute | solution.py:399
  39.3 10.9 %collective-permute-start.9 = (bf16[256,256]{1,0:T(8,128)(2,1)S(1)}, bf16[256,256]{1,0:T(8,128)(2,1)S(1)}, u32[]{:S(2)}, u32[]{:S(2)}) collective-permute-start(bf16[256,256]{1,0:T(8,128)(2,1)S(1)} %get-tuple-element.67), channel_id=1, source_target_pairs={{0,1},{1,2},{2,3},{3,0},{4,5},{5,6},{6,7},{7,4},{8,9},{9,10},{10,1... | collective-permute-start | bytes 393224 | tf_op jit(solution)/shard_map/columns_3/ppermute | solution.py:399
  41.4 12.7 %collective-permute-start.10 = (bf16[256,256]{1,0:T(8,128)(2,1)S(1)}, bf16[256,256]{1,0:T(8,128)(2,1)S(1)}, u32[]{:S(2)}, u32[]{:S(2)}) collective-permute-start(bf16[256,256]{1,0:T(8,128)(2,1)S(1)} %get-tuple-element.68), channel_id=1, source_target_pairs={{0,2},{1,3},{2,0},{3,1},{4,6},{5,7},{6,4},{7,5},{8,10},{9,11},{10,... | collective-permute-start | bytes 393224 | tf_op jit(solution)/shard_map/columns_3/ppermute | solution.py:399
  41.4 12.6 %collective-permute-start.11 = (bf16[256,256]{1,0:T(8,128)(2,1)S(1)}, bf16[256,256]{1,0:T(8,128)(2,1)S(1)}, u32[]{:S(2)}, u32[]{:S(2)}) collective-permute-start(bf16[256,256]{1,0:T(8,128)(2,1)S(1)} %get-tuple-element.69), channel_id=1, source_target_pairs={{0,3},{1,0},{2,1},{3,2},{4,7},{5,4},{6,5},{7,6},{8,11},{9,8},{10,9... | collective-permute-start | bytes 393224 | tf_op jit(solution)/shard_map/columns_3/ppermute | solution.py:399
  55.8 9.1 %collective-permute-start.12 = (bf16[80,1024]{1,0:T(8,128)(2,1)S(1)}, bf16[80,1024]{1,0:T(8,128)(2,1)S(1)}, u32[]{:S(2)}, u32[]{:S(2)}) collective-permute-start(bf16[80,1024]{1,0:T(8,128)(2,1)S(1)} %get-tuple-element.71), channel_id=1, source_target_pairs={{0,1},{1,2},{2,3},{3,0},{4,5},{5,6},{6,7},{7,4},{8,9},{9,10},{10,1... | collective-permute-start | bytes 491528 | tf_op jit(solution)/shard_map/strips_0/ppermute | solution.py:399
  57.8 11.4 %collective-permute-start.13 = (bf16[80,1024]{1,0:T(8,128)(2,1)S(1)}, bf16[80,1024]{1,0:T(8,128)(2,1)S(1)}, u32[]{:S(2)}, u32[]{:S(2)}) collective-permute-start(bf16[80,1024]{1,0:T(8,128)(2,1)S(1)} %get-tuple-element.72), channel_id=1, source_target_pairs={{0,2},{1,3},{2,0},{3,1},{4,6},{5,7},{6,4},{7,5},{8,10},{9,11},{10,... | collective-permute-start | bytes 491528 | tf_op jit(solution)/shard_map/strips_0/ppermute | solution.py:399
  59.5 9.7 %collective-permute-start.14 = (bf16[80,1024]{1,0:T(8,128)(2,1)S(1)}, bf16[80,1024]{1,0:T(8,128)(2,1)S(1)}, u32[]{:S(2)}, u32[]{:S(2)}) collective-permute-start(bf16[80,1024]{1,0:T(8,128)(2,1)S(1)} %get-tuple-element.73), channel_id=1, source_target_pairs={{0,3},{1,0},{2,1},{3,2},{4,7},{5,4},{6,5},{7,6},{8,11},{9,8},{10,9... | collective-permute-start | bytes 491528 | tf_op jit(solution)/shard_map/strips_0/ppermute | solution.py:399
  69.3 10.3 %collective-permute-start.18 = (bf16[80,4096]{1,0:T(8,128)(2,1)S(1)}, bf16[80,4096]{1,0:T(8,128)(2,1)S(1)}, u32[]{:S(2)}, u32[]{:S(2)}) collective-permute-start(bf16[80,4096]{1,0:T(8,128)(2,1)S(1)} %join_strips.4._before.refs_0_.refs_3_), channel_id=1, source_target_pairs={{4,0},{8,4},{12,8},{16,12},{20,16},{24,20},{28,24},{0,28},{5,1},{9... | collective-permute-start | bytes 1966088 | tf_op jit(solution)/shard_map/date_0_0/ppermute | solution.py:405
  72.2 10.5 %collective-permute-start.15 = (bf16[64,1024]{1,0:T(8,128)(2,1)S(1)}, bf16[64,1024]{1,0:T(8,128)(2,1)S(1)}, u32[]{:S(2)}, u32[]{:S(2)}) collective-permute-start(bf16[64,1024]{1,0:T(8,128)(2,1)S(1)} %get-tuple-element.75), channel_id=1, source_target_pairs={{0,1},{1,2},{2,3},{3,0},{4,5},{5,6},{6,7},{7,4},{8,9},{9,10},{10,1... | collective-permute-start | bytes 393224 | tf_op jit(solution)/shard_map/strips_1/ppermute | solution.py:399
  76.3 8.4 %collective-permute-start.16 = (bf16[64,1024]{1,0:T(8,128)(2,1)S(1)}, bf16[64,1024]{1,0:T(8,128)(2,1)S(1)}, u32[]{:S(2)}, u32[]{:S(2)}) collective-permute-start(bf16[64,1024]{1,0:T(8,128)(2,1)S(1)} %get-tuple-element.76), channel_id=1, source_target_pairs={{0,2},{1,3},{2,0},{3,1},{4,6},{5,7},{6,4},{7,5},{8,10},{9,11},{10,... | collective-permute-start | bytes 393224 | tf_op jit(solution)/shard_map/strips_1/ppermute | solution.py:399
  76.3 8.4 %collective-permute-start.17 = (bf16[64,1024]{1,0:T(8,128)(2,1)S(1)}, bf16[64,1024]{1,0:T(8,128)(2,1)S(1)}, u32[]{:S(2)}, u32[]{:S(2)}) collective-permute-start(bf16[64,1024]{1,0:T(8,128)(2,1)S(1)} %get-tuple-element.77), channel_id=1, source_target_pairs={{0,3},{1,0},{2,1},{3,2},{4,7},{5,4},{6,5},{7,6},{8,11},{9,8},{10,9... | collective-permute-start | bytes 393224 | tf_op jit(solution)/shard_map/strips_1/ppermute | solution.py:399
  79.6 20.6 %collective-permute-start.19 = (bf16[80,4096]{1,0:T(8,128)(2,1)S(1)}, bf16[80,4096]{1,0:T(8,128)(2,1)S(1)}, u32[]{:S(2)}, u32[]{:S(2)}) collective-permute-start(bf16[80,4096]{1,0:T(8,128)(2,1)S(1)} %collective-permute-done.18.refs_1_.refs_4_), channel_id=1, source_target_pairs={{4,0},{8,4},{12,8},{16,12},{20,16},{24,20},{28,24},{0,28},{5,1},{9... | collective-permute-start | bytes 1966088 | tf_op jit(solution)/shard_map/date_0_1/ppermute | solution.py:405
  84.8 11.6 %collective-permute-start.23 = (bf16[64,4096]{1,0:T(8,128)(2,1)S(1)}, bf16[64,4096]{1,0:T(8,128)(2,1)S(1)}, u32[]{:S(2)}, u32[]{:S(2)}) collective-permute-start(bf16[64,4096]{1,0:T(8,128)(2,1)S(1)} %join_strips.5._before.refs_0_.refs_3_), channel_id=1, source_target_pairs={{4,0},{8,4},{12,8},{16,12},{20,16},{24,20},{28,24},{0,28},{5,1},{9... | collective-permute-start | bytes 1572872 | tf_op jit(solution)/shard_map/date_1_0/ppermute | solution.py:405
  87.3 21.3 %collective-permute-start.20 = (bf16[64,1024]{1,0:T(8,128)(2,1)S(1)}, bf16[64,1024]{1,0:T(8,128)(2,1)S(1)}, u32[]{:S(2)}, u32[]{:S(2)}) collective-permute-start(bf16[64,1024]{1,0:T(8,128)(2,1)S(1)} %get-tuple-element.80), channel_id=1, source_target_pairs={{0,1},{1,2},{2,3},{3,0},{4,5},{5,6},{6,7},{7,4},{8,9},{9,10},{10,1... | collective-permute-start | bytes 393224 | tf_op jit(solution)/shard_map/strips_2/ppermute | solution.py:399
  90.8 17.9 %collective-permute-start.21 = (bf16[64,1024]{1,0:T(8,128)(2,1)S(1)}, bf16[64,1024]{1,0:T(8,128)(2,1)S(1)}, u32[]{:S(2)}, u32[]{:S(2)}) collective-permute-start(bf16[64,1024]{1,0:T(8,128)(2,1)S(1)} %get-tuple-element.81), channel_id=1, source_target_pairs={{0,2},{1,3},{2,0},{3,1},{4,6},{5,7},{6,4},{7,5},{8,10},{9,11},{10,... | collective-permute-start | bytes 393224 | tf_op jit(solution)/shard_map/strips_2/ppermute | solution.py:399
  92.5 18.8 %collective-permute-start.22 = (bf16[64,1024]{1,0:T(8,128)(2,1)S(1)}, bf16[64,1024]{1,0:T(8,128)(2,1)S(1)}, u32[]{:S(2)}, u32[]{:S(2)}) collective-permute-start(bf16[64,1024]{1,0:T(8,128)(2,1)S(1)} %get-tuple-element.82), channel_id=1, source_target_pairs={{0,3},{1,0},{2,1},{3,2},{4,7},{5,4},{6,5},{7,6},{8,11},{9,8},{10,9... | collective-permute-start | bytes 393224 | tf_op jit(solution)/shard_map/strips_2/ppermute | solution.py:399
  96.4 21.0 %collective-permute-start.25 = (bf16[64,1024]{1,0:T(8,128)(2,1)S(1)}, bf16[64,1024]{1,0:T(8,128)(2,1)S(1)}, u32[]{:S(2)}, u32[]{:S(2)}) collective-permute-start(bf16[64,1024]{1,0:T(8,128)(2,1)S(1)} %get-tuple-element.87), channel_id=1, source_target_pairs={{0,1},{1,2},{2,3},{3,0},{4,5},{5,6},{6,7},{7,4},{8,9},{9,10},{10,1... | collective-permute-start | bytes 393224 | tf_op jit(solution)/shard_map/strips_3/ppermute | solution.py:399
  100.2 11.3 %collective-permute-start.24 = (bf16[64,4096]{1,0:T(8,128)(2,1)S(1)}, bf16[64,4096]{1,0:T(8,128)(2,1)S(1)}, u32[]{:S(2)}, u32[]{:S(2)}) collective-permute-start(bf16[64,4096]{1,0:T(8,128)(2,1)S(1)} %collective-permute-done.23.refs_1_.refs_4_), channel_id=1, source_target_pairs={{4,0},{8,4},{12,8},{16,12},{20,16},{24,20},{28,24},{0,28},{5,1},{9... | collective-permute-start | bytes 1572872 | tf_op jit(solution)/shard_map/date_1_1/ppermute | solution.py:405
  108.7 8.8 %collective-permute-start.26 = (bf16[64,1024]{1,0:T(8,128)(2,1)S(1)}, bf16[64,1024]{1,0:T(8,128)(2,1)S(1)}, u32[]{:S(2)}, u32[]{:S(2)}) collective-permute-start(bf16[64,1024]{1,0:T(8,128)(2,1)S(1)} %get-tuple-element.88), channel_id=1, source_target_pairs={{0,2},{1,3},{2,0},{3,1},{4,6},{5,7},{6,4},{7,5},{8,10},{9,11},{10,... | collective-permute-start | bytes 393224 | tf_op jit(solution)/shard_map/strips_3/ppermute | solution.py:399
  108.7 8.8 %collective-permute-start.27 = (bf16[64,1024]{1,0:T(8,128)(2,1)S(1)}, bf16[64,1024]{1,0:T(8,128)(2,1)S(1)}, u32[]{:S(2)}, u32[]{:S(2)}) collective-permute-start(bf16[64,1024]{1,0:T(8,128)(2,1)S(1)} %get-tuple-element.89), channel_id=1, source_target_pairs={{0,3},{1,0},{2,1},{3,2},{4,7},{5,4},{6,5},{7,6},{8,11},{9,8},{10,9... | collective-permute-start | bytes 393224 | tf_op jit(solution)/shard_map/strips_3/ppermute | solution.py:399
  111.4 7.3 %collective-permute-start.30 = (bf16[64,4096]{1,0:T(8,128)(2,1)S(1)}, bf16[64,4096]{1,0:T(8,128)(2,1)S(1)}, u32[]{:S(2)}, u32[]{:S(2)}) collective-permute-start(bf16[64,4096]{1,0:T(8,128)(2,1)S(1)} %join_strips.6._before.refs_0_.refs_3_), channel_id=1, source_target_pairs={{4,0},{8,4},{12,8},{16,12},{20,16},{24,20},{28,24},{0,28},{5,1},{9... | collective-permute-start | bytes 1572872 | tf_op jit(solution)/shard_map/date_2_0/ppermute | solution.py:405
  117.5 7.8 %collective-permute-start.28 = (bf16[64,4096]{1,0:T(8,128)(2,1)S(1)}, bf16[64,4096]{1,0:T(8,128)(2,1)S(1)}, u32[]{:S(2)}, u32[]{:S(2)}) collective-permute-start(bf16[64,4096]{1,0:T(8,128)(2,1)S(1)} %join_strips.7.refs_0_), channel_id=1, source_target_pairs={{4,0},{8,4},{12,8},{16,12},{20,16},{24,20},{28,24},{0,28},{5,1},{9... | collective-permute-start | bytes 1572872 | tf_op jit(solution)/shard_map/date_3_0/ppermute | solution.py:405
  118.6 12.3 %collective-permute-start.31 = (bf16[64,4096]{1,0:T(8,128)(2,1)S(1)}, bf16[64,4096]{1,0:T(8,128)(2,1)S(1)}, u32[]{:S(2)}, u32[]{:S(2)}) collective-permute-start(bf16[64,4096]{1,0:T(8,128)(2,1)S(1)} %collective-permute-done.30.refs_1_.refs_4_), channel_id=1, source_target_pairs={{4,0},{8,4},{12,8},{16,12},{20,16},{24,20},{28,24},{0,28},{5,1},{9... | collective-permute-start | bytes 1572872 | tf_op jit(solution)/shard_map/date_2_1/ppermute | solution.py:405
  125.3 11.6 %collective-permute-start.29 = (bf16[64,4096]{1,0:T(8,128)(2,1)S(1)}, bf16[64,4096]{1,0:T(8,128)(2,1)S(1)}, u32[]{:S(2)}, u32[]{:S(2)}) collective-permute-start(bf16[64,4096]{1,0:T(8,128)(2,1)S(1)} %collective-permute-done.28.refs_1_), channel_id=1, source_target_pairs={{4,0},{8,4},{12,8},{16,12},{20,16},{24,20},{28,24},{0,28},{5,1},{9... | collective-permute-start | bytes 1572872 | tf_op jit(solution)/shard_map/date_3_1/ppermute | solution.py:405

commit v3 on v2

--- a/solution.py
+++ b/solution.py
@@ -15,7 +15,14 @@
 LANES = 128
 PACK = 16
 RIM = 8
-LINE_STEP = 64
+COLUMN_PARTS = (1, 1, 1, 1)
+LINE_PARTS = (5, 5, 4, 2)
+JOIN_COST = 0.5
+COH_COST = 5.0
+HOP_WAITS = False
+LATER = 0
+LAG = 2
+PACE = 1.0
 
 two_pi = 2.0 * math.pi
 epsilon = 1e-06
@@ -28,7 +35,7 @@
 
 
 def cost(micros):
-    return pl.CostEstimate(flops=int(micros * 1e9), bytes_accessed=0, transcendentals=0)
+    return pl.CostEstimate(flops=int(micros * PACE * 1e9), bytes_accessed=0, transcendentals=0)
 
 
 def vmem():
@@ -87,38 +94,40 @@
             )
 
 
-def range_blocks(me_ref, echo_ref, table, outs, chunk, devices, pulse_len):
+def range_blocks(me_ref, echo_ref, table, outs, offset, devices, pulse_len):
     lines = echo_ref.shape[0] // 2
     samples = echo_ref.shape[1]
     width = outs[0].shape[1] // 2
     lane_blocks = samples // LANES
-    window_blocks = (pulse_len + width) // LANES
+    window_blocks = pulse_len // LANES + 1
     for step in range(devices):
         target = lax.rem(me_ref[0] + step, devices)
-        first = target * (samples // devices // LANES) + chunk * (width // LANES)
-        pieces = [
-            echo_ref[
-                :,
-                pl.ds(pl.multiple_of(lax.rem(first + j, lane_blocks) * LANES, LANES), LANES),
+        for part in range(width // LANES):
+            first = target * (lane_blocks // devices) + offset // LANES + part
+            pieces = [
+                echo_ref[
+                    :,
+                    pl.ds(pl.multiple_of(lax.rem(first + j, lane_blocks) * LANES, LANES), LANES),
+                ]
+                for j in range(window_blocks)
             ]
-            for j in range(window_blocks)
-        ]
-        window = jnp.concatenate(pieces, axis=1)
-        product = jnp.dot(window, table, preferred_element_type=F32)
-        out = outs[step]
-        out[:, :width] = (product[:lines, :width] - product[lines:, width:]).astype(BF16)
-        out[:, width:] = (product[lines:, :width] + product[:lines, width:]).astype(BF16)
+            window = jnp.concatenate(pieces, axis=1)
+            product = jnp.dot(window, table, preferred_element_type=F32)
+            real = product[:lines, :LANES] - product[lines:, LANES:]
+            imag = product[lines:, :LANES] + product[:lines, LANES:]
+            left = part * LANES
+            outs[step][:, left : left + LANES] = real.astype(BF16)
+            outs[step][:, width + left : width + left + LANES] = imag.astype(BF16)
 
 
 def first_range_kernel(devices, pulse_len, me_ref, rate_ref, echo_ref, table_ref, *rest):
     outs, base_ref = rest[:-1], rest[-1]
-    width = table_ref.shape[1] // 2
-    build_chirp(rate_ref, table_ref, base_ref, pulse_len, width)
+    build_chirp(rate_ref, table_ref, base_ref, pulse_len, LANES)
     range_blocks(me_ref, echo_ref, table_ref[...], outs, 0, devices, pulse_len)
 
 
-def next_range_kernel(devices, chunk, pulse_len, me_ref, echo_ref, table_ref, _, *outs):
-    range_blocks(me_ref, echo_ref, table_ref[...], outs, chunk, devices, pulse_len)
+def next_range_kernel(devices, offset, pulse_len, me_ref, echo_ref, table_ref, _, *outs):
+    range_blocks(me_ref, echo_ref, table_ref[...], outs, offset, devices, pulse_len)
 
 
 def tables_kernel(
@@ -210,7 +219,7 @@
     lax.fori_loop(0, half // RIM + 1, filter_rows, 0)
 
 
-def forward_kernel(devices, chunk, me_ref, dft_ref, coef_ref, filt_ref, _, *rest):
+def forward_kernel(devices, offset, me_ref, dft_ref, coef_ref, filt_ref, _, *rest):
     blocks, out_ref, joined = rest[:devices], rest[devices], rest[devices + 1]
     size = dft_ref.shape[0]
     half = size // 2
@@ -236,7 +245,7 @@
         u_im = coefs[0] * even_im + coefs[1] * odd_im
         v_re = coefs[2] * odd_re - coefs[1] * even_re
         v_im = coefs[2] * odd_im - coefs[1] * even_im
-        cols = slice(chunk * width, (chunk + 1) * width)
+        cols = slice(offset, offset + width)
         filt_re, filt_im = filt_ref[0, rows, cols], filt_ref[1, rows, cols]
         out_ref[rows, :width] = (filt_re * u_re - filt_im * u_im).astype(BF16)
         out_ref[rows, width:] = (filt_re * u_im + filt_im * u_re).astype(BF16)
@@ -249,27 +258,28 @@
         out_ref[rows, width:] = (filt_re * v_im + filt_im * v_re).astype(BF16)
 
 
-def inverse_kernel(devices, line_count, first_row, rows, chunk_count, me_ref, inv_ref, _, *rest):
-    spectra, outs = rest[:chunk_count], rest[chunk_count:]
-    pieces = []
-    for step in range(devices):
-        target = lax.rem(me_ref[0] + step, devices)
-        start = pl.multiple_of(target * line_count + first_row, PACK)
-        pieces.append(inv_ref[pl.ds(start, rows), :])
-    left = jnp.concatenate(pieces, axis=0)
-    total = outs[0].shape[1] // 2
-    width = total // chunk_count
-    for chunk in range(chunk_count):
-        product = jnp.dot(left, spectra[chunk][...], preferred_element_type=F32).astype(BF16)
+def inverse_kernel(devices, line_count, pieces, widths, me_ref, inv_ref, _, *rest):
+    spectra, outs = rest[: len(widths)], rest[len(widths) :]
+    total = sum(widths)
+    for piece, (first_row, rows) in enumerate(pieces):
+        left = []
         for step in range(devices):
-            part = product[step * rows : (step + 1) * rows]
-            first = chunk * width
-            outs[step][:, first : first + width] = part[:, :width]
-            first += total
-            outs[step][:, first : first + width] = part[:, width:]
-
-
-def join_kernel(devices, has_first, has_last, me_ref, _before, _passed, *rest):
+            target = lax.rem(me_ref[0] + step, devices)
+            start = pl.multiple_of(target * line_count + first_row, PACK)
+            left.append(inv_ref[pl.ds(start, rows), :])
+        left = jnp.concatenate(left, axis=0)
+        offset = 0
+        for spectrum, width in zip(spectra, widths):
+            product = jnp.dot(left, spectrum[...], preferred_element_type=F32).astype(BF16)
+            for step in range(devices):
+                part = product[step * rows : (step + 1) * rows]
+                out = outs[piece * devices + step]
+                out[:, offset : offset + width] = part[:, :width]
+                out[:, total + offset : total + offset + width] = part[:, width:]
+            offset += width
+
+
+def join_kernel(devices, has_first, has_last, me_ref, _before, _ahead, _ended, *rest):
     blocks, out_ref = rest[:devices], rest[devices]
     rows, width = blocks[0].shape[0], blocks[0].shape[1] // 2
     samples = out_ref.shape[1] // 2
@@ -298,7 +308,7 @@
             clear(rows - PACK, PACK - RIM, PACK)
 
 
-def coherence_kernel(has_before, *refs):
+def coherence_kernel(first_line, has_before, _later, *refs):
     dates = SPAN + 1
     now = refs[:dates]
     position = dates
@@ -306,54 +316,46 @@
     if has_before:
         before = refs[position : position + dates]
         position += dates + 2
-    image_ref, result_ref, token_ref, sums_ref = refs[position : position + 4]
+    image_out, result_out, token_ref, image_ref, result_ref, sums_ref, sems = refs[position:]
     token_ref[...] = jnp.zeros(token_ref.shape, F32)
     lines = image_ref.shape[1]
     samples = image_ref.shape[2]
     window = lines + 2 * RIM
     half_az, half_rg = WIN_AZ // 2, WIN_RG // 2
     block = min(samples, 256)
+    group = min(samples, 512)
     terms = 1 + 3 * SPAN
     out_id = lax.broadcasted_iota(jnp.int32, (lines, window), 0)
     in_id = lax.broadcasted_iota(jnp.int32, (lines, window), 1) - RIM
     down = jnp.where(jnp.abs(in_id - out_id) <= half_az, 1.0, 0.0).astype(BF16)
-    down = jnp.concatenate([down, down], axis=1)
     size = block + 2 * LANES
     in_id = lax.broadcasted_iota(jnp.int32, (size, block), 0) - LANES
     out_id = lax.broadcasted_iota(jnp.int32, (size, block), 1)
     across = jnp.where(jnp.abs(in_id - out_id) <= half_rg, 1.0, 0.0).astype(BF16)
 
-    def halves(value):
-        high = value.astype(BF16)
-        return high, (value - high.astype(F32)).astype(BF16)
-
     def load(date, start):
-        piece = now[date][:, pl.ds(start, block)]
+        piece = now[date][:, start : start + block]
         if has_before:
             held = before[date]
             piece = jnp.concatenate(
-                [held[held.shape[0] - 2 * RIM :, pl.ds(start, block)], piece], axis=0
+                [held[held.shape[0] - 2 * RIM :, start : start + block], piece], axis=0
             )
         return piece.astype(F32)
 
     def add_lines(value, term, start):
-        both = jnp.concatenate(halves(value), axis=0)
-        total = jnp.dot(down, both, preferred_element_type=F32)
+        total = jnp.dot(down, value.astype(BF16), preferred_element_type=F32)
         rows = slice(term * lines, (term + 1) * lines)
-        for half, part in enumerate(halves(total)):
-            sums_ref[half, rows, pl.ds(start + LANES, block)] = part
+        sums_ref[rows, start + LANES : start + LANES + block] = total.astype(BF16)
 
     edge = jnp.zeros((terms * lines, LANES), BF16)
-    for half in range(2):
-        sums_ref[half, :, :LANES] = edge
-        sums_ref[half, :, samples + LANES :] = edge
-
-    def first_pass(index, _):
-        start = pl.multiple_of(index * block, block)
+    sums_ref[:, :LANES] = edge
+    sums_ref[:, samples + LANES :] = edge
+    for start in range(0, samples, block):
+        cols = slice(start, start + block)
         re = load(0, start)
         im = load(0, samples + start)
-        image_ref[0, :, pl.ds(start, block)] = re[RIM : RIM + lines].astype(BF16)
-        image_ref[1, :, pl.ds(start, block)] = im[RIM : RIM + lines].astype(BF16)
+        image_ref[0, :, cols] = re[RIM : RIM + lines].astype(BF16)
+        image_ref[1, :, cols] = im[RIM : RIM + lines].astype(BF16)
         add_lines(re * re + im * im, 0, start)
         for date in range(1, dates):
             other_re = load(date, start)
@@ -362,14 +364,13 @@
             add_lines(re * other_re + im * other_im, term, start)
             add_lines(im * other_re - re * other_im, term + 1, start)
             add_lines(other_re * other_re + other_im * other_im, term + 2, start)
-        return 0
-
-    lax.fori_loop(0, samples // block, first_pass, 0, unroll=2)
-
-    def second_pass(index, _):
-        start = pl.multiple_of(index * block, block)
-        total = jnp.dot(sums_ref[0, :, pl.ds(start, size)], across, preferred_element_type=F32)
-        total += jnp.dot(sums_ref[1, :, pl.ds(start, size)], across, preferred_element_type=F32)
+
+    placed = pl.ds(first_line, lines)
+    copies = [pltpu.make_async_copy(image_ref, image_out.at[:, placed, :], sems.at[0])]
+    copies[0].start()
+    for start in range(0, samples, block):
+        cols = slice(start, start + block)
+        total = jnp.dot(sums_ref[:, start : start + size], across, preferred_element_type=F32)
 
         def box(term):
             return total[term * lines : (term + 1) * lines]
@@ -378,11 +379,20 @@
         for date in range(1, dates):
             term = 3 * date - 2
             scale = lax.rsqrt(own * box(term + 2) + epsilon)
-            result_ref[date - 1, 0, :, pl.ds(start, block)] = (box(term) * scale).astype(BF16)
-            result_ref[date - 1, 1, :, pl.ds(start, block)] = (box(term + 1) * scale).astype(BF16)
-        return 0
-
-    lax.fori_loop(0, samples // block, second_pass, 0, unroll=2)
+            result_ref[date - 1, 0, :, cols] = (box(term) * scale).astype(BF16)
+            result_ref[date - 1, 1, :, cols] = (box(term + 1) * scale).astype(BF16)
+        if (start + block) % group == 0:
+            lanes = pl.ds(start + block - group, group)
+            copies.append(
+                pltpu.make_async_copy(
+                    result_ref.at[:, :, :, lanes],
+                    result_out.at[:, :, placed, lanes],
+                    sems.at[len(copies)],
+                )
+            )
+            copies[-1].start()
+    for copy in copies:
+        copy.wait()
 
 
 def kernel_taps(fraction):
@@ -403,6 +413,67 @@
 def from_next(block, axis):
     count = lax.axis_size(axis)
     return lax.ppermute(block, axis, [((i + 1) % count, i) for i in range(count)])
+
+
+def split(total, parts, unit):
+    share = total // sum(parts)
+    if share * sum(parts) != total or share % unit:
+        return [total]
+    return [part * share for part in parts]
+
+
+def wait_for(block, other):
+    return pl.pallas_call(
+        lambda *refs: None,
+        out_shape=jax.ShapeDtypeStruct(block.shape, block.dtype),
+        in_specs=[vmem(), hold()],
+        out_specs=vmem(),
+        input_output_aliases={0: 0},
+        compiler_params=params(1),
+        cost_estimate=cost(0.1),
+        name="wait_for",
+    )(block, other)
+
+
+def more_hops(block, step):
+    others = []
+    for span in range(1, SPAN):
+        with jax.named_scope(f"date_{step}_{span}"):
+            block = from_next(block, "date")
+        others.append(block)
+    return others
+
+
+def finish(count, first_line, now, held, image, result, later):
+    lines, samples = image.shape[1], image.shape[2]
+    operands = [later] + list(now)
+    in_specs = [hold()] + [vmem()] * len(now)
+    aliases = {}
+    if held is not None:
+        operands += held + [image, result]
+        in_specs += [vmem()] * len(held) + [hold()] * 2
+        aliases = {len(operands) - 2: 0, len(operands) - 1: 1}
+    terms = 1 + 3 * SPAN
+    return pl.pallas_call(
+        functools.partial(coherence_kernel, first_line, held is not None),
+        out_shape=[
+            jax.ShapeDtypeStruct(image.shape, BF16),
+            jax.ShapeDtypeStruct((SPAN, 2, lines, samples), BF16),
+            jax.ShapeDtypeStruct((8, LANES), F32),
+        ],
+        in_specs=in_specs,
+        out_specs=[hold(), hold(), vmem()],
+        scratch_shapes=[
+            pltpu.VMEM((2, count, samples), BF16),
+            pltpu.VMEM((SPAN, 2, count, samples), BF16),
+            pltpu.VMEM((terms * count, samples + 2 * LANES), BF16),
+            pltpu.SemaphoreType.DMA((1 + max(1, samples // 512),)),
+        ],
+        input_output_aliases=aliases,
+        compiler_params=params(48),
+        cost_estimate=cost(COH_COST * count / 64),
+        name="coherence",
+    )(*operands)
 
 
 def body(raw_echo, range_rate, azimuth_rate, line_offset, frac_shift):
@@ -415,34 +486,37 @@
     me = lax.axis_index("swath").astype(jnp.int32).reshape(1)
     echo = raw_echo.reshape(2 * lines, samples)
 
-    chunk_count = max(1, min(4, owned // LANES))
-    width = owned // chunk_count
-    depth = pulse_len + width
-    block_type = jax.ShapeDtypeStruct((lines, 2 * width), BF16)
-    table, *blocks = pl.pallas_call(
-        functools.partial(first_range_kernel, devices, pulse_len),
-        out_shape=[jax.ShapeDtypeStruct((depth, 2 * width), BF16)] + [block_type] * devices,
-        in_specs=[smem(), smem(), vmem()],
-        out_specs=[vmem()] * (devices + 1),
-        scratch_shapes=[pltpu.VMEM((2, PACK, pulse_len + 2 * width + LANES), F32)],
-        compiler_params=params(40),
-        cost_estimate=cost(2),
-        name="range_first",
-    )(me, range_rate.reshape(1), echo)
+    widths = split(owned, COLUMN_PARTS, LANES)
+    depth = pulse_len + LANES
     columns = []
-    for chunk in range(chunk_count):
-        if chunk > 0:
+    offset = 0
+    blocks = table = None
+    for chunk, width in enumerate(widths):
+        block_types = [jax.ShapeDtypeStruct((lines, 2 * width), BF16)] * devices
+        if chunk == 0:
+            table, *blocks = pl.pallas_call(
+                functools.partial(first_range_kernel, devices, pulse_len),
+                out_shape=[jax.ShapeDtypeStruct((depth, 2 * LANES), BF16)] + block_types,
+                in_specs=[smem(), smem(), vmem()],
+                out_specs=[vmem()] * (devices + 1),
+                scratch_shapes=[pltpu.VMEM((2, PACK, pulse_len + 3 * LANES), F32)],
+                compiler_params=params(40),
+                cost_estimate=cost(0.5 + 1.3 * width / LANES),
+                name="range_first",
+            )(me, range_rate.reshape(1), echo)
+        else:
             blocks = pl.pallas_call(
-                functools.partial(next_range_kernel, devices, chunk, pulse_len),
-                out_shape=[block_type] * devices,
+                functools.partial(next_range_kernel, devices, offset, pulse_len),
+                out_shape=block_types,
                 in_specs=[smem(), vmem(), vmem(), hold()],
                 out_specs=[vmem()] * devices,
                 compiler_params=params(40),
-                cost_estimate=cost(1.5),
+                cost_estimate=cost(0.1 + 1.4 * width / LANES),
                 name="range_next",
             )(me, echo, table, blocks[0])
         with jax.named_scope(f"columns_{chunk}"):
             columns.append(scatter(blocks, "swath"))
+        offset += width
 
     taps = kernel_taps(frac_shift[0])
     signs = 1.0 - 2.0 * ((line_offset[0] + jnp.arange(TAPS, dtype=jnp.int32)) % 2).astype(F32)
@@ -463,83 +537,92 @@
     )(line_offset, taps, azimuth_rate.reshape(1, owned), blocks[0])
 
     spectra = []
-    for chunk in range(chunk_count):
+    offset = 0
+    for chunk, width in enumerate(widths):
         spectra.append(
             pl.pallas_call(
-                functools.partial(forward_kernel, devices, chunk),
+                functools.partial(forward_kernel, devices, offset),
                 out_shape=jax.ShapeDtypeStruct((size, 2 * width), BF16),
                 in_specs=[smem()] + [vmem()] * 3 + [hold()] + [vmem()] * devices,
                 out_specs=vmem(),
                 scratch_shapes=[pltpu.VMEM((size, 2 * width), BF16)],
                 compiler_params=params(40),
-                cost_estimate=cost(1),
+                cost_estimate=cost(0.9 * width / LANES),
                 name="azimuth_forward",
             )(me, dft, coef, filt, spectra[-1] if spectra else coef, *columns[chunk])
         )
-
-    step_lines = min(lines, LINE_STEP)
-    steps = lines // step_lines
-    image = result = held = outs = own = None
-    passed = []
-    for step in range(steps):
-        rows = step_lines + (2 * RIM if step == 0 else 0)
-        first_row = step * step_lines + (0 if step == 0 else 2 * RIM)
+        offset += width
+
+    line_counts = split(lines, LINE_PARTS, PACK)
+    pieces = []
+    first_row = 0
+    for step, count in enumerate(line_counts):
+        rows = count + (2 * RIM if step == 0 else 0)
+        pieces.append((first_row, rows))
+        first_row += rows
+
+    def invert(chosen, after):
         outs = pl.pallas_call(
-            functools.partial(inverse_kernel, devices, lines, first_row, rows, chunk_count),
-            out_shape=[jax.ShapeDtypeStruct((rows, 2 * owned), BF16)] * devices,
-            in_specs=[smem(), vmem(), hold()] + [vmem()] * chunk_count,
-            out_specs=[vmem()] * devices,
+            functools.partial(inverse_kernel, devices, lines, chosen, widths),
+            out_shape=[
+                jax.ShapeDtypeStruct((rows, 2 * owned), BF16)
+                for _, rows in chosen
+                for _ in range(devices)
+            ],
+            in_specs=[smem(), vmem(), hold()] + [vmem()] * len(widths),
+            out_specs=[vmem()] * (devices * len(chosen)),
             compiler_params=params(40),
-            cost_estimate=cost(0.8),
+            cost_estimate=cost(3.2 * sum(rows for _, rows in chosen) / (lines + 2 * RIM)),
             name="azimuth_inverse",
-        )(me, inv, outs[0] if outs else spectra[-1], *spectra)
+        )(me, inv, after, *spectra)
+        return [outs[i : i + devices] for i in range(0, len(outs), devices)]
+
+    ready = []
+    for step in range(min(2, len(pieces))):
+        ready += invert([pieces[step]], ready[-1][0] if ready else spectra[-1])
+    image = jax.ShapeDtypeStruct((2, lines, samples), BF16)
+    state = (image, None, me, None)
+    own = hop = None
+    stages = []
+
+    def end_step(step, state):
+        image, result, _, held = state
+        own, hop, others = stages[step]
+        now = [own, hop] + others
+        later = stages[min(step + LATER, len(stages) - 1)][0] if LATER else me
+        image, result, token = finish(
+            line_counts[step], sum(line_counts[:step]), now, held, image, result, later
+        )
+        return image, result, token, now
+
+    for step, (_, rows) in enumerate(pieces):
         with jax.named_scope(f"strips_{step}"):
-            strips = scatter(outs, "swath")
+            strips = scatter(ready[step], "swath")
+        last = step == len(pieces) - 1
         own = pl.pallas_call(
-            functools.partial(join_kernel, devices, step == 0, step == steps - 1),
+            functools.partial(join_kernel, devices, step == 0, last),
             out_shape=jax.ShapeDtypeStruct((rows, 2 * samples), BF16),
-            in_specs=[smem(), hold(), hold()] + [vmem()] * devices,
+            in_specs=[smem()] + [hold()] * 3 + [vmem()] * devices,
             out_specs=vmem(),
             compiler_params=params(40),
-            cost_estimate=cost(0.3),
+            cost_estimate=cost(JOIN_COST),
             name="join_strips",
-        )(me, own if step else me, passed[step - 2] if step > 1 else me, *strips)
-        now = [own]
-        for span in range(SPAN):
-            with jax.named_scope(f"date_{step}_{span}"):
-                now.append(from_next(now[-1], "date"))
-        operands = list(now)
-        in_specs = [vmem()] * len(now)
-        aliases = {}
-        if held is not None:
-            operands += held + [image, result]
-            in_specs += [vmem()] * len(held) + [pl.BlockSpec(memory_space=pl.ANY)] * 2
-            aliases = {len(operands) - 2: 0, len(operands) - 1: 1}
-        image, result, token = pl.pallas_call(
-            functools.partial(coherence_kernel, held is not None),
-            grid=(1,),
-            out_shape=[
-                jax.ShapeDtypeStruct((2, lines, samples), BF16),
-                jax.ShapeDtypeStruct((SPAN, 2, lines, samples), BF16),
-                jax.ShapeDtypeStruct((8, LANES), F32),
-            ],
-            in_specs=in_specs,
-            out_specs=[
-                pl.BlockSpec((2, step_lines, samples), lambda i, s=step: (0, s, 0)),
-                pl.BlockSpec((SPAN, 2, step_lines, samples), lambda i, s=step: (0, 0, s, 0)),
-                pl.BlockSpec((8, LANES), lambda i: (0, 0)),
-            ],
-            scratch_shapes=[
-                pltpu.VMEM((2, (1 + 3 * SPAN) * step_lines, samples + 2 * LANES), BF16)
-            ],
-            input_output_aliases=aliases,
-            compiler_params=params(48),
-            cost_estimate=cost(6),
-            name="coherence",
-        )(*operands)
-        held = now
-        passed.append(token)
-    return (image[None], result[None])
+        )(me, own if step else me, ready[-1][0], state[2], *strips)
+        if step + 2 < len(pieces):
+            ready += invert([pieces[step + 2]], own)
+        if hop is not None:
+            if HOP_WAITS:
+                hop = wait_for(hop, own)
+            stages[-1] = [stages[-1][0], hop, more_hops(hop, step - 1)]
+        with jax.named_scope(f"date_{step}_0"):
+            hop = from_next(own, "date")
+        stages.append([own, hop])
+        if step >= LAG:
+            state = end_step(step - LAG, state)
+    stages[-1].append(more_hops(hop, len(pieces) - 1))
+    for step in range(max(0, len(pieces) - LAG), len(pieces)):
+        state = end_step(step, state)
+    return (state[0][None], state[1][None])
 
 
 def solution(mesh):

time: 144 us -> 137 us (0.951)
  Pallas kernels: 45.9 us -> 37.3 us
  starting transfers between devices: 61.4 us -> 64.1 us
    pallas_call x19, Pallas kernels: 35.5 us -> 26.9 us  [the longest x4 15.4 us: finish(): pl.pallas_call(functools.partial(coherence_kernel, first_line, held is no...]
    ppermute x24, starting transfers between devices: 45.5 us -> 48.8 us  [scatter(): moved.append(lax.ppermute(blocks[step], axis, route))]
    ppermute x8, waiting for transfers between devices: 10.5 us -> 9.01 us  [from_next(): lax.ppermute(block, axis, [((i + 1) % count, i) for i in range(count)])]
  transfers between devices with their start and end apart: 32 -> 32, of which waited for: 9 -> 10; matrix products, arithmetic and copies ran while one was open for 1% -> 1% of each run, Pallas kernels for 25% -> 22%
where the time goes in v3:
time: 137 us
  starting transfers between devices  64.1 us (47%)
  Pallas kernels  37.3 us (27%)
  waiting for transfers between devices  29.3 us (21%)
  between operations  3.02 us (2%)
  local copies, waits for them, and re-layouts  1.59 us (1%)
  other arithmetic  1.46 us (1%)
    ppermute x24, starting transfers between devices, scatter(): moved.append(lax.ppermute(blocks[step], axis, route))  48.8 us
    ppermute x24, waiting for transfers between devices, scatter(): moved.append(lax.ppermute(blocks[step], axis, route))  20.2 us
    pallas_call x4, Pallas kernels, finish(): pl.pallas_call(functools.partial(coherence_kernel, first_line, held is no...  15.4 us
    ppermute x8, starting transfers between devices, from_next(): lax.ppermute(block, axis, [((i + 1) % count, i) for i in range(count)])  15.3 us
    ppermute x8, waiting for transfers between devices, from_next(): lax.ppermute(block, axis, [((i + 1) % count, i) for i in range(count)])  9.01 us
    pallas_call x1, Pallas kernels, body(): pl.pallas_call(tables_kernel, out_shape=[jax.ShapeDtypeStruct((size, size...  8.61 us
    pallas_call x3, Pallas kernels, body(): pl.pallas_call(functools.partial(next_range_kernel, devices, offset, puls...  4.76 us
    pallas_call x4, Pallas kernels, body(): pl.pallas_call(functools.partial(forward_kernel, devices, offset), out_sh...  3.6 us
  transfers between devices with their start and end apart: 32, of which 10 were waited for; matrix products, arithmetic and copies ran while one was open for 1% of the time, Pallas kernels for 22%

profile of v3, /device:TPU:0, one launch (start us, length us, event | category | flops | bytes accessed | tf_op | source)
XLA Modules:
  0.0 136.7 jit_solution(11250990474387960148)
XLA Ops:
  1.3 1.6 %copy-done = bf16[1,2,256,2048]{3,2,1,0:T(8,128)(2,1)S(1)} copy-done((bf16[1,2,256,2048]{3,2,1,0:T(8,128)(2,1)S(1)}, bf16[1,2,256,2048]{3,2,1,0:T(8,128)(2,1)}, u32[]{:S(2)}) %copy-start) | copy-done | bytes 2097176
  2.9 1.8 %range_first.1 = (bf16[1152,256]{1,0:T(8,128)(2,1)S(1)}, bf16[256,256]{1,0:T(8,128)(2,1)S(1)}, bf16[256,256]{1,0:T(8,128)(2,1)S(1)}, bf16[256,256]{1,0:T(8,128)(2,1)S(1)}, bf16[256,256]{1,0:T(8,128)(2,1)S(1)}) custom-call(s32[1]{0:T(128)} %bitcast.me_ref._before._ended._later, f32[1]{0:T(128)} %bitcast.9.rate_ref, bf16[512,2048]{1,0:T(8,128)(2,1)S(1)} %bitcast.12), custom_call_target="tpu_custom_call" | custom-call | flops 1800000000 | tf_op jit(solution)/shard_map/range_first/pallas_call | solution.py:497
  4.6 3.1 %collective-permute-start = (bf16[256,256]{1,0:T(8,128)(2,1)S(1)}, bf16[256,256]{1,0:T(8,128)(2,1)S(1)}, u32[]{:S(2)}, u32[]{:S(2)}) collective-permute-start(bf16[256,256]{1,0:T(8,128)(2,1)S(1)} %get-tuple-element.57), channel_id=1, source_target_pairs={{0,1},{1,2},{2,3},{3,0},{4,5},{5,6},{6,7},{7,4},{8,9},{9,10},{10,1... | collective-permute-start | bytes 393224 | tf_op jit(solution)/shard_map/columns_0/ppermute | solution.py:409
  7.7 2.6 %collective-permute-start.1 = (bf16[256,256]{1,0:T(8,128)(2,1)S(1)}, bf16[256,256]{1,0:T(8,128)(2,1)S(1)}, u32[]{:S(2)}, u32[]{:S(2)}) collective-permute-start(bf16[256,256]{1,0:T(8,128)(2,1)S(1)} %get-tuple-element.58), channel_id=1, source_target_pairs={{0,2},{1,3},{2,0},{3,1},{4,6},{5,7},{6,4},{7,5},{8,10},{9,11},{10,... | collective-permute-start | bytes 393224 | tf_op jit(solution)/shard_map/columns_0/ppermute | solution.py:409
  10.3 1.4 collective-permute-start.2
  11.7 1.6 %range_next.3 = (bf16[256,256]{1,0:T(8,128)(2,1)S(1)}, bf16[256,256]{1,0:T(8,128)(2,1)S(1)}, bf16[256,256]{1,0:T(8,128)(2,1)S(1)}, bf16[256,256]{1,0:T(8,128)(2,1)S(1)}) custom-call(s32[1]{0:T(128)} %bitcast.me_ref._before._ended._later, bf16[512,2048]{1,0:T(8,128)(2,1)S(1)} %bitcast.13, bf16[1152,256]{1,0:T(8,128)(2,1)S(1)} %get-tuple-element.48.table_ref, ...), custom_call_target="tpu_custom_call" | custom-call | flops 1500000000 | tf_op jit(solution)/shard_map/range_next/pallas_call | solution.py:508
  15.6 1.6 %range_next.4 = (bf16[256,256]{1,0:T(8,128)(2,1)S(1)}, bf16[256,256]{1,0:T(8,128)(2,1)S(1)}, bf16[256,256]{1,0:T(8,128)(2,1)S(1)}, bf16[256,256]{1,0:T(8,128)(2,1)S(1)}) custom-call(s32[1]{0:T(128)} %bitcast.me_ref._before._ended._later, bf16[512,2048]{1,0:T(8,128)(2,1)S(1)} %bitcast.14, bf16[1152,256]{1,0:T(8,128)(2,1)S(1)} %get-tuple-element.48.table_ref, ...), custom_call_target="tpu_custom_call" | custom-call | flops 1500000000 | tf_op jit(solution)/shard_map/range_next/pallas_call | solution.py:508
  17.9 0.7 pad_maximum_fusion.taps_ref
  18.7 1.6 %range_next.5 = (bf16[256,256]{1,0:T(8,128)(2,1)S(1)}, bf16[256,256]{1,0:T(8,128)(2,1)S(1)}, bf16[256,256]{1,0:T(8,128)(2,1)S(1)}, bf16[256,256]{1,0:T(8,128)(2,1)S(1)}) custom-call(s32[1]{0:T(128)} %bitcast.me_ref._before._ended._later, bf16[512,2048]{1,0:T(8,128)(2,1)S(1)} %bitcast.15, bf16[1152,256]{1,0:T(8,128)(2,1)S(1)} %get-tuple-element.48.table_ref, ...), custom_call_target="tpu_custom_call" | custom-call | flops 1500000000 | tf_op jit(solution)/shard_map/range_next/pallas_call | solution.py:508
  20.3 2.9 %collective-permute-start.5 = (bf16[256,256]{1,0:T(8,128)(2,1)S(1)}, bf16[256,256]{1,0:T(8,128)(2,1)S(1)}, u32[]{:S(2)}, u32[]{:S(2)}) collective-permute-start(bf16[256,256]{1,0:T(8,128)(2,1)S(1)} %get-tuple-element.62), channel_id=1, source_target_pairs={{0,3},{1,0},{2,1},{3,2},{4,7},{5,4},{6,5},{7,6},{8,11},{9,8},{10,9... | collective-permute-start | bytes 393224 | tf_op jit(solution)/shard_map/columns_1/ppermute | solution.py:409
  23.2 2.8 %collective-permute-start.6 = (bf16[256,256]{1,0:T(8,128)(2,1)S(1)}, bf16[256,256]{1,0:T(8,128)(2,1)S(1)}, u32[]{:S(2)}, u32[]{:S(2)}) collective-permute-start(bf16[256,256]{1,0:T(8,128)(2,1)S(1)} %get-tuple-element.63), channel_id=1, source_target_pairs={{0,1},{1,2},{2,3},{3,0},{4,5},{5,6},{6,7},{7,4},{8,9},{9,10},{10,1... | collective-permute-start | bytes 393224 | tf_op jit(solution)/shard_map/columns_2/ppermute | solution.py:409
  26.0 8.6 %azimuth_tables.1 = (bf16[1024,1024]{1,0:T(8,128)(2,1)S(1)}, bf16[1040,1024]{1,0:T(8,128)(2,1)S(1)}, f32[3,512,128]{2,1,0:T(8,128)S(1)}, f32[2,520,512]{2,1,0:T(8,128)S(1)}) custom-call(s32[1]{0:T(128)} %copy.20.shift_ref, f32[9]{0:T(128)S(1)} %pad_maximum_fusion.taps_ref, f32[1,512]{1,0:T(1,128)S(1)} %bitcast.16, ...), custom_call_target="tpu_custom_call" | custom-call | flops 8499999744 | tf_op jit(solution)/shard_map/azimuth_tables/pallas_call | solution.py:524
  34.6 3.5 %collective-permute-start.7 = (bf16[256,256]{1,0:T(8,128)(2,1)S(1)}, bf16[256,256]{1,0:T(8,128)(2,1)S(1)}, u32[]{:S(2)}, u32[]{:S(2)}) collective-permute-start(bf16[256,256]{1,0:T(8,128)(2,1)S(1)} %get-tuple-element.64), channel_id=1, source_target_pairs={{0,2},{1,3},{2,0},{3,1},{4,6},{5,7},{6,4},{7,5},{8,10},{9,11},{10,... | collective-permute-start | bytes 393224 | tf_op jit(solution)/shard_map/columns_2/ppermute | solution.py:409
  38.1 0.9 azimuth_forward.4._.rest_0_
  39.1 2.1 %collective-permute-start.9 = (bf16[256,256]{1,0:T(8,128)(2,1)S(1)}, bf16[256,256]{1,0:T(8,128)(2,1)S(1)}, u32[]{:S(2)}, u32[]{:S(2)}) collective-permute-start(bf16[256,256]{1,0:T(8,128)(2,1)S(1)} %get-tuple-element.66), channel_id=1, source_target_pairs={{0,1},{1,2},{2,3},{3,0},{4,5},{5,6},{6,7},{7,4},{8,9},{9,10},{10,1... | collective-permute-start | bytes 393224 | tf_op jit(solution)/shard_map/columns_3/ppermute | solution.py:409
  41.2 2.4 %collective-permute-start.11 = (bf16[256,256]{1,0:T(8,128)(2,1)S(1)}, bf16[256,256]{1,0:T(8,128)(2,1)S(1)}, u32[]{:S(2)}, u32[]{:S(2)}) collective-permute-start(bf16[256,256]{1,0:T(8,128)(2,1)S(1)} %get-tuple-element.68), channel_id=1, source_target_pairs={{0,3},{1,0},{2,1},{3,2},{4,7},{5,4},{6,5},{7,6},{8,11},{9,8},{10,9... | collective-permute-start | bytes 393224 | tf_op jit(solution)/shard_map/columns_3/ppermute | solution.py:409
  43.6 0.9 azimuth_forward.5._.rest_1_
  44.5 4.6 %collective-permute-done.7.rest_2_ = bf16[256,256]{1,0:T(8,128)(2,1)S(1)} collective-permute-done((bf16[256,256]{1,0:T(8,128)(2,1)S(1)}, bf16[256,256]{1,0:T(8,128)(2,1)S(1)}, u32[]{:S(2)}, u32[]{:S(2)}) %collective-permute-start.7) | collective-permute-done | bytes 131104 | tf_op jit(solution)/shard_map/columns_2/ppermute | solution.py:409
  49.1 0.9 azimuth_forward.6._.rest_2_
  50.0 3.9 %collective-permute-done.10.rest_2_ = bf16[256,256]{1,0:T(8,128)(2,1)S(1)} collective-permute-done((bf16[256,256]{1,0:T(8,128)(2,1)S(1)}, bf16[256,256]{1,0:T(8,128)(2,1)S(1)}, u32[]{:S(2)}, u32[]{:S(2)}) %collective-permute-start.10) | collective-permute-done | bytes 131104 | tf_op jit(solution)/shard_map/columns_3/ppermute | solution.py:409
  54.0 0.9 azimuth_forward.7._.rest_3_
  54.9 1.0 azimuth_inverse.4
  55.9 2.0 %collective-permute-start.12 = (bf16[96,1024]{1,0:T(8,128)(2,1)S(1)}, bf16[96,1024]{1,0:T(8,128)(2,1)S(1)}, u32[]{:S(2)}, u32[]{:S(2)}) collective-permute-start(bf16[96,1024]{1,0:T(8,128)(2,1)S(1)} %get-tuple-element.71), channel_id=1, source_target_pairs={{0,1},{1,2},{2,3},{3,0},{4,5},{5,6},{6,7},{7,4},{8,9},{9,10},{10,1... | collective-permute-start | bytes 589832 | tf_op jit(solution)/shard_map/strips_0/ppermute | solution.py:409
  57.9 1.7 %collective-permute-start.13 = (bf16[96,1024]{1,0:T(8,128)(2,1)S(1)}, bf16[96,1024]{1,0:T(8,128)(2,1)S(1)}, u32[]{:S(2)}, u32[]{:S(2)}) collective-permute-start(bf16[96,1024]{1,0:T(8,128)(2,1)S(1)} %get-tuple-element.72), channel_id=1, source_target_pairs={{0,2},{1,3},{2,0},{3,1},{4,6},{5,7},{6,4},{7,5},{8,10},{9,11},{10,... | collective-permute-start | bytes 589832 | tf_op jit(solution)/shard_map/strips_0/ppermute | solution.py:409
  60.3 0.9 azimuth_inverse.5
  61.2 4.4 %collective-permute-done.12.rest_1_ = bf16[96,1024]{1,0:T(8,128)(2,1)S(1)} collective-permute-done((bf16[96,1024]{1,0:T(8,128)(2,1)S(1)}, bf16[96,1024]{1,0:T(8,128)(2,1)S(1)}, u32[]{:S(2)}, u32[]{:S(2)}) %collective-permute-start.12) | collective-permute-done | bytes 196640 | tf_op jit(solution)/shard_map/strips_0/ppermute | solution.py:409
  65.6 5.3 %collective-permute-done.13.rest_2_ = bf16[96,1024]{1,0:T(8,128)(2,1)S(1)} collective-permute-done((bf16[96,1024]{1,0:T(8,128)(2,1)S(1)}, bf16[96,1024]{1,0:T(8,128)(2,1)S(1)}, u32[]{:S(2)}, u32[]{:S(2)}) %collective-permute-start.13) | collective-permute-done | bytes 196640 | tf_op jit(solution)/shard_map/strips_0/ppermute | solution.py:409
  71.0 2.1 %collective-permute-start.21 = (bf16[96,4096]{1,0:T(8,128)(2,1)S(1)}, bf16[96,4096]{1,0:T(8,128)(2,1)S(1)}, u32[]{:S(2)}, u32[]{:S(2)}) collective-permute-start(bf16[96,4096]{1,0:T(8,128)(2,1)S(1)} %join_strips.4._._before.refs_0_.refs_3_), channel_id=1, source_target_pairs={{4,0},{8,4},{12,8},{16,12},{20,16},{24,20},{28,24},{0,28},{5,1},{9... | collective-permute-start | bytes 2359304 | tf_op jit(solution)/shard_map/date_0_0/ppermute | solution.py:415
  73.1 4.8 %collective-permute-start.15 = (bf16[80,1024]{1,0:T(8,128)(2,1)S(1)}, bf16[80,1024]{1,0:T(8,128)(2,1)S(1)}, u32[]{:S(2)}, u32[]{:S(2)}) collective-permute-start(bf16[80,1024]{1,0:T(8,128)(2,1)S(1)} %get-tuple-element.75), channel_id=1, source_target_pairs={{0,1},{1,2},{2,3},{3,0},{4,5},{5,6},{6,7},{7,4},{8,9},{9,10},{10,1... | collective-permute-start | bytes 491528 | tf_op jit(solution)/shard_map/strips_1/ppermute | solution.py:409
  77.9 2.4 %collective-permute-start.17 = (bf16[80,1024]{1,0:T(8,128)(2,1)S(1)}, bf16[80,1024]{1,0:T(8,128)(2,1)S(1)}, u32[]{:S(2)}, u32[]{:S(2)}) collective-permute-start(bf16[80,1024]{1,0:T(8,128)(2,1)S(1)} %get-tuple-element.77), channel_id=1, source_target_pairs={{0,3},{1,0},{2,1},{3,2},{4,7},{5,4},{6,5},{7,6},{8,11},{9,8},{10,9... | collective-permute-start | bytes 491528 | tf_op jit(solution)/shard_map/strips_1/ppermute | solution.py:409
  80.2 2.4 %collective-permute-done.21.refs_1_.refs_4_ = bf16[96,4096]{1,0:T(8,128)(2,1)S(1)} collective-permute-done((bf16[96,4096]{1,0:T(8,128)(2,1)S(1)}, bf16[96,4096]{1,0:T(8,128)(2,1)S(1)}, u32[]{:S(2)}, u32[]{:S(2)}) %collective-permute-start.21) | collective-permute-done | bytes 786464 | tf_op jit(solution)/shard_map/date_0_0/ppermute | solution.py:415
  82.6 3.1 %collective-permute-start.22 = (bf16[96,4096]{1,0:T(8,128)(2,1)S(1)}, bf16[96,4096]{1,0:T(8,128)(2,1)S(1)}, u32[]{:S(2)}, u32[]{:S(2)}) collective-permute-start(bf16[96,4096]{1,0:T(8,128)(2,1)S(1)} %collective-permute-done.21.refs_1_.refs_4_), channel_id=1, source_target_pairs={{4,0},{8,4},{12,8},{16,12},{20,16},{24,20},{28,24},{0,28},{5,1},{9... | collective-permute-start | bytes 2359304 | tf_op jit(solution)/shard_map/date_0_1/ppermute | solution.py:415
  86.4 4.5 %collective-permute-start.18 = (bf16[64,1024]{1,0:T(8,128)(2,1)S(1)}, bf16[64,1024]{1,0:T(8,128)(2,1)S(1)}, u32[]{:S(2)}, u32[]{:S(2)}) collective-permute-start(bf16[64,1024]{1,0:T(8,128)(2,1)S(1)} %get-tuple-element.79), channel_id=1, source_target_pairs={{0,1},{1,2},{2,3},{3,0},{4,5},{5,6},{6,7},{7,4},{8,9},{9,10},{10,1... | collective-permute-start | bytes 393224 | tf_op jit(solution)/shard_map/strips_2/ppermute | solution.py:409
  91.0 6.4 %collective-permute-start.20 = (bf16[64,1024]{1,0:T(8,128)(2,1)S(1)}, bf16[64,1024]{1,0:T(8,128)(2,1)S(1)}, u32[]{:S(2)}, u32[]{:S(2)}) collective-permute-start(bf16[64,1024]{1,0:T(8,128)(2,1)S(1)} %get-tuple-element.81), channel_id=1, source_target_pairs={{0,3},{1,0},{2,1},{3,2},{4,7},{5,4},{6,5},{7,6},{8,11},{9,8},{10,9... | collective-permute-start | bytes 393224 | tf_op jit(solution)/shard_map/strips_2/ppermute | solution.py:409
  98.0 1.8 %collective-permute-done.19.rest_2_ = bf16[64,1024]{1,0:T(8,128)(2,1)S(1)} collective-permute-done((bf16[64,1024]{1,0:T(8,128)(2,1)S(1)}, bf16[64,1024]{1,0:T(8,128)(2,1)S(1)}, u32[]{:S(2)}, u32[]{:S(2)}) %collective-permute-start.19) | collective-permute-done | bytes 131104 | tf_op jit(solution)/shard_map/strips_2/ppermute | solution.py:409
  100.0 1.9 %collective-permute-start.28 = (bf16[64,4096]{1,0:T(8,128)(2,1)S(1)}, bf16[64,4096]{1,0:T(8,128)(2,1)S(1)}, u32[]{:S(2)}, u32[]{:S(2)}) collective-permute-start(bf16[64,4096]{1,0:T(8,128)(2,1)S(1)} %join_strips.6._before.refs_0_.refs_3_), channel_id=1, source_target_pairs={{4,0},{8,4},{12,8},{16,12},{20,16},{24,20},{28,24},{0,28},{5,1},{9... | collective-permute-start | bytes 1572872 | tf_op jit(solution)/shard_map/date_2_0/ppermute | solution.py:415
  101.8 3.8 %collective-permute-done.30.refs_1_.refs_4_ = bf16[80,4096]{1,0:T(8,128)(2,1)S(1)} collective-permute-done((bf16[80,4096]{1,0:T(8,128)(2,1)S(1)}, bf16[80,4096]{1,0:T(8,128)(2,1)S(1)}, u32[]{:S(2)}, u32[]{:S(2)}) %collective-permute-start.30) | collective-permute-done | bytes 655392 | tf_op jit(solution)/shard_map/date_1_0/ppermute | solution.py:415
  105.6 2.8 %collective-permute-start.31 = (bf16[80,4096]{1,0:T(8,128)(2,1)S(1)}, bf16[80,4096]{1,0:T(8,128)(2,1)S(1)}, u32[]{:S(2)}, u32[]{:S(2)}) collective-permute-start(bf16[80,4096]{1,0:T(8,128)(2,1)S(1)} %collective-permute-done.30.refs_1_.refs_4_), channel_id=1, source_target_pairs={{4,0},{8,4},{12,8},{16,12},{20,16},{24,20},{28,24},{0,28},{5,1},{9... | collective-permute-start | bytes 1966088 | tf_op jit(solution)/shard_map/date_1_1/ppermute | solution.py:415
  108.4 2.1 %collective-permute-start.23 = (bf16[32,1024]{1,0:T(8,128)(2,1)S(1)}, bf16[32,1024]{1,0:T(8,128)(2,1)S(1)}, u32[]{:S(2)}, u32[]{:S(2)}) collective-permute-start(bf16[32,1024]{1,0:T(8,128)(2,1)S(1)} %get-tuple-element.83), channel_id=1, source_target_pairs={{0,1},{1,2},{2,3},{3,0},{4,5},{5,6},{6,7},{7,4},{8,9},{9,10},{10,1... | collective-permute-start | bytes 196616 | tf_op jit(solution)/shard_map/strips_3/ppermute | solution.py:409
  110.5 0.7 collective-permute-done.28.refs_1_.refs_4_
  111.2 2.3 %collective-permute-start.25 = (bf16[32,1024]{1,0:T(8,128)(2,1)S(1)}, bf16[32,1024]{1,0:T(8,128)(2,1)S(1)}, u32[]{:S(2)}, u32[]{:S(2)}) collective-permute-start(bf16[32,1024]{1,0:T(8,128)(2,1)S(1)} %get-tuple-element.85), channel_id=1, source_target_pairs={{0,3},{1,0},{2,1},{3,2},{4,7},{5,4},{6,5},{7,6},{8,11},{9,8},{10,9... | collective-permute-start | bytes 196616 | tf_op jit(solution)/shard_map/strips_3/ppermute | solution.py:409
  113.5 2.5 %collective-permute-start.29 = (bf16[64,4096]{1,0:T(8,128)(2,1)S(1)}, bf16[64,4096]{1,0:T(8,128)(2,1)S(1)}, u32[]{:S(2)}, u32[]{:S(2)}) collective-permute-start(bf16[64,4096]{1,0:T(8,128)(2,1)S(1)} %collective-permute-done.28.refs_1_.refs_4_), channel_id=1, source_target_pairs={{4,0},{8,4},{12,8},{16,12},{20,16},{24,20},{28,24},{0,28},{5,1},{9... | collective-permute-start | bytes 1572872 | tf_op jit(solution)/shard_map/date_2_1/ppermute | solution.py:415
  116.0 3.8 %coherence.4 = (bf16[2,256,2048]{2,1,0:T(8,128)(2,1)}, bf16[2,2,256,2048]{3,2,1,0:T(8,128)(2,1)}, f32[8,128]{1,0:T(8,128)S(1)}) custom-call(s32[1]{0:T(128)} %bitcast.me_ref._before._ended._later, bf16[96,4096]{1,0:T(8,128)(2,1)S(1)} %join_strips.4._._before.refs_0_.refs_3_, bf16[96,4096]{1,0:T(8,128)(2,1)S(1)} %collective-permute-done.21.refs_1_.refs_4_, ...), custom_call_target="tpu_custom_call" | custom-call | flops 6249999872 | tf_op jit(solution)/shard_map/coherence/pallas_call | solution.py:457
  120.0 4.5 %coherence.5 = (bf16[2,256,2048]{2,1,0:T(8,128)(2,1)}, bf16[2,2,256,2048]{3,2,1,0:T(8,128)(2,1)}, f32[8,128]{1,0:T(8,128)}) custom-call(s32[1]{0:T(128)} %bitcast.me_ref._before._ended._later, bf16[80,4096]{1,0:T(8,128)(2,1)S(1)} %join_strips.5._._before.refs_0_.refs_3_, ...), custom_call_target="tpu_custom_call", output_to_operand_aliasing={{0}: (7, {}), {1}: (8, {})} | custom-call | flops 6249999872 | tf_op jit(solution)/shard_map/coherence/pallas_call | solution.py:457
  124.6 2.1 %collective-permute-done.26.refs_1_ = bf16[32,4096]{1,0:T(8,128)(2,1)S(1)} collective-permute-done((bf16[32,4096]{1,0:T(8,128)(2,1)S(1)}, bf16[32,4096]{1,0:T(8,128)(2,1)S(1)}, u32[]{:S(2)}, u32[]{:S(2)}) %collective-permute-start.26) | collective-permute-done | bytes 262176 | tf_op jit(solution)/shard_map/date_3_0/ppermute | solution.py:415
  126.7 2.8 %collective-permute-start.27 = (bf16[32,4096]{1,0:T(8,128)(2,1)S(1)}, bf16[32,4096]{1,0:T(8,128)(2,1)S(1)}, u32[]{:S(2)}, u32[]{:S(2)}) collective-permute-start(bf16[32,4096]{1,0:T(8,128)(2,1)S(1)} %collective-permute-done.26.refs_1_), channel_id=1, source_target_pairs={{4,0},{8,4},{12,8},{16,12},{20,16},{24,20},{28,24},{0,28},{5,1},{9... | collective-permute-start | bytes 786440 | tf_op jit(solution)/shard_map/date_3_1/ppermute | solution.py:415
  129.5 4.1 %coherence.6 = (bf16[2,256,2048]{2,1,0:T(8,128)(2,1)}, bf16[2,2,256,2048]{3,2,1,0:T(8,128)(2,1)}, f32[8,128]{1,0:T(8,128)}) custom-call(s32[1]{0:T(128)} %bitcast.me_ref._before._ended._later, bf16[64,4096]{1,0:T(8,128)(2,1)S(1)} %join_strips.6._before.refs_0_.refs_3_, ...), custom_call_target="tpu_custom_call", output_to_operand_aliasing={{0}: (7, {}), {1}: (8, {})} | custom-call | flops 5000000000 | tf_op jit(solution)/shard_map/coherence/pallas_call | solution.py:457
  133.6 2.9 %coherence.7 = (bf16[2,256,2048]{2,1,0:T(8,128)(2,1)}, bf16[2,2,256,2048]{3,2,1,0:T(8,128)(2,1)}, f32[8,128]{1,0:T(8,128)}) custom-call(s32[1]{0:T(128)} %bitcast.me_ref._before._ended._later, bf16[32,4096]{1,0:T(8,128)(2,1)S(1)} %join_strips.7.refs_0_, ...), custom_call_target="tpu_custom_call", output_to_operand_aliasing={{0}: (7, {}), {1}: (8, {})} | custom-call | flops 2500000000 | tf_op jit(solution)/shard_map/coherence/pallas_call | solution.py:457
  (43 shorter events, 4.2 us)
Async XLA Ops:
  1.3 1.6 %copy-start = (bf16[1,2,256,2048]{3,2,1,0:T(8,128)(2,1)S(1)}, bf16[1,2,256,2048]{3,2,1,0:T(8,128)(2,1)}, u32[]{:S(2)}) copy-start(bf16[1,2,256,2048]{3,2,1,0:T(8,128)(2,1)} %param.5) | copy-start | bytes 6291460
  4.6 15.6 %collective-permute-start = (bf16[256,256]{1,0:T(8,128)(2,1)S(1)}, bf16[256,256]{1,0:T(8,128)(2,1)S(1)}, u32[]{:S(2)}, u32[]{:S(2)}) collective-permute-start(bf16[256,256]{1,0:T(8,128)(2,1)S(1)} %get-tuple-element.57), channel_id=1, source_target_pairs={{0,1},{1,2},{2,3},{3,0},{4,5},{5,6},{6,7},{7,4},{8,9},{9,10},{10,1... | collective-permute-start | bytes 393224 | tf_op jit(solution)/shard_map/columns_0/ppermute | solution.py:409
  7.7 15.4 %collective-permute-start.1 = (bf16[256,256]{1,0:T(8,128)(2,1)S(1)}, bf16[256,256]{1,0:T(8,128)(2,1)S(1)}, u32[]{:S(2)}, u32[]{:S(2)}) collective-permute-start(bf16[256,256]{1,0:T(8,128)(2,1)S(1)} %get-tuple-element.58), channel_id=1, source_target_pairs={{0,2},{1,3},{2,0},{3,1},{4,6},{5,7},{6,4},{7,5},{8,10},{9,11},{10,... | collective-permute-start | bytes 393224 | tf_op jit(solution)/shard_map/columns_0/ppermute | solution.py:409
  10.3 24.3 %collective-permute-start.2 = (bf16[256,256]{1,0:T(8,128)(2,1)S(1)}, bf16[256,256]{1,0:T(8,128)(2,1)S(1)}, u32[]{:S(2)}, u32[]{:S(2)}) collective-permute-start(bf16[256,256]{1,0:T(8,128)(2,1)S(1)} %get-tuple-element.59), channel_id=1, source_target_pairs={{0,3},{1,0},{2,1},{3,2},{4,7},{5,4},{6,5},{7,6},{8,11},{9,8},{10,9... | collective-permute-start | bytes 393224 | tf_op jit(solution)/shard_map/columns_0/ppermute | solution.py:409
  13.3 24.9 %collective-permute-start.3 = (bf16[256,256]{1,0:T(8,128)(2,1)S(1)}, bf16[256,256]{1,0:T(8,128)(2,1)S(1)}, u32[]{:S(2)}, u32[]{:S(2)}) collective-permute-start(bf16[256,256]{1,0:T(8,128)(2,1)S(1)} %get-tuple-element.60), channel_id=1, source_target_pairs={{0,1},{1,2},{2,3},{3,0},{4,5},{5,6},{6,7},{7,4},{8,9},{9,10},{10,1... | collective-permute-start | bytes 393224 | tf_op jit(solution)/shard_map/columns_1/ppermute | solution.py:409
  14.0 25.1 %collective-permute-start.4 = (bf16[256,256]{1,0:T(8,128)(2,1)S(1)}, bf16[256,256]{1,0:T(8,128)(2,1)S(1)}, u32[]{:S(2)}, u32[]{:S(2)}) collective-permute-start(bf16[256,256]{1,0:T(8,128)(2,1)S(1)} %get-tuple-element.61), channel_id=1, source_target_pairs={{0,2},{1,3},{2,0},{3,1},{4,6},{5,7},{6,4},{7,5},{8,10},{9,11},{10,... | collective-permute-start | bytes 393224 | tf_op jit(solution)/shard_map/columns_1/ppermute | solution.py:409
  18.7 7.3 %copy-start.1 = (f32[512]{0:T(512)S(1)}, f32[512]{0:T(512)}, u32[]{:S(2)}) copy-start(f32[512]{0:T(512)} %param.7) | copy-start | bytes 6148
  20.3 20.9 %collective-permute-start.5 = (bf16[256,256]{1,0:T(8,128)(2,1)S(1)}, bf16[256,256]{1,0:T(8,128)(2,1)S(1)}, u32[]{:S(2)}, u32[]{:S(2)}) collective-permute-start(bf16[256,256]{1,0:T(8,128)(2,1)S(1)} %get-tuple-element.62), channel_id=1, source_target_pairs={{0,3},{1,0},{2,1},{3,2},{4,7},{5,4},{6,5},{7,6},{8,11},{9,8},{10,9... | collective-permute-start | bytes 393224 | tf_op jit(solution)/shard_map/columns_1/ppermute | solution.py:409
  23.2 18.1 %collective-permute-start.6 = (bf16[256,256]{1,0:T(8,128)(2,1)S(1)}, bf16[256,256]{1,0:T(8,128)(2,1)S(1)}, u32[]{:S(2)}, u32[]{:S(2)}) collective-permute-start(bf16[256,256]{1,0:T(8,128)(2,1)S(1)} %get-tuple-element.63), channel_id=1, source_target_pairs={{0,1},{1,2},{2,3},{3,0},{4,5},{5,6},{6,7},{7,4},{8,9},{9,10},{10,1... | collective-permute-start | bytes 393224 | tf_op jit(solution)/shard_map/columns_2/ppermute | solution.py:409
  34.6 14.5 %collective-permute-start.7 = (bf16[256,256]{1,0:T(8,128)(2,1)S(1)}, bf16[256,256]{1,0:T(8,128)(2,1)S(1)}, u32[]{:S(2)}, u32[]{:S(2)}) collective-permute-start(bf16[256,256]{1,0:T(8,128)(2,1)S(1)} %get-tuple-element.64), channel_id=1, source_target_pairs={{0,2},{1,3},{2,0},{3,1},{4,6},{5,7},{6,4},{7,5},{8,10},{9,11},{10,... | collective-permute-start | bytes 393224 | tf_op jit(solution)/shard_map/columns_2/ppermute | solution.py:409
  38.1 11.0 %collective-permute-start.8 = (bf16[256,256]{1,0:T(8,128)(2,1)S(1)}, bf16[256,256]{1,0:T(8,128)(2,1)S(1)}, u32[]{:S(2)}, u32[]{:S(2)}) collective-permute-start(bf16[256,256]{1,0:T(8,128)(2,1)S(1)} %get-tuple-element.65), channel_id=1, source_target_pairs={{0,3},{1,0},{2,1},{3,2},{4,7},{5,4},{6,5},{7,6},{8,11},{9,8},{10,9... | collective-permute-start | bytes 393224 | tf_op jit(solution)/shard_map/columns_2/ppermute | solution.py:409
  39.1 11.0 %collective-permute-start.9 = (bf16[256,256]{1,0:T(8,128)(2,1)S(1)}, bf16[256,256]{1,0:T(8,128)(2,1)S(1)}, u32[]{:S(2)}, u32[]{:S(2)}) collective-permute-start(bf16[256,256]{1,0:T(8,128)(2,1)S(1)} %get-tuple-element.66), channel_id=1, source_target_pairs={{0,1},{1,2},{2,3},{3,0},{4,5},{5,6},{6,7},{7,4},{8,9},{9,10},{10,1... | collective-permute-start | bytes 393224 | tf_op jit(solution)/shard_map/columns_3/ppermute | solution.py:409
  41.2 12.8 %collective-permute-start.10 = (bf16[256,256]{1,0:T(8,128)(2,1)S(1)}, bf16[256,256]{1,0:T(8,128)(2,1)S(1)}, u32[]{:S(2)}, u32[]{:S(2)}) collective-permute-start(bf16[256,256]{1,0:T(8,128)(2,1)S(1)} %get-tuple-element.67), channel_id=1, source_target_pairs={{0,2},{1,3},{2,0},{3,1},{4,6},{5,7},{6,4},{7,5},{8,10},{9,11},{10,... | collective-permute-start | bytes 393224 | tf_op jit(solution)/shard_map/columns_3/ppermute | solution.py:409
  41.2 12.8 %collective-permute-start.11 = (bf16[256,256]{1,0:T(8,128)(2,1)S(1)}, bf16[256,256]{1,0:T(8,128)(2,1)S(1)}, u32[]{:S(2)}, u32[]{:S(2)}) collective-permute-start(bf16[256,256]{1,0:T(8,128)(2,1)S(1)} %get-tuple-element.68), channel_id=1, source_target_pairs={{0,3},{1,0},{2,1},{3,2},{4,7},{5,4},{6,5},{7,6},{8,11},{9,8},{10,9... | collective-permute-start | bytes 393224 | tf_op jit(solution)/shard_map/columns_3/ppermute | solution.py:409
  55.9 9.7 %collective-permute-start.12 = (bf16[96,1024]{1,0:T(8,128)(2,1)S(1)}, bf16[96,1024]{1,0:T(8,128)(2,1)S(1)}, u32[]{:S(2)}, u32[]{:S(2)}) collective-permute-start(bf16[96,1024]{1,0:T(8,128)(2,1)S(1)} %get-tuple-element.71), channel_id=1, source_target_pairs={{0,1},{1,2},{2,3},{3,0},{4,5},{5,6},{6,7},{7,4},{8,9},{9,10},{10,1... | collective-permute-start | bytes 589832 | tf_op jit(solution)/shard_map/strips_0/ppermute | solution.py:409
  57.9 13.0 %collective-permute-start.13 = (bf16[96,1024]{1,0:T(8,128)(2,1)S(1)}, bf16[96,1024]{1,0:T(8,128)(2,1)S(1)}, u32[]{:S(2)}, u32[]{:S(2)}) collective-permute-start(bf16[96,1024]{1,0:T(8,128)(2,1)S(1)} %get-tuple-element.72), channel_id=1, source_target_pairs={{0,2},{1,3},{2,0},{3,1},{4,6},{5,7},{6,4},{7,5},{8,10},{9,11},{10,... | collective-permute-start | bytes 589832 | tf_op jit(solution)/shard_map/strips_0/ppermute | solution.py:409
  59.6 11.3 %collective-permute-start.14 = (bf16[96,1024]{1,0:T(8,128)(2,1)S(1)}, bf16[96,1024]{1,0:T(8,128)(2,1)S(1)}, u32[]{:S(2)}, u32[]{:S(2)}) collective-permute-start(bf16[96,1024]{1,0:T(8,128)(2,1)S(1)} %get-tuple-element.73), channel_id=1, source_target_pairs={{0,3},{1,0},{2,1},{3,2},{4,7},{5,4},{6,5},{7,6},{8,11},{9,8},{10,9... | collective-permute-start | bytes 589832 | tf_op jit(solution)/shard_map/strips_0/ppermute | solution.py:409
  71.0 11.6 %collective-permute-start.21 = (bf16[96,4096]{1,0:T(8,128)(2,1)S(1)}, bf16[96,4096]{1,0:T(8,128)(2,1)S(1)}, u32[]{:S(2)}, u32[]{:S(2)}) collective-permute-start(bf16[96,4096]{1,0:T(8,128)(2,1)S(1)} %join_strips.4._._before.refs_0_.refs_3_), channel_id=1, source_target_pairs={{4,0},{8,4},{12,8},{16,12},{20,16},{24,20},{28,24},{0,28},{5,1},{9... | collective-permute-start | bytes 2359304 | tf_op jit(solution)/shard_map/date_0_0/ppermute | solution.py:415
  73.1 17.9 %collective-permute-start.15 = (bf16[80,1024]{1,0:T(8,128)(2,1)S(1)}, bf16[80,1024]{1,0:T(8,128)(2,1)S(1)}, u32[]{:S(2)}, u32[]{:S(2)}) collective-permute-start(bf16[80,1024]{1,0:T(8,128)(2,1)S(1)} %get-tuple-element.75), channel_id=1, source_target_pairs={{0,1},{1,2},{2,3},{3,0},{4,5},{5,6},{6,7},{7,4},{8,9},{9,10},{10,1... | collective-permute-start | bytes 491528 | tf_op jit(solution)/shard_map/strips_1/ppermute | solution.py:409
  77.9 13.1 %collective-permute-start.16 = (bf16[80,1024]{1,0:T(8,128)(2,1)S(1)}, bf16[80,1024]{1,0:T(8,128)(2,1)S(1)}, u32[]{:S(2)}, u32[]{:S(2)}) collective-permute-start(bf16[80,1024]{1,0:T(8,128)(2,1)S(1)} %get-tuple-element.76), channel_id=1, source_target_pairs={{0,2},{1,3},{2,0},{3,1},{4,6},{5,7},{6,4},{7,5},{8,10},{9,11},{10,... | collective-permute-start | bytes 491528 | tf_op jit(solution)/shard_map/strips_1/ppermute | solution.py:409
  77.9 19.5 %collective-permute-start.17 = (bf16[80,1024]{1,0:T(8,128)(2,1)S(1)}, bf16[80,1024]{1,0:T(8,128)(2,1)S(1)}, u32[]{:S(2)}, u32[]{:S(2)}) collective-permute-start(bf16[80,1024]{1,0:T(8,128)(2,1)S(1)} %get-tuple-element.77), channel_id=1, source_target_pairs={{0,3},{1,0},{2,1},{3,2},{4,7},{5,4},{6,5},{7,6},{8,11},{9,8},{10,9... | collective-permute-start | bytes 491528 | tf_op jit(solution)/shard_map/strips_1/ppermute | solution.py:409
  82.6 30.9 %collective-permute-start.22 = (bf16[96,4096]{1,0:T(8,128)(2,1)S(1)}, bf16[96,4096]{1,0:T(8,128)(2,1)S(1)}, u32[]{:S(2)}, u32[]{:S(2)}) collective-permute-start(bf16[96,4096]{1,0:T(8,128)(2,1)S(1)} %collective-permute-done.21.refs_1_.refs_4_), channel_id=1, source_target_pairs={{4,0},{8,4},{12,8},{16,12},{20,16},{24,20},{28,24},{0,28},{5,1},{9... | collective-permute-start | bytes 2359304 | tf_op jit(solution)/shard_map/date_0_1/ppermute | solution.py:415
  86.4 11.6 %collective-permute-start.18 = (bf16[64,1024]{1,0:T(8,128)(2,1)S(1)}, bf16[64,1024]{1,0:T(8,128)(2,1)S(1)}, u32[]{:S(2)}, u32[]{:S(2)}) collective-permute-start(bf16[64,1024]{1,0:T(8,128)(2,1)S(1)} %get-tuple-element.79), channel_id=1, source_target_pairs={{0,1},{1,2},{2,3},{3,0},{4,5},{5,6},{6,7},{7,4},{8,9},{9,10},{10,1... | collective-permute-start | bytes 393224 | tf_op jit(solution)/shard_map/strips_2/ppermute | solution.py:409
  91.0 8.8 %collective-permute-start.19 = (bf16[64,1024]{1,0:T(8,128)(2,1)S(1)}, bf16[64,1024]{1,0:T(8,128)(2,1)S(1)}, u32[]{:S(2)}, u32[]{:S(2)}) collective-permute-start(bf16[64,1024]{1,0:T(8,128)(2,1)S(1)} %get-tuple-element.80), channel_id=1, source_target_pairs={{0,2},{1,3},{2,0},{3,1},{4,6},{5,7},{6,4},{7,5},{8,10},{9,11},{10,... | collective-permute-start | bytes 393224 | tf_op jit(solution)/shard_map/strips_2/ppermute | solution.py:409
  91.0 9.0 %collective-permute-start.20 = (bf16[64,1024]{1,0:T(8,128)(2,1)S(1)}, bf16[64,1024]{1,0:T(8,128)(2,1)S(1)}, u32[]{:S(2)}, u32[]{:S(2)}) collective-permute-start(bf16[64,1024]{1,0:T(8,128)(2,1)S(1)} %get-tuple-element.81), channel_id=1, source_target_pairs={{0,3},{1,0},{2,1},{3,2},{4,7},{5,4},{6,5},{7,6},{8,11},{9,8},{10,9... | collective-permute-start | bytes 393224 | tf_op jit(solution)/shard_map/strips_2/ppermute | solution.py:409
  97.5 8.2 %collective-permute-start.30 = (bf16[80,4096]{1,0:T(8,128)(2,1)S(1)}, bf16[80,4096]{1,0:T(8,128)(2,1)S(1)}, u32[]{:S(2)}, u32[]{:S(2)}) collective-permute-start(bf16[80,4096]{1,0:T(8,128)(2,1)S(1)} %join_strips.5._._before.refs_0_.refs_3_), channel_id=1, source_target_pairs={{4,0},{8,4},{12,8},{16,12},{20,16},{24,20},{28,24},{0,28},{5,1},{9... | collective-permute-start | bytes 1966088 | tf_op jit(solution)/shard_map/date_1_0/ppermute | solution.py:415
  100.0 11.3 %collective-permute-start.28 = (bf16[64,4096]{1,0:T(8,128)(2,1)S(1)}, bf16[64,4096]{1,0:T(8,128)(2,1)S(1)}, u32[]{:S(2)}, u32[]{:S(2)}) collective-permute-start(bf16[64,4096]{1,0:T(8,128)(2,1)S(1)} %join_strips.6._before.refs_0_.refs_3_), channel_id=1, source_target_pairs={{4,0},{8,4},{12,8},{16,12},{20,16},{24,20},{28,24},{0,28},{5,1},{9... | collective-permute-start | bytes 1572872 | tf_op jit(solution)/shard_map/date_2_0/ppermute | solution.py:415
  105.6 14.4 %collective-permute-start.31 = (bf16[80,4096]{1,0:T(8,128)(2,1)S(1)}, bf16[80,4096]{1,0:T(8,128)(2,1)S(1)}, u32[]{:S(2)}, u32[]{:S(2)}) collective-permute-start(bf16[80,4096]{1,0:T(8,128)(2,1)S(1)} %collective-permute-done.30.refs_1_.refs_4_), channel_id=1, source_target_pairs={{4,0},{8,4},{12,8},{16,12},{20,16},{24,20},{28,24},{0,28},{5,1},{9... | collective-permute-start | bytes 1966088 | tf_op jit(solution)/shard_map/date_1_1/ppermute | solution.py:415
  108.4 11.5 %collective-permute-start.23 = (bf16[32,1024]{1,0:T(8,128)(2,1)S(1)}, bf16[32,1024]{1,0:T(8,128)(2,1)S(1)}, u32[]{:S(2)}, u32[]{:S(2)}) collective-permute-start(bf16[32,1024]{1,0:T(8,128)(2,1)S(1)} %get-tuple-element.83), channel_id=1, source_target_pairs={{0,1},{1,2},{2,3},{3,0},{4,5},{5,6},{6,7},{7,4},{8,9},{9,10},{10,1... | collective-permute-start | bytes 196616 | tf_op jit(solution)/shard_map/strips_3/ppermute | solution.py:409
  110.5 9.4 %collective-permute-start.24 = (bf16[32,1024]{1,0:T(8,128)(2,1)S(1)}, bf16[32,1024]{1,0:T(8,128)(2,1)S(1)}, u32[]{:S(2)}, u32[]{:S(2)}) collective-permute-start(bf16[32,1024]{1,0:T(8,128)(2,1)S(1)} %get-tuple-element.84), channel_id=1, source_target_pairs={{0,2},{1,3},{2,0},{3,1},{4,6},{5,7},{6,4},{7,5},{8,10},{9,11},{10,... | collective-permute-start | bytes 196616 | tf_op jit(solution)/shard_map/strips_3/ppermute | solution.py:409
  111.2 8.7 %collective-permute-start.25 = (bf16[32,1024]{1,0:T(8,128)(2,1)S(1)}, bf16[32,1024]{1,0:T(8,128)(2,1)S(1)}, u32[]{:S(2)}, u32[]{:S(2)}) collective-permute-start(bf16[32,1024]{1,0:T(8,128)(2,1)S(1)} %get-tuple-element.85), channel_id=1, source_target_pairs={{0,3},{1,0},{2,1},{3,2},{4,7},{5,4},{6,5},{7,6},{8,11},{9,8},{10,9... | collective-permute-start | bytes 196616 | tf_op jit(solution)/shard_map/strips_3/ppermute | solution.py:409
  113.5 16.0 %collective-permute-start.29 = (bf16[64,4096]{1,0:T(8,128)(2,1)S(1)}, bf16[64,4096]{1,0:T(8,128)(2,1)S(1)}, u32[]{:S(2)}, u32[]{:S(2)}) collective-permute-start(bf16[64,4096]{1,0:T(8,128)(2,1)S(1)} %collective-permute-done.28.refs_1_.refs_4_), channel_id=1, source_target_pairs={{4,0},{8,4},{12,8},{16,12},{20,16},{24,20},{28,24},{0,28},{5,1},{9... | collective-permute-start | bytes 1572872 | tf_op jit(solution)/shard_map/date_2_1/ppermute | solution.py:415
  120.0 6.7 %collective-permute-start.26 = (bf16[32,4096]{1,0:T(8,128)(2,1)S(1)}, bf16[32,4096]{1,0:T(8,128)(2,1)S(1)}, u32[]{:S(2)}, u32[]{:S(2)}) collective-permute-start(bf16[32,4096]{1,0:T(8,128)(2,1)S(1)} %join_strips.7.refs_0_), channel_id=1, source_target_pairs={{4,0},{8,4},{12,8},{16,12},{20,16},{24,20},{28,24},{0,28},{5,1},{9... | collective-permute-start | bytes 786440 | tf_op jit(solution)/shard_map/date_3_0/ppermute | solution.py:415
  126.7 6.9 %collective-permute-start.27 = (bf16[32,4096]{1,0:T(8,128)(2,1)S(1)}, bf16[32,4096]{1,0:T(8,128)(2,1)S(1)}, u32[]{:S(2)}, u32[]{:S(2)}) collective-permute-start(bf16[32,4096]{1,0:T(8,128)(2,1)S(1)} %collective-permute-done.26.refs_1_), channel_id=1, source_target_pairs={{4,0},{8,4},{12,8},{16,12},{20,16},{24,20},{28,24},{0,28},{5,1},{9... | collective-permute-start | bytes 786440 | tf_op jit(solution)/shard_map/date_3_1/ppermute | solution.py:415

commit v4 on v3

--- a/solution.py
+++ b/solution.py
@@ -22,6 +22,7 @@
 HOP_WAITS = False
 LATER = 0
 LAG = 2
+STEP_SIGN = 1
 PACE = 1.0
 
 two_pi = 2.0 * math.pi
@@ -403,10 +404,10 @@
 
 def scatter(blocks, axis):
     count = lax.axis_size(axis)
-    moved = [blocks[0]]
-    for step in range(1, count):
+    moved = [blocks[0]] + [None] * (count - 1)
+    for step in sorted(range(1, count), key=lambda step: STEP_SIGN * abs(2 * step - count)):
         route = [(i, (i + step) % count) for i in range(count)]
-        moved.append(lax.ppermute(blocks[step], axis, route))
+        moved[step] = lax.ppermute(blocks[step], axis, route)
     return moved
 
 

time: 137 us -> 137 us (level)
  no operation moved by 1% of the time
where the time goes in v4:
time: 137 us
  starting transfers between devices  64.1 us (47%)
  Pallas kernels  37.3 us (27%)
  waiting for transfers between devices  29.3 us (21%)
  between operations  3.02 us (2%)
  local copies, waits for them, and re-layouts  1.59 us (1%)
  other arithmetic  1.46 us (1%)
    ppermute x24, starting transfers between devices, scatter(): moved[step] = lax.ppermute(blocks[step], axis, route)  48.8 us
    ppermute x24, waiting for transfers between devices, scatter(): moved[step] = lax.ppermute(blocks[step], axis, route)  20.2 us
    pallas_call x4, Pallas kernels, finish(): pl.pallas_call(functools.partial(coherence_kernel, first_line, held is no...  15.4 us
    ppermute x8, starting transfers between devices, from_next(): lax.ppermute(block, axis, [((i + 1) % count, i) for i in range(count)])  15.3 us
    ppermute x8, waiting for transfers between devices, from_next(): lax.ppermute(block, axis, [((i + 1) % count, i) for i in range(count)])  9.01 us
    pallas_call x1, Pallas kernels, body(): pl.pallas_call(tables_kernel, out_shape=[jax.ShapeDtypeStruct((size, size...  8.61 us
    pallas_call x3, Pallas kernels, body(): pl.pallas_call(functools.partial(next_range_kernel, devices, offset, puls...  4.76 us
    pallas_call x4, Pallas kernels, body(): pl.pallas_call(functools.partial(forward_kernel, devices, offset), out_sh...  3.6 us
  transfers between devices with their start and end apart: 32, of which 10 were waited for; matrix products, arithmetic and copies ran while one was open for 1% of the time, Pallas kernels for 22%

profile of v4, /device:TPU:0, one launch (start us, length us, event | category | flops | bytes accessed | tf_op | source)
XLA Modules:
  0.0 136.7 jit_solution(11250990474387960148)
XLA Ops:
  1.3 1.6 %copy-done = bf16[1,2,256,2048]{3,2,1,0:T(8,128)(2,1)S(1)} copy-done((bf16[1,2,256,2048]{3,2,1,0:T(8,128)(2,1)S(1)}, bf16[1,2,256,2048]{3,2,1,0:T(8,128)(2,1)}, u32[]{:S(2)}) %copy-start) | copy-done | bytes 2097176
  2.9 1.8 %range_first.1 = (bf16[1152,256]{1,0:T(8,128)(2,1)S(1)}, bf16[256,256]{1,0:T(8,128)(2,1)S(1)}, bf16[256,256]{1,0:T(8,128)(2,1)S(1)}, bf16[256,256]{1,0:T(8,128)(2,1)S(1)}, bf16[256,256]{1,0:T(8,128)(2,1)S(1)}) custom-call(s32[1]{0:T(128)} %bitcast.me_ref._before._ended._later, f32[1]{0:T(128)} %bitcast.9.rate_ref, bf16[512,2048]{1,0:T(8,128)(2,1)S(1)} %bitcast.12), custom_call_target="tpu_custom_call" | custom-call | flops 1800000000 | tf_op jit(solution)/shard_map/range_first/pallas_call | solution.py:498
  4.6 3.1 %collective-permute-start = (bf16[256,256]{1,0:T(8,128)(2,1)S(1)}, bf16[256,256]{1,0:T(8,128)(2,1)S(1)}, u32[]{:S(2)}, u32[]{:S(2)}) collective-permute-start(bf16[256,256]{1,0:T(8,128)(2,1)S(1)} %get-tuple-element.57), channel_id=1, source_target_pairs={{0,1},{1,2},{2,3},{3,0},{4,5},{5,6},{6,7},{7,4},{8,9},{9,10},{10,1... | collective-permute-start | bytes 393224 | tf_op jit(solution)/shard_map/columns_0/ppermute | solution.py:410
  7.7 2.6 %collective-permute-start.1 = (bf16[256,256]{1,0:T(8,128)(2,1)S(1)}, bf16[256,256]{1,0:T(8,128)(2,1)S(1)}, u32[]{:S(2)}, u32[]{:S(2)}) collective-permute-start(bf16[256,256]{1,0:T(8,128)(2,1)S(1)} %get-tuple-element.58), channel_id=1, source_target_pairs={{0,2},{1,3},{2,0},{3,1},{4,6},{5,7},{6,4},{7,5},{8,10},{9,11},{10,... | collective-permute-start | bytes 393224 | tf_op jit(solution)/shard_map/columns_0/ppermute | solution.py:410
  10.3 1.4 collective-permute-start.2
  11.7 1.6 %range_next.3 = (bf16[256,256]{1,0:T(8,128)(2,1)S(1)}, bf16[256,256]{1,0:T(8,128)(2,1)S(1)}, bf16[256,256]{1,0:T(8,128)(2,1)S(1)}, bf16[256,256]{1,0:T(8,128)(2,1)S(1)}) custom-call(s32[1]{0:T(128)} %bitcast.me_ref._before._ended._later, bf16[512,2048]{1,0:T(8,128)(2,1)S(1)} %bitcast.13, bf16[1152,256]{1,0:T(8,128)(2,1)S(1)} %get-tuple-element.48.table_ref, ...), custom_call_target="tpu_custom_call" | custom-call | flops 1500000000 | tf_op jit(solution)/shard_map/range_next/pallas_call | solution.py:509
  15.6 1.6 %range_next.4 = (bf16[256,256]{1,0:T(8,128)(2,1)S(1)}, bf16[256,256]{1,0:T(8,128)(2,1)S(1)}, bf16[256,256]{1,0:T(8,128)(2,1)S(1)}, bf16[256,256]{1,0:T(8,128)(2,1)S(1)}) custom-call(s32[1]{0:T(128)} %bitcast.me_ref._before._ended._later, bf16[512,2048]{1,0:T(8,128)(2,1)S(1)} %bitcast.14, bf16[1152,256]{1,0:T(8,128)(2,1)S(1)} %get-tuple-element.48.table_ref, ...), custom_call_target="tpu_custom_call" | custom-call | flops 1500000000 | tf_op jit(solution)/shard_map/range_next/pallas_call | solution.py:509
  17.9 0.7 pad_maximum_fusion.taps_ref
  18.7 1.6 %range_next.5 = (bf16[256,256]{1,0:T(8,128)(2,1)S(1)}, bf16[256,256]{1,0:T(8,128)(2,1)S(1)}, bf16[256,256]{1,0:T(8,128)(2,1)S(1)}, bf16[256,256]{1,0:T(8,128)(2,1)S(1)}) custom-call(s32[1]{0:T(128)} %bitcast.me_ref._before._ended._later, bf16[512,2048]{1,0:T(8,128)(2,1)S(1)} %bitcast.15, bf16[1152,256]{1,0:T(8,128)(2,1)S(1)} %get-tuple-element.48.table_ref, ...), custom_call_target="tpu_custom_call" | custom-call | flops 1500000000 | tf_op jit(solution)/shard_map/range_next/pallas_call | solution.py:509
  20.3 2.9 %collective-permute-start.5 = (bf16[256,256]{1,0:T(8,128)(2,1)S(1)}, bf16[256,256]{1,0:T(8,128)(2,1)S(1)}, u32[]{:S(2)}, u32[]{:S(2)}) collective-permute-start(bf16[256,256]{1,0:T(8,128)(2,1)S(1)} %get-tuple-element.62), channel_id=1, source_target_pairs={{0,3},{1,0},{2,1},{3,2},{4,7},{5,4},{6,5},{7,6},{8,11},{9,8},{10,9... | collective-permute-start | bytes 393224 | tf_op jit(solution)/shard_map/columns_1/ppermute | solution.py:410
  23.2 2.8 %collective-permute-start.6 = (bf16[256,256]{1,0:T(8,128)(2,1)S(1)}, bf16[256,256]{1,0:T(8,128)(2,1)S(1)}, u32[]{:S(2)}, u32[]{:S(2)}) collective-permute-start(bf16[256,256]{1,0:T(8,128)(2,1)S(1)} %get-tuple-element.63), channel_id=1, source_target_pairs={{0,1},{1,2},{2,3},{3,0},{4,5},{5,6},{6,7},{7,4},{8,9},{9,10},{10,1... | collective-permute-start | bytes 393224 | tf_op jit(solution)/shard_map/columns_2/ppermute | solution.py:410
  26.0 8.6 %azimuth_tables.1 = (bf16[1024,1024]{1,0:T(8,128)(2,1)S(1)}, bf16[1040,1024]{1,0:T(8,128)(2,1)S(1)}, f32[3,512,128]{2,1,0:T(8,128)S(1)}, f32[2,520,512]{2,1,0:T(8,128)S(1)}) custom-call(s32[1]{0:T(128)} %copy.20.shift_ref, f32[9]{0:T(128)S(1)} %pad_maximum_fusion.taps_ref, f32[1,512]{1,0:T(1,128)S(1)} %bitcast.16, ...), custom_call_target="tpu_custom_call" | custom-call | flops 8499999744 | tf_op jit(solution)/shard_map/azimuth_tables/pallas_call | solution.py:525
  34.6 3.5 %collective-permute-start.7 = (bf16[256,256]{1,0:T(8,128)(2,1)S(1)}, bf16[256,256]{1,0:T(8,128)(2,1)S(1)}, u32[]{:S(2)}, u32[]{:S(2)}) collective-permute-start(bf16[256,256]{1,0:T(8,128)(2,1)S(1)} %get-tuple-element.64), channel_id=1, source_target_pairs={{0,2},{1,3},{2,0},{3,1},{4,6},{5,7},{6,4},{7,5},{8,10},{9,11},{10,... | collective-permute-start | bytes 393224 | tf_op jit(solution)/shard_map/columns_2/ppermute | solution.py:410
  38.1 0.9 azimuth_forward.4._.rest_0_
  39.1 2.1 %collective-permute-start.9 = (bf16[256,256]{1,0:T(8,128)(2,1)S(1)}, bf16[256,256]{1,0:T(8,128)(2,1)S(1)}, u32[]{:S(2)}, u32[]{:S(2)}) collective-permute-start(bf16[256,256]{1,0:T(8,128)(2,1)S(1)} %get-tuple-element.66), channel_id=1, source_target_pairs={{0,1},{1,2},{2,3},{3,0},{4,5},{5,6},{6,7},{7,4},{8,9},{9,10},{10,1... | collective-permute-start | bytes 393224 | tf_op jit(solution)/shard_map/columns_3/ppermute | solution.py:410
  41.2 2.4 %collective-permute-start.11 = (bf16[256,256]{1,0:T(8,128)(2,1)S(1)}, bf16[256,256]{1,0:T(8,128)(2,1)S(1)}, u32[]{:S(2)}, u32[]{:S(2)}) collective-permute-start(bf16[256,256]{1,0:T(8,128)(2,1)S(1)} %get-tuple-element.68), channel_id=1, source_target_pairs={{0,3},{1,0},{2,1},{3,2},{4,7},{5,4},{6,5},{7,6},{8,11},{9,8},{10,9... | collective-permute-start | bytes 393224 | tf_op jit(solution)/shard_map/columns_3/ppermute | solution.py:410
  43.6 0.9 azimuth_forward.5._.rest_1_
  44.5 4.6 %collective-permute-done.7.rest_2_ = bf16[256,256]{1,0:T(8,128)(2,1)S(1)} collective-permute-done((bf16[256,256]{1,0:T(8,128)(2,1)S(1)}, bf16[256,256]{1,0:T(8,128)(2,1)S(1)}, u32[]{:S(2)}, u32[]{:S(2)}) %collective-permute-start.7) | collective-permute-done | bytes 131104 | tf_op jit(solution)/shard_map/columns_2/ppermute | solution.py:410
  49.1 0.9 azimuth_forward.6._.rest_2_
  50.0 3.9 %collective-permute-done.10.rest_2_ = bf16[256,256]{1,0:T(8,128)(2,1)S(1)} collective-permute-done((bf16[256,256]{1,0:T(8,128)(2,1)S(1)}, bf16[256,256]{1,0:T(8,128)(2,1)S(1)}, u32[]{:S(2)}, u32[]{:S(2)}) %collective-permute-start.10) | collective-permute-done | bytes 131104 | tf_op jit(solution)/shard_map/columns_3/ppermute | solution.py:410
  54.0 0.9 azimuth_forward.7._.rest_3_
  54.9 1.0 azimuth_inverse.4
  55.9 2.0 %collective-permute-start.12 = (bf16[96,1024]{1,0:T(8,128)(2,1)S(1)}, bf16[96,1024]{1,0:T(8,128)(2,1)S(1)}, u32[]{:S(2)}, u32[]{:S(2)}) collective-permute-start(bf16[96,1024]{1,0:T(8,128)(2,1)S(1)} %get-tuple-element.71), channel_id=1, source_target_pairs={{0,1},{1,2},{2,3},{3,0},{4,5},{5,6},{6,7},{7,4},{8,9},{9,10},{10,1... | collective-permute-start | bytes 589832 | tf_op jit(solution)/shard_map/strips_0/ppermute | solution.py:410
  57.9 1.7 %collective-permute-start.13 = (bf16[96,1024]{1,0:T(8,128)(2,1)S(1)}, bf16[96,1024]{1,0:T(8,128)(2,1)S(1)}, u32[]{:S(2)}, u32[]{:S(2)}) collective-permute-start(bf16[96,1024]{1,0:T(8,128)(2,1)S(1)} %get-tuple-element.72), channel_id=1, source_target_pairs={{0,2},{1,3},{2,0},{3,1},{4,6},{5,7},{6,4},{7,5},{8,10},{9,11},{10,... | collective-permute-start | bytes 589832 | tf_op jit(solution)/shard_map/strips_0/ppermute | solution.py:410
  60.3 0.9 azimuth_inverse.5
  61.2 4.4 %collective-permute-done.12.rest_1_ = bf16[96,1024]{1,0:T(8,128)(2,1)S(1)} collective-permute-done((bf16[96,1024]{1,0:T(8,128)(2,1)S(1)}, bf16[96,1024]{1,0:T(8,128)(2,1)S(1)}, u32[]{:S(2)}, u32[]{:S(2)}) %collective-permute-start.12) | collective-permute-done | bytes 196640 | tf_op jit(solution)/shard_map/strips_0/ppermute | solution.py:410
  65.6 5.3 %collective-permute-done.13.rest_2_ = bf16[96,1024]{1,0:T(8,128)(2,1)S(1)} collective-permute-done((bf16[96,1024]{1,0:T(8,128)(2,1)S(1)}, bf16[96,1024]{1,0:T(8,128)(2,1)S(1)}, u32[]{:S(2)}, u32[]{:S(2)}) %collective-permute-start.13) | collective-permute-done | bytes 196640 | tf_op jit(solution)/shard_map/strips_0/ppermute | solution.py:410
  71.0 2.1 %collective-permute-start.21 = (bf16[96,4096]{1,0:T(8,128)(2,1)S(1)}, bf16[96,4096]{1,0:T(8,128)(2,1)S(1)}, u32[]{:S(2)}, u32[]{:S(2)}) collective-permute-start(bf16[96,4096]{1,0:T(8,128)(2,1)S(1)} %join_strips.4._._before.refs_0_.refs_3_), channel_id=1, source_target_pairs={{4,0},{8,4},{12,8},{16,12},{20,16},{24,20},{28,24},{0,28},{5,1},{9... | collective-permute-start | bytes 2359304 | tf_op jit(solution)/shard_map/date_0_0/ppermute | solution.py:416
  73.1 4.8 %collective-permute-start.15 = (bf16[80,1024]{1,0:T(8,128)(2,1)S(1)}, bf16[80,1024]{1,0:T(8,128)(2,1)S(1)}, u32[]{:S(2)}, u32[]{:S(2)}) collective-permute-start(bf16[80,1024]{1,0:T(8,128)(2,1)S(1)} %get-tuple-element.75), channel_id=1, source_target_pairs={{0,1},{1,2},{2,3},{3,0},{4,5},{5,6},{6,7},{7,4},{8,9},{9,10},{10,1... | collective-permute-start | bytes 491528 | tf_op jit(solution)/shard_map/strips_1/ppermute | solution.py:410
  77.9 2.4 %collective-permute-start.17 = (bf16[80,1024]{1,0:T(8,128)(2,1)S(1)}, bf16[80,1024]{1,0:T(8,128)(2,1)S(1)}, u32[]{:S(2)}, u32[]{:S(2)}) collective-permute-start(bf16[80,1024]{1,0:T(8,128)(2,1)S(1)} %get-tuple-element.77), channel_id=1, source_target_pairs={{0,3},{1,0},{2,1},{3,2},{4,7},{5,4},{6,5},{7,6},{8,11},{9,8},{10,9... | collective-permute-start | bytes 491528 | tf_op jit(solution)/shard_map/strips_1/ppermute | solution.py:410
  80.2 2.4 %collective-permute-done.21.refs_1_.refs_4_ = bf16[96,4096]{1,0:T(8,128)(2,1)S(1)} collective-permute-done((bf16[96,4096]{1,0:T(8,128)(2,1)S(1)}, bf16[96,4096]{1,0:T(8,128)(2,1)S(1)}, u32[]{:S(2)}, u32[]{:S(2)}) %collective-permute-start.21) | collective-permute-done | bytes 786464 | tf_op jit(solution)/shard_map/date_0_0/ppermute | solution.py:416
  82.6 3.1 %collective-permute-start.22 = (bf16[96,4096]{1,0:T(8,128)(2,1)S(1)}, bf16[96,4096]{1,0:T(8,128)(2,1)S(1)}, u32[]{:S(2)}, u32[]{:S(2)}) collective-permute-start(bf16[96,4096]{1,0:T(8,128)(2,1)S(1)} %collective-permute-done.21.refs_1_.refs_4_), channel_id=1, source_target_pairs={{4,0},{8,4},{12,8},{16,12},{20,16},{24,20},{28,24},{0,28},{5,1},{9... | collective-permute-start | bytes 2359304 | tf_op jit(solution)/shard_map/date_0_1/ppermute | solution.py:416
  86.4 4.5 %collective-permute-start.18 = (bf16[64,1024]{1,0:T(8,128)(2,1)S(1)}, bf16[64,1024]{1,0:T(8,128)(2,1)S(1)}, u32[]{:S(2)}, u32[]{:S(2)}) collective-permute-start(bf16[64,1024]{1,0:T(8,128)(2,1)S(1)} %get-tuple-element.79), channel_id=1, source_target_pairs={{0,1},{1,2},{2,3},{3,0},{4,5},{5,6},{6,7},{7,4},{8,9},{9,10},{10,1... | collective-permute-start | bytes 393224 | tf_op jit(solution)/shard_map/strips_2/ppermute | solution.py:410
  91.0 6.4 %collective-permute-start.20 = (bf16[64,1024]{1,0:T(8,128)(2,1)S(1)}, bf16[64,1024]{1,0:T(8,128)(2,1)S(1)}, u32[]{:S(2)}, u32[]{:S(2)}) collective-permute-start(bf16[64,1024]{1,0:T(8,128)(2,1)S(1)} %get-tuple-element.81), channel_id=1, source_target_pairs={{0,3},{1,0},{2,1},{3,2},{4,7},{5,4},{6,5},{7,6},{8,11},{9,8},{10,9... | collective-permute-start | bytes 393224 | tf_op jit(solution)/shard_map/strips_2/ppermute | solution.py:410
  98.0 1.8 %collective-permute-done.19.rest_2_ = bf16[64,1024]{1,0:T(8,128)(2,1)S(1)} collective-permute-done((bf16[64,1024]{1,0:T(8,128)(2,1)S(1)}, bf16[64,1024]{1,0:T(8,128)(2,1)S(1)}, u32[]{:S(2)}, u32[]{:S(2)}) %collective-permute-start.19) | collective-permute-done | bytes 131104 | tf_op jit(solution)/shard_map/strips_2/ppermute | solution.py:410
  100.0 1.9 %collective-permute-start.28 = (bf16[64,4096]{1,0:T(8,128)(2,1)S(1)}, bf16[64,4096]{1,0:T(8,128)(2,1)S(1)}, u32[]{:S(2)}, u32[]{:S(2)}) collective-permute-start(bf16[64,4096]{1,0:T(8,128)(2,1)S(1)} %join_strips.6._before.refs_0_.refs_3_), channel_id=1, source_target_pairs={{4,0},{8,4},{12,8},{16,12},{20,16},{24,20},{28,24},{0,28},{5,1},{9... | collective-permute-start | bytes 1572872 | tf_op jit(solution)/shard_map/date_2_0/ppermute | solution.py:416
  101.8 3.8 %collective-permute-done.30.refs_1_.refs_4_ = bf16[80,4096]{1,0:T(8,128)(2,1)S(1)} collective-permute-done((bf16[80,4096]{1,0:T(8,128)(2,1)S(1)}, bf16[80,4096]{1,0:T(8,128)(2,1)S(1)}, u32[]{:S(2)}, u32[]{:S(2)}) %collective-permute-start.30) | collective-permute-done | bytes 655392 | tf_op jit(solution)/shard_map/date_1_0/ppermute | solution.py:416
  105.6 2.8 %collective-permute-start.31 = (bf16[80,4096]{1,0:T(8,128)(2,1)S(1)}, bf16[80,4096]{1,0:T(8,128)(2,1)S(1)}, u32[]{:S(2)}, u32[]{:S(2)}) collective-permute-start(bf16[80,4096]{1,0:T(8,128)(2,1)S(1)} %collective-permute-done.30.refs_1_.refs_4_), channel_id=1, source_target_pairs={{4,0},{8,4},{12,8},{16,12},{20,16},{24,20},{28,24},{0,28},{5,1},{9... | collective-permute-start | bytes 1966088 | tf_op jit(solution)/shard_map/date_1_1/ppermute | solution.py:416
  108.4 2.1 %collective-permute-start.23 = (bf16[32,1024]{1,0:T(8,128)(2,1)S(1)}, bf16[32,1024]{1,0:T(8,128)(2,1)S(1)}, u32[]{:S(2)}, u32[]{:S(2)}) collective-permute-start(bf16[32,1024]{1,0:T(8,128)(2,1)S(1)} %get-tuple-element.83), channel_id=1, source_target_pairs={{0,1},{1,2},{2,3},{3,0},{4,5},{5,6},{6,7},{7,4},{8,9},{9,10},{10,1... | collective-permute-start | bytes 196616 | tf_op jit(solution)/shard_map/strips_3/ppermute | solution.py:410
  110.5 0.7 collective-permute-done.28.refs_1_.refs_4_
  111.2 2.3 %collective-permute-start.25 = (bf16[32,1024]{1,0:T(8,128)(2,1)S(1)}, bf16[32,1024]{1,0:T(8,128)(2,1)S(1)}, u32[]{:S(2)}, u32[]{:S(2)}) collective-permute-start(bf16[32,1024]{1,0:T(8,128)(2,1)S(1)} %get-tuple-element.85), channel_id=1, source_target_pairs={{0,3},{1,0},{2,1},{3,2},{4,7},{5,4},{6,5},{7,6},{8,11},{9,8},{10,9... | collective-permute-start | bytes 196616 | tf_op jit(solution)/shard_map/strips_3/ppermute | solution.py:410
  113.5 2.5 %collective-permute-start.29 = (bf16[64,4096]{1,0:T(8,128)(2,1)S(1)}, bf16[64,4096]{1,0:T(8,128)(2,1)S(1)}, u32[]{:S(2)}, u32[]{:S(2)}) collective-permute-start(bf16[64,4096]{1,0:T(8,128)(2,1)S(1)} %collective-permute-done.28.refs_1_.refs_4_), channel_id=1, source_target_pairs={{4,0},{8,4},{12,8},{16,12},{20,16},{24,20},{28,24},{0,28},{5,1},{9... | collective-permute-start | bytes 1572872 | tf_op jit(solution)/shard_map/date_2_1/ppermute | solution.py:416
  116.0 3.8 %coherence.4 = (bf16[2,256,2048]{2,1,0:T(8,128)(2,1)}, bf16[2,2,256,2048]{3,2,1,0:T(8,128)(2,1)}, f32[8,128]{1,0:T(8,128)S(1)}) custom-call(s32[1]{0:T(128)} %bitcast.me_ref._before._ended._later, bf16[96,4096]{1,0:T(8,128)(2,1)S(1)} %join_strips.4._._before.refs_0_.refs_3_, bf16[96,4096]{1,0:T(8,128)(2,1)S(1)} %collective-permute-done.21.refs_1_.refs_4_, ...), custom_call_target="tpu_custom_call" | custom-call | flops 6249999872 | tf_op jit(solution)/shard_map/coherence/pallas_call | solution.py:458
  120.0 4.5 %coherence.5 = (bf16[2,256,2048]{2,1,0:T(8,128)(2,1)}, bf16[2,2,256,2048]{3,2,1,0:T(8,128)(2,1)}, f32[8,128]{1,0:T(8,128)}) custom-call(s32[1]{0:T(128)} %bitcast.me_ref._before._ended._later, bf16[80,4096]{1,0:T(8,128)(2,1)S(1)} %join_strips.5._._before.refs_0_.refs_3_, ...), custom_call_target="tpu_custom_call", output_to_operand_aliasing={{0}: (7, {}), {1}: (8, {})} | custom-call | flops 6249999872 | tf_op jit(solution)/shard_map/coherence/pallas_call | solution.py:458
  124.6 2.1 %collective-permute-done.26.refs_1_ = bf16[32,4096]{1,0:T(8,128)(2,1)S(1)} collective-permute-done((bf16[32,4096]{1,0:T(8,128)(2,1)S(1)}, bf16[32,4096]{1,0:T(8,128)(2,1)S(1)}, u32[]{:S(2)}, u32[]{:S(2)}) %collective-permute-start.26) | collective-permute-done | bytes 262176 | tf_op jit(solution)/shard_map/date_3_0/ppermute | solution.py:416
  126.7 2.8 %collective-permute-start.27 = (bf16[32,4096]{1,0:T(8,128)(2,1)S(1)}, bf16[32,4096]{1,0:T(8,128)(2,1)S(1)}, u32[]{:S(2)}, u32[]{:S(2)}) collective-permute-start(bf16[32,4096]{1,0:T(8,128)(2,1)S(1)} %collective-permute-done.26.refs_1_), channel_id=1, source_target_pairs={{4,0},{8,4},{12,8},{16,12},{20,16},{24,20},{28,24},{0,28},{5,1},{9... | collective-permute-start | bytes 786440 | tf_op jit(solution)/shard_map/date_3_1/ppermute | solution.py:416
  129.5 4.1 %coherence.6 = (bf16[2,256,2048]{2,1,0:T(8,128)(2,1)}, bf16[2,2,256,2048]{3,2,1,0:T(8,128)(2,1)}, f32[8,128]{1,0:T(8,128)}) custom-call(s32[1]{0:T(128)} %bitcast.me_ref._before._ended._later, bf16[64,4096]{1,0:T(8,128)(2,1)S(1)} %join_strips.6._before.refs_0_.refs_3_, ...), custom_call_target="tpu_custom_call", output_to_operand_aliasing={{0}: (7, {}), {1}: (8, {})} | custom-call | flops 5000000000 | tf_op jit(solution)/shard_map/coherence/pallas_call | solution.py:458
  133.6 2.9 %coherence.7 = (bf16[2,256,2048]{2,1,0:T(8,128)(2,1)}, bf16[2,2,256,2048]{3,2,1,0:T(8,128)(2,1)}, f32[8,128]{1,0:T(8,128)}) custom-call(s32[1]{0:T(128)} %bitcast.me_ref._before._ended._later, bf16[32,4096]{1,0:T(8,128)(2,1)S(1)} %join_strips.7.refs_0_, ...), custom_call_target="tpu_custom_call", output_to_operand_aliasing={{0}: (7, {}), {1}: (8, {})} | custom-call | flops 2500000000 | tf_op jit(solution)/shard_map/coherence/pallas_call | solution.py:458
  (43 shorter events, 4.2 us)
Async XLA Ops:
  1.3 1.6 %copy-start = (bf16[1,2,256,2048]{3,2,1,0:T(8,128)(2,1)S(1)}, bf16[1,2,256,2048]{3,2,1,0:T(8,128)(2,1)}, u32[]{:S(2)}) copy-start(bf16[1,2,256,2048]{3,2,1,0:T(8,128)(2,1)} %param.5) | copy-start | bytes 6291460
  4.6 15.6 %collective-permute-start = (bf16[256,256]{1,0:T(8,128)(2,1)S(1)}, bf16[256,256]{1,0:T(8,128)(2,1)S(1)}, u32[]{:S(2)}, u32[]{:S(2)}) collective-permute-start(bf16[256,256]{1,0:T(8,128)(2,1)S(1)} %get-tuple-element.57), channel_id=1, source_target_pairs={{0,1},{1,2},{2,3},{3,0},{4,5},{5,6},{6,7},{7,4},{8,9},{9,10},{10,1... | collective-permute-start | bytes 393224 | tf_op jit(solution)/shard_map/columns_0/ppermute | solution.py:410
  7.7 15.4 %collective-permute-start.1 = (bf16[256,256]{1,0:T(8,128)(2,1)S(1)}, bf16[256,256]{1,0:T(8,128)(2,1)S(1)}, u32[]{:S(2)}, u32[]{:S(2)}) collective-permute-start(bf16[256,256]{1,0:T(8,128)(2,1)S(1)} %get-tuple-element.58), channel_id=1, source_target_pairs={{0,2},{1,3},{2,0},{3,1},{4,6},{5,7},{6,4},{7,5},{8,10},{9,11},{10,... | collective-permute-start | bytes 393224 | tf_op jit(solution)/shard_map/columns_0/ppermute | solution.py:410
  10.3 24.3 %collective-permute-start.2 = (bf16[256,256]{1,0:T(8,128)(2,1)S(1)}, bf16[256,256]{1,0:T(8,128)(2,1)S(1)}, u32[]{:S(2)}, u32[]{:S(2)}) collective-permute-start(bf16[256,256]{1,0:T(8,128)(2,1)S(1)} %get-tuple-element.59), channel_id=1, source_target_pairs={{0,3},{1,0},{2,1},{3,2},{4,7},{5,4},{6,5},{7,6},{8,11},{9,8},{10,9... | collective-permute-start | bytes 393224 | tf_op jit(solution)/shard_map/columns_0/ppermute | solution.py:410
  13.3 24.9 %collective-permute-start.3 = (bf16[256,256]{1,0:T(8,128)(2,1)S(1)}, bf16[256,256]{1,0:T(8,128)(2,1)S(1)}, u32[]{:S(2)}, u32[]{:S(2)}) collective-permute-start(bf16[256,256]{1,0:T(8,128)(2,1)S(1)} %get-tuple-element.60), channel_id=1, source_target_pairs={{0,1},{1,2},{2,3},{3,0},{4,5},{5,6},{6,7},{7,4},{8,9},{9,10},{10,1... | collective-permute-start | bytes 393224 | tf_op jit(solution)/shard_map/columns_1/ppermute | solution.py:410
  14.0 25.1 %collective-permute-start.4 = (bf16[256,256]{1,0:T(8,128)(2,1)S(1)}, bf16[256,256]{1,0:T(8,128)(2,1)S(1)}, u32[]{:S(2)}, u32[]{:S(2)}) collective-permute-start(bf16[256,256]{1,0:T(8,128)(2,1)S(1)} %get-tuple-element.61), channel_id=1, source_target_pairs={{0,2},{1,3},{2,0},{3,1},{4,6},{5,7},{6,4},{7,5},{8,10},{9,11},{10,... | collective-permute-start | bytes 393224 | tf_op jit(solution)/shard_map/columns_1/ppermute | solution.py:410
  18.7 7.3 %copy-start.1 = (f32[512]{0:T(512)S(1)}, f32[512]{0:T(512)}, u32[]{:S(2)}) copy-start(f32[512]{0:T(512)} %param.7) | copy-start | bytes 6148
  20.3 20.9 %collective-permute-start.5 = (bf16[256,256]{1,0:T(8,128)(2,1)S(1)}, bf16[256,256]{1,0:T(8,128)(2,1)S(1)}, u32[]{:S(2)}, u32[]{:S(2)}) collective-permute-start(bf16[256,256]{1,0:T(8,128)(2,1)S(1)} %get-tuple-element.62), channel_id=1, source_target_pairs={{0,3},{1,0},{2,1},{3,2},{4,7},{5,4},{6,5},{7,6},{8,11},{9,8},{10,9... | collective-permute-start | bytes 393224 | tf_op jit(solution)/shard_map/columns_1/ppermute | solution.py:410
  23.2 18.1 %collective-permute-start.6 = (bf16[256,256]{1,0:T(8,128)(2,1)S(1)}, bf16[256,256]{1,0:T(8,128)(2,1)S(1)}, u32[]{:S(2)}, u32[]{:S(2)}) collective-permute-start(bf16[256,256]{1,0:T(8,128)(2,1)S(1)} %get-tuple-element.63), channel_id=1, source_target_pairs={{0,1},{1,2},{2,3},{3,0},{4,5},{5,6},{6,7},{7,4},{8,9},{9,10},{10,1... | collective-permute-start | bytes 393224 | tf_op jit(solution)/shard_map/columns_2/ppermute | solution.py:410
  34.6 14.5 %collective-permute-start.7 = (bf16[256,256]{1,0:T(8,128)(2,1)S(1)}, bf16[256,256]{1,0:T(8,128)(2,1)S(1)}, u32[]{:S(2)}, u32[]{:S(2)}) collective-permute-start(bf16[256,256]{1,0:T(8,128)(2,1)S(1)} %get-tuple-element.64), channel_id=1, source_target_pairs={{0,2},{1,3},{2,0},{3,1},{4,6},{5,7},{6,4},{7,5},{8,10},{9,11},{10,... | collective-permute-start | bytes 393224 | tf_op jit(solution)/shard_map/columns_2/ppermute | solution.py:410
  38.1 11.0 %collective-permute-start.8 = (bf16[256,256]{1,0:T(8,128)(2,1)S(1)}, bf16[256,256]{1,0:T(8,128)(2,1)S(1)}, u32[]{:S(2)}, u32[]{:S(2)}) collective-permute-start(bf16[256,256]{1,0:T(8,128)(2,1)S(1)} %get-tuple-element.65), channel_id=1, source_target_pairs={{0,3},{1,0},{2,1},{3,2},{4,7},{5,4},{6,5},{7,6},{8,11},{9,8},{10,9... | collective-permute-start | bytes 393224 | tf_op jit(solution)/shard_map/columns_2/ppermute | solution.py:410
  39.1 11.0 %collective-permute-start.9 = (bf16[256,256]{1,0:T(8,128)(2,1)S(1)}, bf16[256,256]{1,0:T(8,128)(2,1)S(1)}, u32[]{:S(2)}, u32[]{:S(2)}) collective-permute-start(bf16[256,256]{1,0:T(8,128)(2,1)S(1)} %get-tuple-element.66), channel_id=1, source_target_pairs={{0,1},{1,2},{2,3},{3,0},{4,5},{5,6},{6,7},{7,4},{8,9},{9,10},{10,1... | collective-permute-start | bytes 393224 | tf_op jit(solution)/shard_map/columns_3/ppermute | solution.py:410
  41.2 12.8 %collective-permute-start.10 = (bf16[256,256]{1,0:T(8,128)(2,1)S(1)}, bf16[256,256]{1,0:T(8,128)(2,1)S(1)}, u32[]{:S(2)}, u32[]{:S(2)}) collective-permute-start(bf16[256,256]{1,0:T(8,128)(2,1)S(1)} %get-tuple-element.67), channel_id=1, source_target_pairs={{0,2},{1,3},{2,0},{3,1},{4,6},{5,7},{6,4},{7,5},{8,10},{9,11},{10,... | collective-permute-start | bytes 393224 | tf_op jit(solution)/shard_map/columns_3/ppermute | solution.py:410
  41.2 12.8 %collective-permute-start.11 = (bf16[256,256]{1,0:T(8,128)(2,1)S(1)}, bf16[256,256]{1,0:T(8,128)(2,1)S(1)}, u32[]{:S(2)}, u32[]{:S(2)}) collective-permute-start(bf16[256,256]{1,0:T(8,128)(2,1)S(1)} %get-tuple-element.68), channel_id=1, source_target_pairs={{0,3},{1,0},{2,1},{3,2},{4,7},{5,4},{6,5},{7,6},{8,11},{9,8},{10,9... | collective-permute-start | bytes 393224 | tf_op jit(solution)/shard_map/columns_3/ppermute | solution.py:410
  55.9 9.7 %collective-permute-start.12 = (bf16[96,1024]{1,0:T(8,128)(2,1)S(1)}, bf16[96,1024]{1,0:T(8,128)(2,1)S(1)}, u32[]{:S(2)}, u32[]{:S(2)}) collective-permute-start(bf16[96,1024]{1,0:T(8,128)(2,1)S(1)} %get-tuple-element.71), channel_id=1, source_target_pairs={{0,1},{1,2},{2,3},{3,0},{4,5},{5,6},{6,7},{7,4},{8,9},{9,10},{10,1... | collective-permute-start | bytes 589832 | tf_op jit(solution)/shard_map/strips_0/ppermute | solution.py:410
  57.9 13.0 %collective-permute-start.13 = (bf16[96,1024]{1,0:T(8,128)(2,1)S(1)}, bf16[96,1024]{1,0:T(8,128)(2,1)S(1)}, u32[]{:S(2)}, u32[]{:S(2)}) collective-permute-start(bf16[96,1024]{1,0:T(8,128)(2,1)S(1)} %get-tuple-element.72), channel_id=1, source_target_pairs={{0,2},{1,3},{2,0},{3,1},{4,6},{5,7},{6,4},{7,5},{8,10},{9,11},{10,... | collective-permute-start | bytes 589832 | tf_op jit(solution)/shard_map/strips_0/ppermute | solution.py:410
  59.6 11.3 %collective-permute-start.14 = (bf16[96,1024]{1,0:T(8,128)(2,1)S(1)}, bf16[96,1024]{1,0:T(8,128)(2,1)S(1)}, u32[]{:S(2)}, u32[]{:S(2)}) collective-permute-start(bf16[96,1024]{1,0:T(8,128)(2,1)S(1)} %get-tuple-element.73), channel_id=1, source_target_pairs={{0,3},{1,0},{2,1},{3,2},{4,7},{5,4},{6,5},{7,6},{8,11},{9,8},{10,9... | collective-permute-start | bytes 589832 | tf_op jit(solution)/shard_map/strips_0/ppermute | solution.py:410
  71.0 11.6 %collective-permute-start.21 = (bf16[96,4096]{1,0:T(8,128)(2,1)S(1)}, bf16[96,4096]{1,0:T(8,128)(2,1)S(1)}, u32[]{:S(2)}, u32[]{:S(2)}) collective-permute-start(bf16[96,4096]{1,0:T(8,128)(2,1)S(1)} %join_strips.4._._before.refs_0_.refs_3_), channel_id=1, source_target_pairs={{4,0},{8,4},{12,8},{16,12},{20,16},{24,20},{28,24},{0,28},{5,1},{9... | collective-permute-start | bytes 2359304 | tf_op jit(solution)/shard_map/date_0_0/ppermute | solution.py:416
  73.1 17.9 %collective-permute-start.15 = (bf16[80,1024]{1,0:T(8,128)(2,1)S(1)}, bf16[80,1024]{1,0:T(8,128)(2,1)S(1)}, u32[]{:S(2)}, u32[]{:S(2)}) collective-permute-start(bf16[80,1024]{1,0:T(8,128)(2,1)S(1)} %get-tuple-element.75), channel_id=1, source_target_pairs={{0,1},{1,2},{2,3},{3,0},{4,5},{5,6},{6,7},{7,4},{8,9},{9,10},{10,1... | collective-permute-start | bytes 491528 | tf_op jit(solution)/shard_map/strips_1/ppermute | solution.py:410
  77.9 13.1 %collective-permute-start.16 = (bf16[80,1024]{1,0:T(8,128)(2,1)S(1)}, bf16[80,1024]{1,0:T(8,128)(2,1)S(1)}, u32[]{:S(2)}, u32[]{:S(2)}) collective-permute-start(bf16[80,1024]{1,0:T(8,128)(2,1)S(1)} %get-tuple-element.76), channel_id=1, source_target_pairs={{0,2},{1,3},{2,0},{3,1},{4,6},{5,7},{6,4},{7,5},{8,10},{9,11},{10,... | collective-permute-start | bytes 491528 | tf_op jit(solution)/shard_map/strips_1/ppermute | solution.py:410
  77.9 19.5 %collective-permute-start.17 = (bf16[80,1024]{1,0:T(8,128)(2,1)S(1)}, bf16[80,1024]{1,0:T(8,128)(2,1)S(1)}, u32[]{:S(2)}, u32[]{:S(2)}) collective-permute-start(bf16[80,1024]{1,0:T(8,128)(2,1)S(1)} %get-tuple-element.77), channel_id=1, source_target_pairs={{0,3},{1,0},{2,1},{3,2},{4,7},{5,4},{6,5},{7,6},{8,11},{9,8},{10,9... | collective-permute-start | bytes 491528 | tf_op jit(solution)/shard_map/strips_1/ppermute | solution.py:410
  82.6 30.9 %collective-permute-start.22 = (bf16[96,4096]{1,0:T(8,128)(2,1)S(1)}, bf16[96,4096]{1,0:T(8,128)(2,1)S(1)}, u32[]{:S(2)}, u32[]{:S(2)}) collective-permute-start(bf16[96,4096]{1,0:T(8,128)(2,1)S(1)} %collective-permute-done.21.refs_1_.refs_4_), channel_id=1, source_target_pairs={{4,0},{8,4},{12,8},{16,12},{20,16},{24,20},{28,24},{0,28},{5,1},{9... | collective-permute-start | bytes 2359304 | tf_op jit(solution)/shard_map/date_0_1/ppermute | solution.py:416
  86.4 11.6 %collective-permute-start.18 = (bf16[64,1024]{1,0:T(8,128)(2,1)S(1)}, bf16[64,1024]{1,0:T(8,128)(2,1)S(1)}, u32[]{:S(2)}, u32[]{:S(2)}) collective-permute-start(bf16[64,1024]{1,0:T(8,128)(2,1)S(1)} %get-tuple-element.79), channel_id=1, source_target_pairs={{0,1},{1,2},{2,3},{3,0},{4,5},{5,6},{6,7},{7,4},{8,9},{9,10},{10,1... | collective-permute-start | bytes 393224 | tf_op jit(solution)/shard_map/strips_2/ppermute | solution.py:410
  91.0 8.8 %collective-permute-start.19 = (bf16[64,1024]{1,0:T(8,128)(2,1)S(1)}, bf16[64,1024]{1,0:T(8,128)(2,1)S(1)}, u32[]{:S(2)}, u32[]{:S(2)}) collective-permute-start(bf16[64,1024]{1,0:T(8,128)(2,1)S(1)} %get-tuple-element.80), channel_id=1, source_target_pairs={{0,2},{1,3},{2,0},{3,1},{4,6},{5,7},{6,4},{7,5},{8,10},{9,11},{10,... | collective-permute-start | bytes 393224 | tf_op jit(solution)/shard_map/strips_2/ppermute | solution.py:410
  91.0 9.0 %collective-permute-start.20 = (bf16[64,1024]{1,0:T(8,128)(2,1)S(1)}, bf16[64,1024]{1,0:T(8,128)(2,1)S(1)}, u32[]{:S(2)}, u32[]{:S(2)}) collective-permute-start(bf16[64,1024]{1,0:T(8,128)(2,1)S(1)} %get-tuple-element.81), channel_id=1, source_target_pairs={{0,3},{1,0},{2,1},{3,2},{4,7},{5,4},{6,5},{7,6},{8,11},{9,8},{10,9... | collective-permute-start | bytes 393224 | tf_op jit(solution)/shard_map/strips_2/ppermute | solution.py:410
  97.5 8.2 %collective-permute-start.30 = (bf16[80,4096]{1,0:T(8,128)(2,1)S(1)}, bf16[80,4096]{1,0:T(8,128)(2,1)S(1)}, u32[]{:S(2)}, u32[]{:S(2)}) collective-permute-start(bf16[80,4096]{1,0:T(8,128)(2,1)S(1)} %join_strips.5._._before.refs_0_.refs_3_), channel_id=1, source_target_pairs={{4,0},{8,4},{12,8},{16,12},{20,16},{24,20},{28,24},{0,28},{5,1},{9... | collective-permute-start | bytes 1966088 | tf_op jit(solution)/shard_map/date_1_0/ppermute | solution.py:416
  100.0 11.3 %collective-permute-start.28 = (bf16[64,4096]{1,0:T(8,128)(2,1)S(1)}, bf16[64,4096]{1,0:T(8,128)(2,1)S(1)}, u32[]{:S(2)}, u32[]{:S(2)}) collective-permute-start(bf16[64,4096]{1,0:T(8,128)(2,1)S(1)} %join_strips.6._before.refs_0_.refs_3_), channel_id=1, source_target_pairs={{4,0},{8,4},{12,8},{16,12},{20,16},{24,20},{28,24},{0,28},{5,1},{9... | collective-permute-start | bytes 1572872 | tf_op jit(solution)/shard_map/date_2_0/ppermute | solution.py:416
  105.6 14.4 %collective-permute-start.31 = (bf16[80,4096]{1,0:T(8,128)(2,1)S(1)}, bf16[80,4096]{1,0:T(8,128)(2,1)S(1)}, u32[]{:S(2)}, u32[]{:S(2)}) collective-permute-start(bf16[80,4096]{1,0:T(8,128)(2,1)S(1)} %collective-permute-done.30.refs_1_.refs_4_), channel_id=1, source_target_pairs={{4,0},{8,4},{12,8},{16,12},{20,16},{24,20},{28,24},{0,28},{5,1},{9... | collective-permute-start | bytes 1966088 | tf_op jit(solution)/shard_map/date_1_1/ppermute | solution.py:416
  108.4 11.5 %collective-permute-start.23 = (bf16[32,1024]{1,0:T(8,128)(2,1)S(1)}, bf16[32,1024]{1,0:T(8,128)(2,1)S(1)}, u32[]{:S(2)}, u32[]{:S(2)}) collective-permute-start(bf16[32,1024]{1,0:T(8,128)(2,1)S(1)} %get-tuple-element.83), channel_id=1, source_target_pairs={{0,1},{1,2},{2,3},{3,0},{4,5},{5,6},{6,7},{7,4},{8,9},{9,10},{10,1... | collective-permute-start | bytes 196616 | tf_op jit(solution)/shard_map/strips_3/ppermute | solution.py:410
  110.5 9.4 %collective-permute-start.24 = (bf16[32,1024]{1,0:T(8,128)(2,1)S(1)}, bf16[32,1024]{1,0:T(8,128)(2,1)S(1)}, u32[]{:S(2)}, u32[]{:S(2)}) collective-permute-start(bf16[32,1024]{1,0:T(8,128)(2,1)S(1)} %get-tuple-element.84), channel_id=1, source_target_pairs={{0,2},{1,3},{2,0},{3,1},{4,6},{5,7},{6,4},{7,5},{8,10},{9,11},{10,... | collective-permute-start | bytes 196616 | tf_op jit(solution)/shard_map/strips_3/ppermute | solution.py:410
  111.2 8.7 %collective-permute-start.25 = (bf16[32,1024]{1,0:T(8,128)(2,1)S(1)}, bf16[32,1024]{1,0:T(8,128)(2,1)S(1)}, u32[]{:S(2)}, u32[]{:S(2)}) collective-permute-start(bf16[32,1024]{1,0:T(8,128)(2,1)S(1)} %get-tuple-element.85), channel_id=1, source_target_pairs={{0,3},{1,0},{2,1},{3,2},{4,7},{5,4},{6,5},{7,6},{8,11},{9,8},{10,9... | collective-permute-start | bytes 196616 | tf_op jit(solution)/shard_map/strips_3/ppermute | solution.py:410
  113.5 16.0 %collective-permute-start.29 = (bf16[64,4096]{1,0:T(8,128)(2,1)S(1)}, bf16[64,4096]{1,0:T(8,128)(2,1)S(1)}, u32[]{:S(2)}, u32[]{:S(2)}) collective-permute-start(bf16[64,4096]{1,0:T(8,128)(2,1)S(1)} %collective-permute-done.28.refs_1_.refs_4_), channel_id=1, source_target_pairs={{4,0},{8,4},{12,8},{16,12},{20,16},{24,20},{28,24},{0,28},{5,1},{9... | collective-permute-start | bytes 1572872 | tf_op jit(solution)/shard_map/date_2_1/ppermute | solution.py:416
  120.0 6.7 %collective-permute-start.26 = (bf16[32,4096]{1,0:T(8,128)(2,1)S(1)}, bf16[32,4096]{1,0:T(8,128)(2,1)S(1)}, u32[]{:S(2)}, u32[]{:S(2)}) collective-permute-start(bf16[32,4096]{1,0:T(8,128)(2,1)S(1)} %join_strips.7.refs_0_), channel_id=1, source_target_pairs={{4,0},{8,4},{12,8},{16,12},{20,16},{24,20},{28,24},{0,28},{5,1},{9... | collective-permute-start | bytes 786440 | tf_op jit(solution)/shard_map/date_3_0/ppermute | solution.py:416
  126.7 6.9 %collective-permute-start.27 = (bf16[32,4096]{1,0:T(8,128)(2,1)S(1)}, bf16[32,4096]{1,0:T(8,128)(2,1)S(1)}, u32[]{:S(2)}, u32[]{:S(2)}) collective-permute-start(bf16[32,4096]{1,0:T(8,128)(2,1)S(1)} %collective-permute-done.26.refs_1_), channel_id=1, source_target_pairs={{4,0},{8,4},{12,8},{16,12},{20,16},{24,20},{28,24},{0,28},{5,1},{9... | collective-permute-start | bytes 786440 | tf_op jit(solution)/shard_map/date_3_1/ppermute | solution.py:416
